TPU v7x, 32 devices: a whole 2x2x4 slice. The times are simulated.
32 devices in a mesh: grp: 4 (over z), srv: 8 (over y, x, core).
Axes of the slice: x: 2, y: 2, z: 4, core: 2. Of those that a mesh axis runs over, the one named last changes fastest.
Arguments:
- queries: bfloat16 [2048, 1024], P('srv', 'grp'), may hold values from -8 to 8
- key_rows: bfloat16 [2048, 128], P('srv'), may hold values from -8 to 8
- value_rows: bfloat16 [2048, 128], P('srv'), may hold values from -6 to 6
- grad_output: bfloat16 [2048, 1024], P('srv', 'grp'), may hold values from -6 to 6
- doc_ids: int32 [2048], replicated, may hold values from 0 to 7, never falling along the last dimension, each value on 1 to 1280 neighbouring positions
Outputs:
- grad_query: bfloat16 [2048, 1024], P('srv', 'grp')
- grad_key: bfloat16 [2048, 128], P('srv', 'grp')
- grad_value: bfloat16 [2048, 128], P('srv', 'grp')
Inputs may be any that keep to these rules, and one draw needn't show every extreme that they name: `doc_ids`: document numbers never fall along the pack; each document has 1 to 1280 tokens, and one has exactly 1280.
All inputs are finite; a program needn't handle non-finite values.
Results may differ from a plain program's by a relative error of at most 0.0069.
Values may be sent and summed in bfloat16 or wider, within the bound.
No kernel may reach another device: no remote copies, remote signals or barrier semaphores. Data moves between devices by JAX's collectives and lax.ppermute only.
A program may use at most 64 MiB of HBM per device.

v0:
```python
import jax
import jax.numpy as jnp
from jax import lax
from jax.sharding import PartitionSpec as P

HD = 128


big_negative = -1e30


def partner(block, axis, bit):
    count = lax.axis_size(axis)
    route = []
    for low in range(count):
        high = low | 1 << bit
        if high != low and high < count:
            route += [(low, high), (high, low)]
    return lax.ppermute(block, axis, route)


def score_block(query_heads, key_block, row_pos, row_doc, key_pos, key_doc):
    head_dim = key_block.shape[1]
    scores = jnp.einsum(
        "rhd,kd->hrk", query_heads, key_block, preferred_element_type=jnp.float32
    ) * head_dim ** (-0.5)
    allowed = (row_doc[:, None] == key_doc[None, :]) & (key_pos[None, :] <= row_pos[:, None])
    return (scores, allowed[None])


def stats_update(
    state_now, query_heads, grad_heads, key_block, value_block, row_pos, row_doc, key_pos, key_doc
):
    run_max, run_sum, run_acc = state_now
    scores, allowed = score_block(query_heads, key_block, row_pos, row_doc, key_pos, key_doc)
    grad_probs = jnp.einsum(
        "rhd,kd->hrk", grad_heads, value_block, preferred_element_type=jnp.float32
    )
    new_max = jnp.maximum(run_max, jnp.max(jnp.where(allowed, scores, big_negative), axis=2))
    factor = jnp.exp(run_max - new_max)
    weights = jnp.where(allowed, jnp.exp(scores - new_max[:, :, None]), 0.0)
    return (
        new_max,
        run_sum * factor + jnp.sum(weights, axis=2),
        run_acc * factor + jnp.sum(weights * grad_probs, axis=2),
    )


def gradient_terms(
    query_heads,
    grad_heads,
    key_block,
    value_block,
    log_norm,
    row_delta,
    row_pos,
    row_doc,
    key_pos,
    key_doc,
):
    scores, allowed = score_block(query_heads, key_block, row_pos, row_doc, key_pos, key_doc)
    weights = jnp.where(allowed, jnp.exp(scores - log_norm[:, :, None]), 0.0)
    grad_probs = jnp.einsum(
        "rhd,kd->hrk", grad_heads, value_block, preferred_element_type=jnp.float32
    )
    grad_scores = (weights * (grad_probs - row_delta[:, :, None])).astype(jnp.bfloat16)
    return (weights.astype(jnp.bfloat16), grad_scores)


def query_part(grad_scores, key_block):
    return jnp.einsum("hrk,kd->rhd", grad_scores, key_block, preferred_element_type=jnp.float32)


def key_value_part(weights_low, grad_scores, query_heads, grad_heads):
    head_dim = query_heads.shape[2]
    key_part = jnp.einsum(
        "hrk,rhd->kd", grad_scores, query_heads, preferred_element_type=jnp.float32
    ) * head_dim ** (-0.5)
    value_part = jnp.einsum(
        "hrk,rhd->kd", weights_low, grad_heads, preferred_element_type=jnp.float32
    )
    return jnp.concatenate([key_part, value_part], axis=1)


def on_device(queries, key_rows, value_rows, grad_output, doc_ids):
    row_count = queries.shape[0]
    head_dim = HD
    heads_here = queries.shape[1] // head_dim
    query_heads = queries.reshape(row_count, heads_here, head_dim)
    grad_heads = grad_output.reshape(row_count, heads_here, head_dim)
    kv_heads = key_rows.shape[1] // head_dim
    share = lax.axis_size("grp") // kv_heads
    kv_col = lax.axis_index("grp") // share * head_dim
    own_block = jnp.concatenate(
        [
            lax.dynamic_slice_in_dim(key_rows, kv_col, head_dim, 1),
            lax.dynamic_slice_in_dim(value_rows, kv_col, head_dim, 1),
        ],
        axis=1,
    )
    seq_index = lax.axis_index("srv")
    row_first = seq_index * row_count
    row_last = row_first + row_count - 1
    row_pos = row_first + jnp.arange(row_count, dtype=jnp.int32)
    row_doc = lax.dynamic_slice_in_dim(doc_ids, row_first, row_count)
    start_state = (
        jnp.full((heads_here, row_count), big_negative, jnp.float32),
        jnp.zeros((heads_here, row_count), jnp.float32),
        jnp.zeros((heads_here, row_count), jnp.float32),
    )
    zero_acc = jnp.zeros((row_count, heads_here, head_dim), jnp.float32)

    def reaches(first_key, span):
        last_doc = lax.dynamic_slice_in_dim(doc_ids, first_key + span - 1, 1)[0]
        return (first_key <= row_last) & (last_doc >= row_doc[0])

    def key_info(first_key, span):
        return (
            first_key + jnp.arange(span, dtype=jnp.int32),
            lax.dynamic_slice_in_dim(doc_ids, first_key, span),
        )

    def stats_on(state_now, kv_block, first_key):
        span = kv_block.shape[0]
        key_pos, key_doc = key_info(first_key, span)

        def stats_active(state_in):
            return stats_update(
                state_in,
                query_heads,
                grad_heads,
                kv_block[:, :head_dim],
                kv_block[:, head_dim:],
                row_pos,
                row_doc,
                key_pos,
                key_doc,
            )

        def stats_resting(state_in):
            return state_in

        return lax.cond(reaches(first_key, span), stats_active, stats_resting, state_now)

    def both_on(acc_now, kv_block, first_key, log_norm, row_delta):
        span = kv_block.shape[0]
        key_pos, key_doc = key_info(first_key, span)

        def both_active(acc_in):
            weights_low, grad_scores = gradient_terms(
                query_heads,
                grad_heads,
                kv_block[:, :head_dim],
                kv_block[:, head_dim:],
                log_norm,
                row_delta,
                row_pos,
                row_doc,
                key_pos,
                key_doc,
            )
            return (
                acc_in + query_part(grad_scores, kv_block[:, :head_dim]),
                key_value_part(weights_low, grad_scores, query_heads, grad_heads),
            )

        def both_resting(acc_in):
            return (acc_in, jnp.zeros((span, 2 * head_dim), jnp.float32))

        return lax.cond(reaches(first_key, span), both_active, both_resting, acc_now)

    pack = lax.all_gather(own_block, "srv", axis=0, tiled=True)
    pack_rows = pack.shape[0]
    block_rows = min(512, pack_rows)

    def pack_stats(block_index, state_now):
        first_key = block_index * block_rows
        return stats_on(
            state_now, lax.dynamic_slice_in_dim(pack, first_key, block_rows, 0), first_key
        )

    final_state = lax.fori_loop(0, pack_rows // block_rows, pack_stats, start_state)
    run_max, run_sum, run_acc = final_state
    log_norm = run_max + jnp.log(run_sum)
    row_delta = run_acc / run_sum

    def pack_grads(block_index, carried):
        acc_now, terms_now = carried
        first_key = block_index * block_rows
        acc_new, part_new = both_on(
            acc_now,
            lax.dynamic_slice_in_dim(pack, first_key, block_rows, 0),
            first_key,
            log_norm,
            row_delta,
        )
        return (acc_new, lax.dynamic_update_slice_in_dim(terms_now, part_new, first_key, 0))

    query_acc, kv_terms = lax.fori_loop(
        0,
        pack_rows // block_rows,
        pack_grads,
        (zero_acc, jnp.zeros((pack_rows, 2 * head_dim), jnp.float32)),
    )
    kv_grads = lax.psum_scatter(kv_terms, "srv", scatter_dimension=0, tiled=True)
    grad_query = (
        (query_acc * head_dim ** (-0.5))
        .reshape(row_count, heads_here * head_dim)
        .astype(jnp.bfloat16)
    )
    current = kv_grads.reshape(row_count, 2, share, head_dim // share)
    member = lax.axis_index("grp") % share
    for bit_number in reversed(range(share.bit_length() - 1)):
        half_width = current.shape[2] // 2
        lower = current[:, :, :half_width]
        upper = current[:, :, half_width:]
        upper_side = member >> bit_number & 1 == 1
        keep_part = jnp.where(upper_side, upper, lower)
        send_part = jnp.where(upper_side, lower, upper)
        current = keep_part + partner(send_part, "grp", bit_number)
    key_sum = current[:, 0, 0, :]
    value_sum = current[:, 1, 0, :]
    return (grad_query, key_sum.astype(jnp.bfloat16), value_sum.astype(jnp.bfloat16))


def solution(mesh):
    in_specs = (P("srv", "grp"), P("srv", None), P("srv", None), P("srv", "grp"), P())
    out_specs = (P("srv", "grp"), P("srv", "grp"), P("srv", "grp"))
    return jax.shard_map(
        on_device, mesh=mesh, in_specs=in_specs, out_specs=out_specs, check_vma=False
    )
```

profile of v0, /device:TPU:0, one launch (start us, length us, event | category | flops | bytes accessed | tf_op | source)
XLA Modules:
  0.0 156.1 jit_solution(14106266723528307201)
XLA Ops:
  7.2 1.5 pad_maximum_fusion.1
  8.8 1.0 copy.13
  10.6 1.0 copy.14
  11.8 0.8 dynamic_slice.81
  12.5 24.2 %all-gather.2.cloned.1.call-done = bf16[2048,256]{1,0:T(8,128)(2,1)} async-done(((bf16[256,256]{1,0:T(8,128)(2,1)}), bf16[2048,256]{1,0:T(8,128)(2,1)}) %all-gather.2.cloned.1.call-update) | async-done | bytes 1048592 | tf_op jit(solution)/shard_map/all_gather | solution.py:172
  36.7 16.1 %while.45 = (s32[]{:T(128)}, f32[2,256]{1,0:T(2,128)S(1)}, f32[2,256]{1,0:T(2,128)S(1)}, f32[2,256]{1,0:T(2,128)S(1)}, s32[]{:T(128)}, /*index=5*/s32[2048]{0:T(...) while((s32[]{:T(128)}, f32[2,256]{1,0:T(2,128)S(1)}, ...), condition=%wide.region_6.7_spmd.clone, body=%wide.region_0.6_spmd.clone.sunk | while | flops 137234704 | bytes 4251107 | solution.py:182
  36.7 1.3 dynamic_slice.86
  39.7 3.8 %conditional.6 = ((f32[2,256]{1,0:T(2,128)S(1)}, f32[2,256]{1,0:T(2,128)S(1)}, f32[2,256]{1,0:T(2,128)S(1)})) conditional(s32[]{:T(128)} %convert_element_type.65, (f32[2,256]{1,0:T(2,128)S(1)}, f32[2,256]{1,0:T(2,128)S(1)}, f32[2,256]{1,0:T(2,128)S(1)}) %tuple.148, (s32[256]{0:T(256)S(1)}, s32[]{:T(128)}, s32[2048]{0:T(1024)}, s32[512]{0:T(512)S(1)}, ...), branch_computations={%region_1.1_spmd, %region_2.5_spmd} | conditional | flops 137234688 | bytes 4247654 | solution.py:143
  39.8 0.8 dynamic_slice.74
  40.8 1.2 select_reduce_fusion
  42.0 1.3 fusion.6
  43.6 1.3 dynamic_slice.86
  46.7 1.3 dynamic_slice.86
  49.7 1.3 dynamic_slice.86
  53.1 18.9 %while.46 = (s32[]{:T(128)}, f32[256,2,128]{2,0,1:T(8,128)S(1)}, f32[2048,256]{0,1:T(8,128)S(1)}, s32[]{:T(128)}, s32[2048]{0:T(1024)}, /*index=5*/s32[256]{0:T(...) while((s32[]{:T(128)}, f32[256,2,128]{2,0,1:T(8,128)S(1)}, ...), condition=%wide.region_10.11_spmd.clone, body=%wide.region_7.10_spmd.clone.sunk | while | flops 338035456 | bytes 9593835 | solution.py:199
  53.1 1.3 dynamic_slice.87
  56.3 5.6 %conditional.7 = (f32[256,2,128]{2,0,1:T(8,128)S(1)}, f32[512,256]{0,1:T(8,128)S(1)}) conditional(s32[]{:T(128)} %convert_element_type.66, f32[256,2,128]{2,0,1:T(8,128)S(1)} %get-tuple-element.1349, (s32[256]{0:T(256)S(1)}, s32[2048]{0:T(1024)}, s32[]{:T(128)}, s32[]{:T(128)}, s32[512]{0:T(512)S(1)}, /*index=5*/s32[]{:T(128)}, ...), branch_computations={%region_8.8_spmd, %region_9.9_spmd} | conditional | flops 338035456 | bytes 8541768 | solution.py:170
  56.4 0.8 dynamic_slice.77
  57.3 1.3 fusion.13
  58.7 1.2 fusion.15
  59.9 1.3 fusion.17
  62.0 1.3 dynamic_slice.87
  65.3 1.3 dynamic_slice.87
  68.7 1.3 dynamic_slice.87
  72.0 1.3 copy-done
  73.4 59.9 %reduce-scatter.2.cloned.1.call-done = f32[256,256]{0,1:T(8,128)} async-done(((f32[2048,256]{0,1:T(8,128)}), f32[256,256]{0,1:T(8,128)}) %reduce-scatter.2.cloned.1.call-update) | async-done | bytes 262160 | tf_op jit(solution)/shard_map/reduce_scatter | solution.py:205
  133.3 1.0 slice_select_fusion
  134.3 2.5 %collective-permute-start = (f32[256,2,2,32]{0,3,2,1:T(8,128)S(1)}, f32[256,2,2,32]{0,3,2,1:T(8,128)S(1)}, u32[]{:S(2)}, u32[]{:S(2)}) collective-permute-start(f32[256,2,2,32]{0,3,2,1:T(8,128)S(1)} %slice_select_fusion), channel_id=1, source_target_pairs={{0,16},{16,0},{8,24},{24,8},{1,17},{17,1},{9,25},{25,9},{2,18},{18... | collective-permute-start | bytes 393224 | tf_op jit(solution)/shard_map/ppermute | solution.py:19
  136.8 6.5 %collective-permute-done = f32[256,2,2,32]{0,3,2,1:T(8,128)S(1)} collective-permute-done((f32[256,2,2,32]{0,3,2,1:T(8,128)S(1)}, f32[256,2,2,32]{0,3,2,1:T(8,128)S(1)}, u32[]{:S(2)}, u32[]{:S(2)}) %collective-permute-start) | collective-permute-done | bytes 131104 | tf_op jit(solution)/shard_map/ppermute | solution.py:19
  143.3 1.0 select_add_fusion
  144.9 0.7 copy_bitcast_fusion
  145.6 3.1 %collective-permute-done.1 = f32[256,2,1,32]{0,3,2,1:T(8,128)S(1)} collective-permute-done((f32[256,2,1,32]{0,3,2,1:T(8,128)S(1)}, f32[256,2,1,32]{0,3,2,1:T(8,128)S(1)}, u32[]{:S(2)}, u32[]{:S(2)}) %collective-permute-start.1) | collective-permute-done | bytes 65568 | tf_op jit(solution)/shard_map/ppermute | solution.py:19
  (71 shorter events, 8.7 us)
Async XLA Ops:
  7.2 29.5 %all-gather.2.cloned.1.call-start = ((), (), s32[]{:S(2)}) async-start(), calls=%async_computation.1 | async-start | bytes 1179648 | tf_op jit(solution)/shard_map/all_gather | solution.py:172
  8.8 124.5 %reduce-scatter.2.cloned.1.call-start = ((), (), s32[]{:S(2)}) async-start(), calls=%async_computation.2 | async-start | bytes 2359296 | tf_op jit(solution)/shard_map/reduce_scatter | solution.py:205
  9.8 0.7 copy-start.1
  58.7 2.8 %copy-start.2 = (bf16[256,2,128]{0,2,1:T(8,128)(2,1)S(1)}, bf16[256,2,128]{0,2,1:T(8,128)(2,1)}, u32[]{:S(2)}) copy-start(bf16[256,2,128]{0,2,1:T(8,128)(2,1)} %get-tuple-element.962) | copy-start | bytes 393220 | tf_op jit(solution)/shard_map/while/body/eval_jaxpr/cond
  72.0 1.3 copy-start
  134.3 9.0 %collective-permute-start = (f32[256,2,2,32]{0,3,2,1:T(8,128)S(1)}, f32[256,2,2,32]{0,3,2,1:T(8,128)S(1)}, u32[]{:S(2)}, u32[]{:S(2)}) collective-permute-start(f32[256,2,2,32]{0,3,2,1:T(8,128)S(1)} %slice_select_fusion), channel_id=1, source_target_pairs={{0,16},{16,0},{8,24},{24,8},{1,17},{17,1},{9,25},{25,9},{2,18},{18... | collective-permute-start | bytes 393224 | tf_op jit(solution)/shard_map/ppermute | solution.py:19
  144.3 4.3 %collective-permute-start.1 = (f32[256,2,1,32]{0,3,2,1:T(8,128)S(1)}, f32[256,2,1,32]{0,3,2,1:T(8,128)S(1)}, u32[]{:S(2)}, u32[]{:S(2)}) collective-permute-start(f32[256,2,1,32]{0,3,2,1:T(8,128)S(1)} %slice_select_fusion.1), channel_id=1, source_target_pairs={{0,8},{8,0},{16,24},{24,16},{1,9},{9,1},{17,25},{25,17},{2,10},{10... | collective-permute-start | bytes 196616 | tf_op jit(solution)/shard_map/ppermute | solution.py:19
Sparse Core Ops, SparseCore 0:
  10.5 26.1 all-gather.1
  73.5 59.7 reduce-scatter.1
where the time goes:
time: 157 us; the launch traced here: 156 us
  waiting for transfers between devices  93.7 us (60%)
  local copies, waits for them, and re-layouts  22.6 us (14%)
  between operations  14.2 us (9%)
  loops' own time  10.7 us (7%)
  matrix products  6.95 us (4%)
  other arithmetic  4.95 us (3%)
  starting transfers between devices  3.12 us (2%)
    reduce_scatter x1, waiting for transfers between devices, on_device(): lax.psum_scatter(kv_terms, 'srv', scatter_dimension=0, tiled=True)  59.9 us
    all_gather x1, waiting for transfers between devices, on_device(): pack = lax.all_gather(own_block, 'srv', axis=0, tiled=True)  24.2 us
    dynamic_slice x8, local copies, waits for them, and re-layouts, reaches(): last_doc = lax.dynamic_slice_in_dim(doc_ids, first_key + span - 1, 1)[0]  10.6 us
    ppermute x2, waiting for transfers between devices, partner(): return lax.ppermute(block, axis, route)  9.62 us
    another operation x1, loops' own time, on_device(): lax.fori_loop(0, pack_rows // block_rows, pack_grads, (zero_acc, jnp.zero...  5.39 us
    another operation x1, loops' own time, on_device(): lax.fori_loop(0, pack_rows // block_rows, pack_stats, start_state)  4.95 us
    slice x8, local copies, waits for them, and re-layouts, reaches(): return (first_key <= row_last) & (last_doc >= row_doc[0])  4.24 us
    unnamed x8, local copies, waits for them, and re-layouts  4.23 us
  transfers between devices with their start and end apart: 4, of which 4 were waited for; matrix products, arithmetic and copies ran while one was open for 2% of the time, Pallas kernels for 0%

commit v1 on v0

v1 whole, which is shorter than its diff:
```python
import functools

import jax
import jax.numpy as jnp
from jax import lax
from jax.experimental import pallas as pl
from jax.experimental.pallas import tpu as pltpu
from jax.sharding import PartitionSpec as P

HD = 128
SCALE = HD**-0.5
LOG2E = 1.4426950408889634
MASKED = -1.0e30
LOWEST = -1.0e20
F32 = jnp.float32
BF16 = jnp.bfloat16


def nn(a, b):
    return lax.dot_general(a, b, (((1,), (0,)), ((), ())), preferred_element_type=F32)


def nt(a, b):
    return lax.dot_general(a, b, (((1,), (1,)), ((), ())), preferred_element_type=F32)


def tn(a, b):
    return lax.dot_general(a, b, (((0,), (0,)), ((), ())), preferred_element_type=F32)


def key_doc_column(docs_ref, block):
    row = docs_ref[pl.ds(block, 1), :]
    span = row.shape[1]
    column = jnp.transpose(jnp.broadcast_to(row, (128, span)))
    return jnp.concatenate([column] * (span // 128), axis=1)


def scores_of(kv, qt, key_doc, row_doc, causal):
    scores = nn(kv[:, :HD], qt) * (SCALE * LOG2E)
    allowed = key_doc == row_doc
    if causal:
        key_pos = lax.broadcasted_iota(jnp.int32, scores.shape, 0)
        row_pos = lax.broadcasted_iota(jnp.int32, scores.shape, 1)
        allowed = allowed & (key_pos <= row_pos)
    return jnp.where(allowed, scores, MASKED)


def add_stats(stats_ref, kv, qt_ref, dot_ref, docs_ref, key_block, row_block, chunks, causal):
    rows = docs_ref.shape[1]
    key_doc = key_doc_column(docs_ref, key_block)
    row_doc = docs_ref[pl.ds(row_block, 1), :]
    for chunk in chunks:
        lanes = slice(chunk * rows, (chunk + 1) * rows)
        scores = scores_of(kv, qt_ref[:, lanes], key_doc, row_doc, causal)
        grad_probs = nn(kv[:, HD:], dot_ref[:, lanes])
        old = stats_ref[0:1, lanes]
        new = jnp.maximum(old, jnp.max(scores, axis=0, keepdims=True))
        factor = jnp.exp2(old - new)
        weights = jnp.exp2(scores - new)
        stats_ref[0:1, lanes] = new
        stats_ref[1:2, lanes] = stats_ref[1:2, lanes] * factor + jnp.sum(
            weights, axis=0, keepdims=True
        )
        stats_ref[2:3, lanes] = stats_ref[2:3, lanes] * factor + jnp.sum(
            weights * grad_probs, axis=0, keepdims=True
        )


def add_grads(
    kv, qt_ref, dot_ref, docs_ref, key_block, row_block, chunks, causal, norm_ref, dqt_ref
):
    rows = docs_ref.shape[1]
    key_doc = key_doc_column(docs_ref, key_block)
    row_doc = docs_ref[pl.ds(row_block, 1), :]
    dkt = jnp.zeros((HD, rows), F32)
    dvt = jnp.zeros((HD, rows), F32)
    for chunk in chunks:
        lanes = slice(chunk * rows, (chunk + 1) * rows)
        qt = qt_ref[:, lanes]
        dot = dot_ref[:, lanes]
        scores = scores_of(kv, qt, key_doc, row_doc, causal)
        weights = jnp.exp2(scores - norm_ref[0:1, lanes])
        grad_probs = nn(kv[:, HD:], dot)
        grad_scores = (weights * (grad_probs - norm_ref[1:2, lanes])).astype(BF16)
        dkt += nt(qt, grad_scores)
        dvt += nt(dot, weights.astype(BF16))
        dqt_ref[:, lanes] += tn(kv[:, :HD], grad_scores)
    return dkt, dvt


def place():
    srv = lax.axis_index("srv")
    return srv // 2, srv % 2


def reaches(ids_ref, rows, key_block, row_block):
    return ids_ref[key_block * rows + rows - 1] >= ids_ref[row_block * rows]


def own_stats_kernel(heads, ids_ref, docs_ref, q_own, q_par, do_own, do_par, kv_ref, qt_ref, dot_ref, stats_ref):
    rows = docs_ref.shape[1]
    chip, core = place()
    for side, (q_ref, do_ref) in enumerate(((q_own, do_own), (q_par, do_par))):
        qt = jnp.transpose(q_ref[...])
        dot = jnp.transpose(do_ref[...])
        for head in range(heads):
            lanes = slice((side * heads + head) * rows, (side * heads + head + 1) * rows)
            qt_ref[:, lanes] = qt[head * HD : (head + 1) * HD, :]
            dot_ref[:, lanes] = dot[head * HD : (head + 1) * HD, :]
    stats_ref[...] = jnp.zeros(stats_ref.shape, F32)
    stats_ref[0:1, :] = jnp.full((1, stats_ref.shape[1]), LOWEST, F32)
    block = chip * 2 + core
    kv = kv_ref[...]
    add_stats(stats_ref, kv, qt_ref, dot_ref, docs_ref, block, block, range(heads), True)
    other = chip * 2 + 1 - core

    @pl.when((core == 0) & reaches(ids_ref, rows, block, other))
    def _():
        add_stats(stats_ref, kv, qt_ref, dot_ref, docs_ref, block, other, range(heads, 2 * heads), False)


def each_remote(groups, ids_ref, rows, body):
    chip, core = place()

    def step(group, slot, away):
        source = chip ^ away
        key_block = source * 2 + core
        for side in range(2):
            row_block = chip * 2 + (core if side == 0 else 1 - core)
            active = (source < chip) & reaches(ids_ref, rows, key_block, row_block)
            pl.when(active)(functools.partial(body, group, slot, key_block, row_block, side))

    first = 1
    for group, amount in enumerate(groups):
        if amount == 1:
            step(group, 0, first)
        else:
            base = first

            @pl.loop(0, amount)
            def _(slot):
                step(group, slot, base + slot)

        first += amount


def far_stats_kernel(heads, groups, ids_ref, docs_ref, qt_ref, dot_ref, stats_in, *rest):
    kv_refs, stats_ref = rest[:-1], rest[-1]
    rows = docs_ref.shape[1]
    stats_ref[...] = stats_in[...]

    def body(group, slot, key_block, row_block, side):
        add_stats(
            stats_ref,
            kv_refs[group][slot],
            qt_ref,
            dot_ref,
            docs_ref,
            key_block,
            row_block,
            range(side * heads, (side + 1) * heads),
            False,
        )

    each_remote(groups, ids_ref, rows, body)


def far_grads_kernel(heads, groups, ids_ref, docs_ref, qt_ref, dot_ref, stats_ref, other_ref, *rest):
    count = len(groups)
    kv_refs, out_refs = rest[:count], rest[count : 2 * count]
    dqt_ref, norm_ref = rest[2 * count :]
    rows = docs_ref.shape[1]
    half = heads * rows
    mine = stats_ref[...]
    other = other_ref[...]
    other = jnp.concatenate([other[:, half:], other[:, :half]], axis=1)
    top = jnp.maximum(mine[0:1], other[0:1])
    mine_by = jnp.exp2(mine[0:1] - top)
    other_by = jnp.exp2(other[0:1] - top)
    total = mine[1:2] * mine_by + other[1:2] * other_by
    norm_ref[...] = jnp.zeros(norm_ref.shape, F32)
    norm_ref[0:1, :] = top + jnp.log2(total)
    norm_ref[1:2, :] = (mine[2:3] * mine_by + other[2:3] * other_by) / total
    dqt_ref[...] = jnp.zeros(dqt_ref.shape, F32)
    for out_ref in out_refs:
        out_ref[...] = jnp.zeros(out_ref.shape, BF16)

    def body(group, slot, key_block, row_block, side):
        kv = kv_refs[group][slot]
        dkt, dvt = add_grads(
            kv,
            qt_ref,
            dot_ref,
            docs_ref,
            key_block,
            row_block,
            range(side * heads, (side + 1) * heads),
            False,
            norm_ref,
            dqt_ref,
        )
        both = jnp.concatenate([dkt * SCALE, dvt], axis=0)
        if side == 1:
            both = both + out_refs[group][slot].astype(F32)
        out_refs[group][slot] = both.astype(BF16)

    each_remote(groups, ids_ref, rows, body)


def own_grads_kernel(heads, ids_ref, docs_ref, qt_ref, dot_ref, norm_ref, kv_ref, dqt_in, dkv_ref, dq_own, dq_par, dqt_ref):
    rows = docs_ref.shape[1]
    chip, core = place()
    block = chip * 2 + core
    other = chip * 2 + 1 - core
    dqt_ref[...] = dqt_in[...]
    kv = kv_ref[...]
    dkt, dvt = add_grads(
        kv, qt_ref, dot_ref, docs_ref, block, block, range(heads), True, norm_ref, dqt_ref
    )
    dkv_ref[...] = jnp.concatenate([dkt * SCALE, dvt], axis=0)

    @pl.when((core == 0) & reaches(ids_ref, rows, block, other))
    def _():
        dkt, dvt = add_grads(
            kv, qt_ref, dot_ref, docs_ref, block, other, range(heads, 2 * heads), False, norm_ref, dqt_ref
        )
        dkv_ref[...] += jnp.concatenate([dkt * SCALE, dvt], axis=0)

    for side, out_ref in enumerate((dq_own, dq_par)):
        parts = [
            dqt_ref[:, (side * heads + head) * rows : (side * heads + head + 1) * rows]
            for head in range(heads)
        ]
        out_ref[...] = jnp.concatenate(parts, axis=0) * SCALE


def combine_kernel(share, count, own_ref, dq_own, dq_far, *rest):
    parts, outs = rest[:count], rest[count:]
    dq_ref, keep_ref, send_refs, sum_ref = outs[0], outs[1], outs[2:-1], outs[-1]
    width = HD // share
    total = own_ref[...]
    for part in parts:
        for slot in range(part.shape[0]):
            total = total + part[slot].astype(F32)
    sum_ref[...] = total
    member = lax.axis_index("grp") % share
    for away, out_ref in enumerate((keep_ref, *send_refs)):
        first = pl.multiple_of((member ^ away) * width, width)
        for half in range(2):
            piece = sum_ref[pl.ds(half * HD + first, width), :]
            out_ref[half * width : (half + 1) * width, :] = piece.astype(out_ref.dtype)
    dq_ref[...] = jnp.transpose(dq_own[...] + dq_far[...]).astype(BF16)


def finish_kernel(keep_ref, *rest):
    parts, (dk_ref, dv_ref) = rest[:-2], rest[-2:]
    total = keep_ref[...]
    for part in parts:
        total = total + part[...].astype(F32)
    width = total.shape[0] // 2
    dk_ref[...] = total[:width].astype(BF16)
    dv_ref[...] = total[width:].astype(BF16)


SMEM = pl.BlockSpec(memory_space=pltpu.SMEM)
VMEM = pl.BlockSpec(memory_space=pltpu.VMEM)


def call(kernel, out_shape, operands, scratch=(), smem=0, cost=None):
    return pl.pallas_call(
        kernel,
        out_shape=out_shape,
        in_specs=[SMEM] * smem + [VMEM] * (len(operands) - smem),
        out_specs=[VMEM] * len(out_shape),
        scratch_shapes=list(scratch),
        cost_estimate=cost,
        compiler_params=pltpu.CompilerParams(vmem_limit_bytes=24 << 20),
    )(*operands)


def sds(shape, dtype):
    return jax.ShapeDtypeStruct(shape, dtype)


def on_device(queries, key_rows, value_rows, grad_output, doc_ids):
    rows, columns = queries.shape
    heads = columns // HD
    srv = lax.axis_size("srv")
    chips = srv // 2
    grp = lax.axis_size("grp")
    kv_heads = key_rows.shape[1] // HD
    share = grp // kv_heads
    lanes = 2 * heads * rows
    if kv_heads > 1:
        first = lax.axis_index("grp") // share * HD
        key_rows = lax.dynamic_slice_in_dim(key_rows, first, HD, 1)
        value_rows = lax.dynamic_slice_in_dim(value_rows, first, HD, 1)
    own_kv = jnp.concatenate([key_rows, value_rows], axis=1)
    docs = doc_ids.reshape(srv, rows)

    def swap(block):
        return lax.ppermute(block, "srv", [(i, i ^ 1) for i in range(srv)])

    up = [
        [(i, i ^ 2 * away) for i in range(srv) if i ^ 2 * away > i] for away in range(chips)
    ]
    far_kv = [lax.ppermute(own_kv, "srv", up[away])[None] for away in range(1, chips)]
    groups = [1] * len(far_kv)
    if chips > 4:
        groups = [len(far_kv)]
        far_kv = [jnp.concatenate(far_kv, axis=0)]
    q_par = swap(queries)
    do_par = swap(grad_output)

    work = 2 * rows * rows * HD * heads
    qt, dot, stats = call(
        functools.partial(own_stats_kernel, heads),
        [sds((HD, lanes), BF16), sds((HD, lanes), BF16), sds((8, lanes), F32)],
        [doc_ids, docs, queries, q_par, grad_output, do_par, own_kv],
        smem=1,
        cost=pl.CostEstimate(flops=work * 4, bytes_accessed=2 << 20, transcendentals=0),
    )
    (stats,) = call(
        functools.partial(far_stats_kernel, heads, groups),
        [sds((8, lanes), F32)],
        [doc_ids, docs, qt, dot, stats, *far_kv],
        smem=1,
    )
    other_stats = swap(stats)
    *far_dkv, dqt, norm = call(
        functools.partial(far_grads_kernel, heads, groups),
        [sds((amount, 2 * HD, rows), BF16) for amount in groups]
        + [sds((HD, lanes), F32), sds((8, lanes), F32)],
        [doc_ids, docs, qt, dot, stats, other_stats, *far_kv],
        smem=1,
    )
    if chips > 4:
        far_dkv = [far_dkv[0][i : i + 1] for i in range(chips - 1)]
    came = [
        lax.ppermute(part, "srv", [(b, a) for a, b in up[away + 1]])
        for away, part in enumerate(far_dkv)
    ]
    own_dkv, dq_own, dq_par = call(
        functools.partial(own_grads_kernel, heads),
        [sds((2 * HD, rows), F32)] + [sds((columns, rows), F32)] * 2,
        [doc_ids, docs, qt, dot, norm, own_kv, dqt],
        scratch=[pltpu.VMEM((HD, lanes), F32)],
        smem=1,
        cost=pl.CostEstimate(flops=work * 6, bytes_accessed=2 << 20, transcendentals=0),
    )
    dq_far = swap(dq_par)
    width = HD // share
    grad_query, keep, *send = call(
        functools.partial(combine_kernel, share, len(came)),
        [sds((rows, columns), BF16), sds((2 * width, rows), F32)]
        + [sds((2 * width, rows), BF16)] * (share - 1),
        [own_dkv, dq_own, dq_far, *came],
        scratch=[pltpu.VMEM((2 * HD, rows), F32)],
    )
    back = [
        lax.ppermute(part, "grp", [(i, i ^ (away + 1)) for i in range(grp)])
        for away, part in enumerate(send)
    ]
    grad_key, grad_value = call(
        finish_kernel, [sds((width, rows), BF16)] * 2, [keep, *back]
    )
    return grad_query, grad_key.T, grad_value.T


def solution(mesh):
    in_specs = (P("srv", "grp"), P("srv", None), P("srv", None), P("srv", "grp"), P())
    out_specs = (P("srv", "grp"), P("srv", "grp"), P("srv", "grp"))
    return jax.shard_map(
        on_device, mesh=mesh, in_specs=in_specs, out_specs=out_specs, check_vma=False
    )
```

time: 157 us -> 46.9 us (0.30)
  waiting for transfers between devices: 93.7 us -> 18.9 us
  local copies, waits for them, and re-layouts: 22.6 us -> 1.77 us
  starting transfers between devices: 3.12 us -> 18.6 us
  between operations: 14.2 us -> 0.82 us
  loops' own time: 10.7 us -> 0 us
  matrix products: 6.95 us -> 0 us
  Pallas kernels: 0 us -> 6.57 us
  other arithmetic: 4.95 us -> 0 us
    reduce_scatter x1 -> x0, waiting for transfers between devices: 59.9 us -> none  [on_device(): lax.psum_scatter(kv_terms, 'srv', scatter_dimension=0, tiled=True)]
    all_gather x1 -> x0, waiting for transfers between devices: 24.2 us -> none  [on_device(): pack = lax.all_gather(own_block, 'srv', axis=0, tiled=True)]
    ppermute x2 -> x13, starting transfers between devices: 3.04 us -> 18.6 us  [the longest x3 9.55 us: on_device(): lax.ppermute(own_kv, 'srv', up[away])[None]]
    dynamic_slice x11 -> x0, local copies, waits for them, and re-layouts: 12.9 us -> none  [the longest x8 10.6 us: reaches(): last_doc = lax.dynamic_slice_in_dim(doc_ids, first_key + span - 1, 1)[0]]
    another operation x10 -> x0, loops' own time: 10.7 us -> none  [the longest x1 5.39 us: on_device(): lax.fori_loop(0, pack_rows // block_rows, pack_grads, (zero_acc, jnp.zero...]
    ppermute x2 -> x13, waiting for transfers between devices: 9.62 us -> 18.9 us  [the longest x3 11 us: on_device(): lax.ppermute(part, 'srv', [(b, a) for a, b in up[away + 1]])]
    dot_general x7 -> x0, matrix products: 6.95 us -> none  [the longest x2 2.55 us: score_block(): jnp.einsum('rhd,kd->hrk', query_heads, key_block, preferred_element_type=...]
    pallas_call x0 -> x6, Pallas kernels: none -> 6.57 us  [call(): pl.pallas_call(kernel, out_shape=out_shape, in_specs=[SMEM] * smem + [VME...]
  transfers between devices with their start and end apart: 4 -> 13, of which waited for: 4 -> 8; matrix products, arithmetic and copies ran while one was open for 2% -> 4% of each run, Pallas kernels for 0% -> 3%
where the time goes in v1:
time: 46.9 us; the launch traced here: 46.6 us
  waiting for transfers between devices  18.9 us (40%)
  starting transfers between devices  18.6 us (40%)
  Pallas kernels  6.57 us (14%)
  local copies, waits for them, and re-layouts  1.77 us (4%)
  between operations  0.82 us (2%)
    ppermute x3, waiting for transfers between devices, on_device(): lax.ppermute(part, 'srv', [(b, a) for a, b in up[away + 1]])  11 us
    ppermute x3, starting transfers between devices, on_device(): lax.ppermute(own_kv, 'srv', up[away])[None]  9.55 us
    pallas_call x6, Pallas kernels, call(): pl.pallas_call(kernel, out_shape=out_shape, in_specs=[SMEM] * smem + [VME...  6.57 us
    ppermute x3, waiting for transfers between devices, on_device(): lax.ppermute(part, 'grp', [(i, i ^ away + 1) for i in range(grp)])  5.49 us
    ppermute x3, starting transfers between devices, on_device(): lax.ppermute(part, 'grp', [(i, i ^ away + 1) for i in range(grp)])  4.39 us
    ppermute x3, starting transfers between devices, on_device(): lax.ppermute(part, 'srv', [(b, a) for a, b in up[away + 1]])  3.88 us
    ppermute x4, waiting for transfers between devices, swap(): return lax.ppermute(block, 'srv', [(i, i ^ 1) for i in range(srv)])  1.2 us
    ppermute x3, waiting for transfers between devices, on_device(): lax.ppermute(own_kv, 'srv', up[away])[None]  1.13 us
  transfers between devices with their start and end apart: 13, of which 8 were waited for; matrix products, arithmetic and copies ran while one was open for 4% of the time, Pallas kernels for 3%

profile of v1, /device:TPU:0, one launch (start us, length us, event | category | flops | bytes accessed | tf_op | source)
XLA Modules:
  0.0 46.6 jit_solution(676283825931836787)
XLA Ops:
  0.6 0.5 %collective-permute-start = (bf16[256,256]{1,0:T(8,128)(2,1)}, bf16[256,256]{1,0:T(8,128)(2,1)S(1)}, u32[]{:S(2)}, u32[]{:S(2)}) collective-permute-start(bf16[256,256]{1,0:T(8,128)(2,1)} %q_own.1), channel_id=1, source_target_pairs={{0,1},{1,0},{2,3},{3,2},{4,5},{5,4},{6,7},{7,6},{8,9},{9,8},{10,11... | collective-permute-start | bytes 393224 | tf_op jit(solution)/shard_map/ppermute | solution.py:302
  1.2 0.1 collective-permute-start.1
  1.2 0.9 %constant_dynamic-update-slice_fusion.1 = bf16[256,256]{1,0:T(8,128)(2,1)S(1)} fusion(bf16[256,128]{1,0:T(8,128)(2,1)} %param.6), kind=kLoop, calls=%fused_computation.1 | loop fusion | bytes 131072
  2.1 0.0 copy-start
  2.1 0.0 copy-start.2
  2.1 0.9 %constant_dynamic-update-slice_fusion.kv_ref = bf16[256,256]{1,0:T(8,128)(2,1)S(1)} fusion(bf16[256,256]{1,0:T(8,128)(2,1)S(1)} %constant_dynamic-update-slice_fusion.1, bf16[256,128]{1,0:T(8,128)(2,1)} %param.7), kind=kLoop, calls=%fused_computation | loop fusion | bytes 131072 | tf_op jit(solution)/shard_map/concatenate | solution.py:298
  3.0 5.8 %collective-permute-start.4 = (bf16[256,256]{1,0:T(8,128)(2,1)S(1)}, bf16[256,256]{1,0:T(8,128)(2,1)S(1)}, u32[]{:S(2)}, u32[]{:S(2)}) collective-permute-start(bf16[256,256]{1,0:T(8,128)(2,1)S(1)} %constant_dynamic-update-slice_fusion.kv_ref), channel_id=1, source_target_pairs={{0,6},{1,7},{2,4},{3,5},{8,14},{9,15},{10,12},{11,13},{16,22},{17,... | collective-permute-start | bytes 393224 | tf_op jit(solution)/shard_map/ppermute | solution.py:307
  8.8 1.3 %collective-permute-start.3 = (bf16[256,256]{1,0:T(8,128)(2,1)S(1)}, bf16[256,256]{1,0:T(8,128)(2,1)S(1)}, u32[]{:S(2)}, u32[]{:S(2)}) collective-permute-start(bf16[256,256]{1,0:T(8,128)(2,1)S(1)} %constant_dynamic-update-slice_fusion.kv_ref), channel_id=1, source_target_pairs={{0,4},{1,5},{2,6},{3,7},{8,12},{9,13},{10,14},{11,15},{16,20},{17,... | collective-permute-start | bytes 393224 | tf_op jit(solution)/shard_map/ppermute | solution.py:307
  10.1 2.5 %collective-permute-start.2 = (bf16[256,256]{1,0:T(8,128)(2,1)S(1)}, bf16[256,256]{1,0:T(8,128)(2,1)S(1)}, u32[]{:S(2)}, u32[]{:S(2)}) collective-permute-start(bf16[256,256]{1,0:T(8,128)(2,1)S(1)} %constant_dynamic-update-slice_fusion.kv_ref), channel_id=1, source_target_pairs={{0,2},{1,3},{4,6},{5,7},{8,10},{9,11},{12,14},{13,15},{16,18},{17,... | collective-permute-start | bytes 393224 | tf_op jit(solution)/shard_map/ppermute | solution.py:307
  12.7 1.5 %shard_map.76 = (bf16[128,1024]{1,0:T(8,128)(2,1)S(1)}, bf16[128,1024]{1,0:T(8,128)(2,1)S(1)}, f32[8,1024]{1,0:T(8,128)S(1)}) custom-call(s32[2048]{0:T(1024)S(1)} %copy-done, s32[8,256]{1,0:T(8,128)S(1)} %reshape.9.docs_ref, bf16[256,256]{1,0:T(8,128)(2,1)S(1)} %copy-done.1, bf16[256,256]{1,0:T(8,128)(2,1)S(1)} %collective-permute-done.q_par, ...), custom_call_target="tpu_custom_call" | custom-call | flops 134217728 | bytes 2097152 | tf_op jit(solution)/shard_map/pallas_call | solution.py:270
  14.1 0.0 collective-permute-done.4
  14.2 0.4 collective-permute-done.3
  14.6 0.7 %collective-permute-done.2 = bf16[256,256]{1,0:T(8,128)(2,1)S(1)} collective-permute-done((bf16[256,256]{1,0:T(8,128)(2,1)S(1)}, bf16[256,256]{1,0:T(8,128)(2,1)S(1)}, u32[]{:S(2)}, u32[]{:S(2)}) %collective-permute-start.2) | collective-permute-done | bytes 131104 | tf_op jit(solution)/shard_map/ppermute | solution.py:307
  15.3 0.7 %shard_map.77.stats_ref = f32[8,1024]{1,0:T(8,128)S(1)} custom-call(s32[2048]{0:T(1024)S(1)} %copy-done, s32[8,256]{1,0:T(8,128)S(1)} %reshape.9.docs_ref, bf16[128,1024]{1,0:T(8,128)(2,1)S(1)} %get-tuple-element.21.qt_ref, bf16[128,1024]{1,0:T(8,128)(2,1)S(1)} %get-tuple-element.22.dot_ref, f32[8,1024]{1,0:T(8,128)S(1)} %get-tuple-element.23.stats_in, ...), custom_call_target="tpu_custom_call" | custom-call | tf_op jit(solution)/shard_map/pallas_call | solution.py:270
  16.0 0.1 collective-permute-start.5
  16.1 1.2 %collective-permute-done.5.other_ref = f32[8,1024]{1,0:T(8,128)S(1)} collective-permute-done((f32[8,1024]{1,0:T(8,128)S(1)}, f32[8,1024]{1,0:T(8,128)S(1)}, u32[]{:S(2)}, u32[]{:S(2)}) %collective-permute-start.5) | collective-permute-done | bytes 32800 | tf_op jit(solution)/shard_map/ppermute | solution.py:302
  17.3 0.8 %shard_map.78 = (bf16[1,256,256]{2,1,0:T(8,128)(2,1)S(1)}, bf16[1,256,256]{2,1,0:T(8,128)(2,1)S(1)}, bf16[1,256,256]{2,1,0:T(8,128)(2,1)S(1)}, f32[128,1024]{1,0:T(8,128)S(1)}, f32[8,1024]{1,0:T(8,128)S(1)}) custom-call(s32[2048]{0:T(1024)S(1)} %copy-done, s32[8,256]{1,0:T(8,128)S(1)} %reshape.9.docs_ref, bf16[128,1024]{1,0:T(8,128)(2,1)S(1)} %get-tuple-element.21.qt_ref, ...), custom_call_target="tpu_custom_call" | custom-call | tf_op jit(solution)/shard_map/pallas_call | solution.py:270
  18.1 2.2 %shard_map.79 = (f32[256,256]{1,0:T(8,128)S(1)}, f32[256,256]{1,0:T(8,128)S(1)}, f32[256,256]{1,0:T(8,128)S(1)}) custom-call(s32[2048]{0:T(1024)S(1)} %copy-done, s32[8,256]{1,0:T(8,128)S(1)} %reshape.9.docs_ref, bf16[128,1024]{1,0:T(8,128)(2,1)S(1)} %get-tuple-element.21.qt_ref, bf16[128,1024]{1,0:T(8,128)(2,1)S(1)} %get-tuple-element.22.dot_ref, ...), custom_call_target="tpu_custom_call" | custom-call | flops 201326592 | bytes 2097152 | tf_op jit(solution)/shard_map/pallas_call | solution.py:270
  20.3 0.1 collective-permute-start.6
  20.4 1.3 %collective-permute-start.7 = (bf16[1,256,256]{2,1,0:T(8,128)(2,1)S(1)}, bf16[1,256,256]{2,1,0:T(8,128)(2,1)S(1)}, u32[]{:S(2)}, u32[]{:S(2)}) collective-permute-start(bf16[1,256,256]{2,1,0:T(8,128)(2,1)S(1)} %get-tuple-element.29), channel_id=1, source_target_pairs={{2,0},{3,1},{6,4},{7,5},{10,8},{11,9},{14,12},{15,13},{18,16},{19,... | collective-permute-start | bytes 393224 | tf_op jit(solution)/shard_map/ppermute | solution.py:340
  21.7 1.3 %collective-permute-start.8 = (bf16[1,256,256]{2,1,0:T(8,128)(2,1)S(1)}, bf16[1,256,256]{2,1,0:T(8,128)(2,1)S(1)}, u32[]{:S(2)}, u32[]{:S(2)}) collective-permute-start(bf16[1,256,256]{2,1,0:T(8,128)(2,1)S(1)} %get-tuple-element.30), channel_id=1, source_target_pairs={{4,0},{5,1},{6,2},{7,3},{12,8},{13,9},{14,10},{15,11},{20,16},{21,... | collective-permute-start | bytes 393224 | tf_op jit(solution)/shard_map/ppermute | solution.py:340
  23.0 1.3 %collective-permute-start.9 = (bf16[1,256,256]{2,1,0:T(8,128)(2,1)S(1)}, bf16[1,256,256]{2,1,0:T(8,128)(2,1)S(1)}, u32[]{:S(2)}, u32[]{:S(2)}) collective-permute-start(bf16[1,256,256]{2,1,0:T(8,128)(2,1)S(1)} %get-tuple-element.31), channel_id=1, source_target_pairs={{6,0},{7,1},{4,2},{5,3},{14,8},{15,9},{12,10},{13,11},{22,16},{23,... | collective-permute-start | bytes 393224 | tf_op jit(solution)/shard_map/ppermute | solution.py:340
  24.3 4.4 %collective-permute-done.7.rest_0_ = bf16[1,256,256]{2,1,0:T(8,128)(2,1)S(1)} collective-permute-done((bf16[1,256,256]{2,1,0:T(8,128)(2,1)S(1)}, bf16[1,256,256]{2,1,0:T(8,128)(2,1)S(1)}, u32[]{:S(2)}, u32[]{:S(2)}) %collective-permute-start.7) | collective-permute-done | bytes 131104 | tf_op jit(solution)/shard_map/ppermute | solution.py:340
  28.6 3.4 %collective-permute-done.8.rest_1_ = bf16[1,256,256]{2,1,0:T(8,128)(2,1)S(1)} collective-permute-done((bf16[1,256,256]{2,1,0:T(8,128)(2,1)S(1)}, bf16[1,256,256]{2,1,0:T(8,128)(2,1)S(1)}, u32[]{:S(2)}, u32[]{:S(2)}) %collective-permute-start.8) | collective-permute-done | bytes 131104 | tf_op jit(solution)/shard_map/ppermute | solution.py:340
  32.0 3.3 %collective-permute-done.9.rest_2_ = bf16[1,256,256]{2,1,0:T(8,128)(2,1)S(1)} collective-permute-done((bf16[1,256,256]{2,1,0:T(8,128)(2,1)S(1)}, bf16[1,256,256]{2,1,0:T(8,128)(2,1)S(1)}, u32[]{:S(2)}, u32[]{:S(2)}) %collective-permute-start.9) | collective-permute-done | bytes 131104 | tf_op jit(solution)/shard_map/ppermute | solution.py:340
  35.3 0.8 %shard_map.80 = (bf16[256,256]{1,0:T(8,128)(2,1)}, f32[64,256]{1,0:T(8,128)S(1)}, bf16[64,256]{1,0:T(8,128)(2,1)S(1)}, bf16[64,256]{1,0:T(8,128)(2,1)S(1)}, bf16[64,256]{1,0:T(8,128)(2,1)S(1)}) custom-call(f32[256,256]{1,0:T(8,128)S(1)} %get-tuple-element.26.own_ref, f32[256,256]{1,0:T(8,128)S(1)} %get-tuple-element.27.dq_own, ...), custom_call_target="tpu_custom_call" | custom-call | tf_op jit(solution)/shard_map/pallas_call | solution.py:270
  36.1 1.6 %collective-permute-start.10 = (bf16[64,256]{1,0:T(8,128)(2,1)S(1)}, bf16[64,256]{1,0:T(8,128)(2,1)S(1)}, u32[]{:S(2)}, u32[]{:S(2)}) collective-permute-start(bf16[64,256]{1,0:T(8,128)(2,1)S(1)} %get-tuple-element.34), channel_id=1, source_target_pairs={{0,8},{8,0},{16,24},{24,16},{1,9},{9,1},{17,25},{25,17},{2,10},{10... | collective-permute-start | bytes 98312 | tf_op jit(solution)/shard_map/ppermute | solution.py:361
  37.6 2.6 %collective-permute-start.11 = (bf16[64,256]{1,0:T(8,128)(2,1)S(1)}, bf16[64,256]{1,0:T(8,128)(2,1)S(1)}, u32[]{:S(2)}, u32[]{:S(2)}) collective-permute-start(bf16[64,256]{1,0:T(8,128)(2,1)S(1)} %get-tuple-element.35), channel_id=1, source_target_pairs={{0,16},{8,24},{16,0},{24,8},{1,17},{9,25},{17,1},{25,9},{2,18},{10... | collective-permute-start | bytes 98312 | tf_op jit(solution)/shard_map/ppermute | solution.py:361
  40.2 0.2 collective-permute-start.12
  40.5 2.3 %collective-permute-done.11.rest_1_ = bf16[64,256]{1,0:T(8,128)(2,1)S(1)} collective-permute-done((bf16[64,256]{1,0:T(8,128)(2,1)S(1)}, bf16[64,256]{1,0:T(8,128)(2,1)S(1)}, u32[]{:S(2)}, u32[]{:S(2)}) %collective-permute-start.11) | collective-permute-done | bytes 32800 | tf_op jit(solution)/shard_map/ppermute | solution.py:361
  42.7 3.2 %collective-permute-done.12.rest_2_ = bf16[64,256]{1,0:T(8,128)(2,1)S(1)} collective-permute-done((bf16[64,256]{1,0:T(8,128)(2,1)S(1)}, bf16[64,256]{1,0:T(8,128)(2,1)S(1)}, u32[]{:S(2)}, u32[]{:S(2)}) %collective-permute-start.12) | collective-permute-done | bytes 32800 | tf_op jit(solution)/shard_map/ppermute | solution.py:361
  45.9 0.6 %shard_map.81 = (bf16[32,256]{1,0:T(8,128)(2,1)}, bf16[32,256]{1,0:T(8,128)(2,1)}) custom-call(f32[64,256]{1,0:T(8,128)S(1)} %get-tuple-element.33.keep_ref, bf16[64,256]{1,0:T(8,128)(2,1)S(1)} %collective-permute-done.10.rest_0_, bf16[64,256]{1,0:T(8,128)(2,1)S(1)} %collective-permute-done.11.rest_1_, bf16[64,256]{1,0:T(8,128)(2,1)S(1)} %collective-permute-done.12.rest_2_), custom_call_target="tpu_custom_call" | custom-call | tf_op jit(solution)/shard_map/pallas_call | solution.py:270
  (9 shorter events, 0.0 us)
Async XLA Ops:
  0.6 12.0 %copy-start.1 = (bf16[256,256]{1,0:T(8,128)(2,1)S(1)}, bf16[256,256]{1,0:T(8,128)(2,1)}, u32[]{:S(2)}) copy-start(bf16[256,256]{1,0:T(8,128)(2,1)} %q_own.1) | copy-start | bytes 393220
  0.6 12.0 %collective-permute-start = (bf16[256,256]{1,0:T(8,128)(2,1)}, bf16[256,256]{1,0:T(8,128)(2,1)S(1)}, u32[]{:S(2)}, u32[]{:S(2)}) collective-permute-start(bf16[256,256]{1,0:T(8,128)(2,1)} %q_own.1), channel_id=1, source_target_pairs={{0,1},{1,0},{2,3},{3,2},{4,5},{5,4},{6,7},{7,6},{8,9},{9,8},{10,11... | collective-permute-start | bytes 393224 | tf_op jit(solution)/shard_map/ppermute | solution.py:302
  1.2 11.5 %collective-permute-start.1 = (bf16[256,256]{1,0:T(8,128)(2,1)}, bf16[256,256]{1,0:T(8,128)(2,1)S(1)}, u32[]{:S(2)}, u32[]{:S(2)}) collective-permute-start(bf16[256,256]{1,0:T(8,128)(2,1)} %do_own.1), channel_id=1, source_target_pairs={{0,1},{1,0},{2,3},{3,2},{4,5},{5,4},{6,7},{7,6},{8,9},{9,8},{10,11... | collective-permute-start | bytes 393224 | tf_op jit(solution)/shard_map/ppermute | solution.py:302
  2.1 10.5 %copy-start = (s32[2048]{0:T(1024)S(1)}, s32[2048]{0:T(1024)}, u32[]{:S(2)}) copy-start(s32[2048]{0:T(1024)} %ids_ref.7) | copy-start | bytes 24580
  2.1 10.5 %copy-start.2 = (bf16[256,256]{1,0:T(8,128)(2,1)S(1)}, bf16[256,256]{1,0:T(8,128)(2,1)}, u32[]{:S(2)}) copy-start(bf16[256,256]{1,0:T(8,128)(2,1)} %do_own.1) | copy-start | bytes 393220
  3.0 11.1 %collective-permute-start.4 = (bf16[256,256]{1,0:T(8,128)(2,1)S(1)}, bf16[256,256]{1,0:T(8,128)(2,1)S(1)}, u32[]{:S(2)}, u32[]{:S(2)}) collective-permute-start(bf16[256,256]{1,0:T(8,128)(2,1)S(1)} %constant_dynamic-update-slice_fusion.kv_ref), channel_id=1, source_target_pairs={{0,6},{1,7},{2,4},{3,5},{8,14},{9,15},{10,12},{11,13},{16,22},{17,... | collective-permute-start | bytes 393224 | tf_op jit(solution)/shard_map/ppermute | solution.py:307
  8.8 5.8 %collective-permute-start.3 = (bf16[256,256]{1,0:T(8,128)(2,1)S(1)}, bf16[256,256]{1,0:T(8,128)(2,1)S(1)}, u32[]{:S(2)}, u32[]{:S(2)}) collective-permute-start(bf16[256,256]{1,0:T(8,128)(2,1)S(1)} %constant_dynamic-update-slice_fusion.kv_ref), channel_id=1, source_target_pairs={{0,4},{1,5},{2,6},{3,7},{8,12},{9,13},{10,14},{11,15},{16,20},{17,... | collective-permute-start | bytes 393224 | tf_op jit(solution)/shard_map/ppermute | solution.py:307
  10.1 5.2 %collective-permute-start.2 = (bf16[256,256]{1,0:T(8,128)(2,1)S(1)}, bf16[256,256]{1,0:T(8,128)(2,1)S(1)}, u32[]{:S(2)}, u32[]{:S(2)}) collective-permute-start(bf16[256,256]{1,0:T(8,128)(2,1)S(1)} %constant_dynamic-update-slice_fusion.kv_ref), channel_id=1, source_target_pairs={{0,2},{1,3},{4,6},{5,7},{8,10},{9,11},{12,14},{13,15},{16,18},{17,... | collective-permute-start | bytes 393224 | tf_op jit(solution)/shard_map/ppermute | solution.py:307
  16.0 1.3 %collective-permute-start.5 = (f32[8,1024]{1,0:T(8,128)S(1)}, f32[8,1024]{1,0:T(8,128)S(1)}, u32[]{:S(2)}, u32[]{:S(2)}) collective-permute-start(f32[8,1024]{1,0:T(8,128)S(1)} %shard_map.77.stats_ref), channel_id=1, source_target_pairs={{0,1},{1,0},{2,3},{3,2},{4,5},{5,4},{6,7},{7,6},{8,9},{9,8},{10,11... | collective-permute-start | bytes 98312 | tf_op jit(solution)/shard_map/ppermute | solution.py:302
  20.3 15.0 %collective-permute-start.6 = (f32[256,256]{1,0:T(8,128)S(1)}, f32[256,256]{1,0:T(8,128)S(1)}, u32[]{:S(2)}, u32[]{:S(2)}) collective-permute-start(f32[256,256]{1,0:T(8,128)S(1)} %get-tuple-element.28), channel_id=1, source_target_pairs={{0,1},{1,0},{2,3},{3,2},{4,5},{5,4},{6,7},{7,6},{8,9},{9,8},{10,11... | collective-permute-start | bytes 786440 | tf_op jit(solution)/shard_map/ppermute | solution.py:302
  20.4 8.3 %collective-permute-start.7 = (bf16[1,256,256]{2,1,0:T(8,128)(2,1)S(1)}, bf16[1,256,256]{2,1,0:T(8,128)(2,1)S(1)}, u32[]{:S(2)}, u32[]{:S(2)}) collective-permute-start(bf16[1,256,256]{2,1,0:T(8,128)(2,1)S(1)} %get-tuple-element.29), channel_id=1, source_target_pairs={{2,0},{3,1},{6,4},{7,5},{10,8},{11,9},{14,12},{15,13},{18,16},{19,... | collective-permute-start | bytes 393224 | tf_op jit(solution)/shard_map/ppermute | solution.py:340
  21.7 10.3 %collective-permute-start.8 = (bf16[1,256,256]{2,1,0:T(8,128)(2,1)S(1)}, bf16[1,256,256]{2,1,0:T(8,128)(2,1)S(1)}, u32[]{:S(2)}, u32[]{:S(2)}) collective-permute-start(bf16[1,256,256]{2,1,0:T(8,128)(2,1)S(1)} %get-tuple-element.30), channel_id=1, source_target_pairs={{4,0},{5,1},{6,2},{7,3},{12,8},{13,9},{14,10},{15,11},{20,16},{21,... | collective-permute-start | bytes 393224 | tf_op jit(solution)/shard_map/ppermute | solution.py:340
  23.0 12.3 %collective-permute-start.9 = (bf16[1,256,256]{2,1,0:T(8,128)(2,1)S(1)}, bf16[1,256,256]{2,1,0:T(8,128)(2,1)S(1)}, u32[]{:S(2)}, u32[]{:S(2)}) collective-permute-start(bf16[1,256,256]{2,1,0:T(8,128)(2,1)S(1)} %get-tuple-element.31), channel_id=1, source_target_pairs={{6,0},{7,1},{4,2},{5,3},{14,8},{15,9},{12,10},{13,11},{22,16},{23,... | collective-permute-start | bytes 393224 | tf_op jit(solution)/shard_map/ppermute | solution.py:340
  36.1 4.4 %collective-permute-start.10 = (bf16[64,256]{1,0:T(8,128)(2,1)S(1)}, bf16[64,256]{1,0:T(8,128)(2,1)S(1)}, u32[]{:S(2)}, u32[]{:S(2)}) collective-permute-start(bf16[64,256]{1,0:T(8,128)(2,1)S(1)} %get-tuple-element.34), channel_id=1, source_target_pairs={{0,8},{8,0},{16,24},{24,16},{1,9},{9,1},{17,25},{25,17},{2,10},{10... | collective-permute-start | bytes 98312 | tf_op jit(solution)/shard_map/ppermute | solution.py:361
  37.6 5.1 %collective-permute-start.11 = (bf16[64,256]{1,0:T(8,128)(2,1)S(1)}, bf16[64,256]{1,0:T(8,128)(2,1)S(1)}, u32[]{:S(2)}, u32[]{:S(2)}) collective-permute-start(bf16[64,256]{1,0:T(8,128)(2,1)S(1)} %get-tuple-element.35), channel_id=1, source_target_pairs={{0,16},{8,24},{16,0},{24,8},{1,17},{9,25},{17,1},{25,9},{2,18},{10... | collective-permute-start | bytes 98312 | tf_op jit(solution)/shard_map/ppermute | solution.py:361
  40.2 5.7 %collective-permute-start.12 = (bf16[64,256]{1,0:T(8,128)(2,1)S(1)}, bf16[64,256]{1,0:T(8,128)(2,1)S(1)}, u32[]{:S(2)}, u32[]{:S(2)}) collective-permute-start(bf16[64,256]{1,0:T(8,128)(2,1)S(1)} %get-tuple-element.36), channel_id=1, source_target_pairs={{0,24},{8,16},{16,8},{24,0},{1,25},{9,17},{17,9},{25,1},{2,26},{10... | collective-permute-start | bytes 98312 | tf_op jit(solution)/shard_map/ppermute | solution.py:361

commit v2 on v1

v2 whole, which is shorter than its diff:
```python
import functools

import jax
import jax.numpy as jnp
from jax import lax
from jax.experimental import pallas as pl
from jax.experimental.pallas import tpu as pltpu
from jax.sharding import PartitionSpec as P

HD = 128
SCALE = HD**-0.5
LOG2E = 1.4426950408889634
MASKED = -1.0e30
LOWEST = -1.0e20
F32 = jnp.float32
BF16 = jnp.bfloat16


def nn(a, b):
    return lax.dot_general(a, b, (((1,), (0,)), ((), ())), preferred_element_type=F32)


def nt(a, b):
    return lax.dot_general(a, b, (((1,), (1,)), ((), ())), preferred_element_type=F32)


def tn(a, b):
    return lax.dot_general(a, b, (((0,), (0,)), ((), ())), preferred_element_type=F32)


def key_doc_column(docs_ref, block):
    row = docs_ref[pl.ds(block, 1), :]
    span = row.shape[1]
    column = jnp.transpose(jnp.broadcast_to(row, (128, span)))
    return jnp.concatenate([column] * (span // 128), axis=1)


def scores_of(kv, qt, key_doc, row_doc, causal):
    scores = nn(kv[:, :HD], qt) * (SCALE * LOG2E)
    allowed = key_doc == row_doc
    if causal:
        key_pos = lax.broadcasted_iota(jnp.int32, scores.shape, 0)
        row_pos = lax.broadcasted_iota(jnp.int32, scores.shape, 1)
        allowed = allowed & (key_pos <= row_pos)
    return jnp.where(allowed, scores, MASKED)


def add_stats(stats_ref, kv, qd_ref, docs_ref, key_block, row_block, side, causal):
    rows = docs_ref.shape[1]
    key_doc = key_doc_column(docs_ref, key_block)
    row_doc = docs_ref[pl.ds(row_block, 1), :]
    heads = qd_ref.shape[1] // rows
    for head in range(heads):
        local = slice(head * rows, (head + 1) * rows)
        lanes = slice((side * heads + head) * rows, (side * heads + head + 1) * rows)
        scores = scores_of(kv, qd_ref[:HD, local], key_doc, row_doc, causal)
        grad_probs = nn(kv[:, HD:], qd_ref[HD:, local])
        old = stats_ref[0:1, lanes]
        new = jnp.maximum(old, jnp.max(scores, axis=0, keepdims=True))
        factor = jnp.exp2(old - new)
        weights = jnp.exp2(scores - new)
        stats_ref[0:1, lanes] = new
        stats_ref[1:2, lanes] = stats_ref[1:2, lanes] * factor + jnp.sum(
            weights, axis=0, keepdims=True
        )
        stats_ref[2:3, lanes] = stats_ref[2:3, lanes] * factor + jnp.sum(
            weights * grad_probs, axis=0, keepdims=True
        )


def add_grads(kv, qd_ref, docs_ref, key_block, row_block, side, causal, norm_ref, dqt_ref):
    rows = docs_ref.shape[1]
    key_doc = key_doc_column(docs_ref, key_block)
    row_doc = docs_ref[pl.ds(row_block, 1), :]
    dkt = jnp.zeros((HD, rows), F32)
    dvt = jnp.zeros((HD, rows), F32)
    heads = qd_ref.shape[1] // rows
    for head in range(heads):
        local = slice(head * rows, (head + 1) * rows)
        lanes = slice((side * heads + head) * rows, (side * heads + head + 1) * rows)
        qt = qd_ref[:HD, local]
        dot = qd_ref[HD:, local]
        scores = scores_of(kv, qt, key_doc, row_doc, causal)
        weights = jnp.exp2(scores - norm_ref[0:1, lanes])
        grad_probs = nn(kv[:, HD:], dot)
        grad_scores = (weights * (grad_probs - norm_ref[1:2, lanes])).astype(BF16)
        dkt += nt(qt, grad_scores)
        dvt += nt(dot, weights.astype(BF16))
        dqt_ref[:, lanes] += tn(kv[:, :HD], grad_scores)
    return dkt, dvt


def place():
    srv = lax.axis_index("srv")
    return srv // 2, srv % 2


def reaches(ids_ref, rows, key_block, row_block):
    return ids_ref[key_block * rows + rows - 1] >= ids_ref[row_block * rows]


def pack_kernel(key_ref, value_ref, kv_ref):
    kv_ref[:, :HD] = key_ref[...]
    kv_ref[:, HD:] = value_ref[...]


def turn_kernel(q_ref, do_ref, after_ref, qd_ref):
    rows, columns = q_ref.shape
    for top, ref in ((0, q_ref), (HD, do_ref)):
        turned = jnp.transpose(ref[...])
        for head in range(columns // HD):
            qd_ref[top : top + HD, head * rows : (head + 1) * rows] = turned[
                head * HD : (head + 1) * HD, :
            ]


def own_stats_kernel(ids_ref, docs_ref, qd_own, qd_par, kv_ref, stats_ref):
    rows = docs_ref.shape[1]
    chip, core = place()
    stats_ref[...] = jnp.zeros(stats_ref.shape, F32)
    stats_ref[0:1, :] = jnp.full((1, stats_ref.shape[1]), LOWEST, F32)
    block = chip * 2 + core
    kv = kv_ref[...]
    add_stats(stats_ref, kv, qd_own, docs_ref, block, block, 0, True)
    other = chip * 2 + 1 - core

    @pl.when((core == 0) & reaches(ids_ref, rows, block, other))
    def _():
        add_stats(stats_ref, kv, qd_par, docs_ref, block, other, 1, False)


def each_remote(groups, ids_ref, rows, body):
    chip, core = place()

    def step(group, slot, away):
        source = chip ^ away
        key_block = source * 2 + core
        for side in range(2):
            row_block = chip * 2 + (core if side == 0 else 1 - core)
            active = (source < chip) & reaches(ids_ref, rows, key_block, row_block)
            pl.when(active)(functools.partial(body, group, slot, key_block, row_block, side))

    first = 1
    for group, amount in enumerate(groups):
        if amount == 1:
            step(group, 0, first)
        else:
            base = first

            @pl.loop(0, amount)
            def _(slot):
                step(group, slot, base + slot)

        first += amount


def far_stats_kernel(groups, ids_ref, docs_ref, qd_own, qd_par, stats_in, *rest):
    kv_refs, stats_ref = rest[:-1], rest[-1]
    rows = docs_ref.shape[1]
    stats_ref[...] = stats_in[...]

    def body(group, slot, key_block, row_block, side):
        qd_ref = (qd_own, qd_par)[side]
        kv = kv_refs[group][slot]
        add_stats(stats_ref, kv, qd_ref, docs_ref, key_block, row_block, side, False)

    each_remote(groups, ids_ref, rows, body)


def far_grads_kernel(groups, ids_ref, docs_ref, qd_own, qd_par, stats_ref, other_ref, *rest):
    count = len(groups)
    kv_refs, out_refs = rest[:count], rest[count : 2 * count]
    dqt_ref, norm_ref = rest[2 * count :]
    rows = docs_ref.shape[1]
    half = qd_own.shape[1]
    mine = stats_ref[...]
    other = other_ref[...]
    other = jnp.concatenate([other[:, half:], other[:, :half]], axis=1)
    top = jnp.maximum(mine[0:1], other[0:1])
    mine_by = jnp.exp2(mine[0:1] - top)
    other_by = jnp.exp2(other[0:1] - top)
    total = mine[1:2] * mine_by + other[1:2] * other_by
    norm_ref[...] = jnp.zeros(norm_ref.shape, F32)
    norm_ref[0:1, :] = top + jnp.log2(total)
    norm_ref[1:2, :] = (mine[2:3] * mine_by + other[2:3] * other_by) / total
    dqt_ref[...] = jnp.zeros(dqt_ref.shape, F32)
    for out_ref in out_refs:
        out_ref[...] = jnp.zeros(out_ref.shape, BF16)

    def body(group, slot, key_block, row_block, side):
        qd_ref = (qd_own, qd_par)[side]
        kv = kv_refs[group][slot]
        dkt, dvt = add_grads(
            kv, qd_ref, docs_ref, key_block, row_block, side, False, norm_ref, dqt_ref
        )
        both = jnp.concatenate([dkt * SCALE, dvt], axis=0)
        if side == 1:
            both = both + out_refs[group][slot].astype(F32)
        out_refs[group][slot] = both.astype(BF16)

    each_remote(groups, ids_ref, rows, body)


def own_grads_kernel(
    ids_ref, docs_ref, qd_own, qd_par, norm_ref, kv_ref, dqt_in, dkv_ref, dq_own, dq_par, dqt_ref
):
    rows = docs_ref.shape[1]
    heads = qd_own.shape[1] // rows
    chip, core = place()
    block = chip * 2 + core
    other = chip * 2 + 1 - core
    dqt_ref[...] = dqt_in[...]
    kv = kv_ref[...]
    dkt, dvt = add_grads(kv, qd_own, docs_ref, block, block, 0, True, norm_ref, dqt_ref)
    dkv_ref[...] = jnp.concatenate([dkt * SCALE, dvt], axis=0)

    @pl.when((core == 0) & reaches(ids_ref, rows, block, other))
    def _():
        dkt, dvt = add_grads(kv, qd_par, docs_ref, block, other, 1, False, norm_ref, dqt_ref)
        dkv_ref[...] += jnp.concatenate([dkt * SCALE, dvt], axis=0)

    for side, out_ref in enumerate((dq_own, dq_par)):
        for head in range(heads):
            chunk = side * heads + head
            out_ref[head * HD : (head + 1) * HD, :] = (
                dqt_ref[:, chunk * rows : (chunk + 1) * rows] * SCALE
            )


def query_kernel(dq_own, dq_far, dq_ref, token_ref):
    token_ref[...] = jnp.zeros(token_ref.shape, F32)
    dq_ref[...] = jnp.transpose(dq_own[...] + dq_far[...]).astype(BF16)


def combine_kernel(share, count, dq_in, own_ref, *rest):
    parts, outs = rest[:count], rest[count:]
    keep_ref, send_refs, sum_ref = outs[1], outs[2:-1], outs[-1]
    width = HD // share
    total = own_ref[...]
    for part in parts:
        for slot in range(part.shape[0]):
            total = total + part[slot].astype(F32)
    sum_ref[...] = total
    member = lax.axis_index("grp") % share
    for away, out_ref in enumerate((keep_ref, *send_refs)):
        first = pl.multiple_of((member ^ away) * width, width)
        for half in range(2):
            piece = sum_ref[pl.ds(half * HD + first, width), :]
            out_ref[half * width : (half + 1) * width, :] = piece.astype(out_ref.dtype)


def finish_kernel(after_ref, keep_ref, *rest):
    parts, (dk_ref, dv_ref) = rest[:-2], rest[-2:]
    total = keep_ref[...]
    for part in parts:
        total = total + part[...].astype(F32)
    width = total.shape[0] // 2
    dk_ref[...] = total[:width].astype(BF16)
    dv_ref[...] = total[width:].astype(BF16)


SMEM = pl.BlockSpec(memory_space=pltpu.SMEM)
VMEM = pl.BlockSpec(memory_space=pltpu.VMEM)
ANY = pl.BlockSpec(memory_space=pl.ANY)


def call(kernel, out_shape, operands, scratch=(), smem=0, unread=(), aliases={}, us=0):
    kinds = [SMEM] * smem + [VMEM] * (len(operands) - smem)
    results = [VMEM] * len(out_shape)
    for place_of in unread:
        kinds[place_of] = ANY
    for source, target in aliases.items():
        kinds[source] = ANY
        results[target] = ANY
    cost = pl.CostEstimate(flops=us * 10**9, bytes_accessed=1 << 19, transcendentals=0)
    return pl.pallas_call(
        kernel,
        out_shape=out_shape,
        in_specs=kinds,
        out_specs=results,
        scratch_shapes=list(scratch),
        input_output_aliases=aliases,
        cost_estimate=cost,
        compiler_params=pltpu.CompilerParams(vmem_limit_bytes=24 << 20),
    )(*operands)


def sds(shape, dtype):
    return jax.ShapeDtypeStruct(shape, dtype)


def on_device(queries, key_rows, value_rows, grad_output, doc_ids):
    rows, columns = queries.shape
    heads = columns // HD
    srv = lax.axis_size("srv")
    chips = srv // 2
    grp = lax.axis_size("grp")
    kv_heads = key_rows.shape[1] // HD
    share = grp // kv_heads
    lanes = 2 * heads * rows
    if kv_heads > 1:
        first = lax.axis_index("grp") // share * HD
        key_rows = lax.dynamic_slice_in_dim(key_rows, first, HD, 1)
        value_rows = lax.dynamic_slice_in_dim(value_rows, first, HD, 1)
    (own_kv,) = call(pack_kernel, [sds((rows, 2 * HD), BF16)], [key_rows, value_rows])
    docs = doc_ids.reshape(srv, rows)

    def trade(block, away):
        return lax.ppermute(block, "srv", [(i, i ^ 2 * away) for i in range(srv)])

    def swap(block):
        return lax.ppermute(block, "srv", [(i, i ^ 1) for i in range(srv)])

    far_kv = [trade(own_kv, away)[None] for away in range(chips - 1, 0, -1)][::-1]
    groups = [1] * len(far_kv)
    if chips > 4:
        groups = [len(far_kv)]
        far_kv = [jnp.concatenate(far_kv, axis=0)]
    (qd_own,) = call(
        turn_kernel,
        [sds((2 * HD, heads * rows), BF16)],
        [queries, grad_output, own_kv],
        unread=[2],
    )
    qd_par = swap(qd_own)
    shared = [doc_ids, docs, qd_own, qd_par]
    (stats,) = call(
        own_stats_kernel, [sds((8, lanes), F32)], [*shared, own_kv], smem=1
    )
    (stats,) = call(
        functools.partial(far_stats_kernel, groups),
        [sds((8, lanes), F32)],
        [*shared, stats, *far_kv],
        smem=1,
    )
    other_stats = swap(stats)
    *far_dkv, dqt, norm = call(
        functools.partial(far_grads_kernel, groups),
        [sds((amount, 2 * HD, rows), BF16) for amount in groups]
        + [sds((HD, lanes), F32), sds((8, lanes), F32)],
        [*shared, stats, other_stats, *far_kv],
        smem=1,
    )
    if chips > 4:
        far_dkv = [far_dkv[0][i : i + 1] for i in range(chips - 1)]
    came = [trade(part, away + 1) for away, part in enumerate(far_dkv)]
    own_dkv, dq_own, dq_par = call(
        own_grads_kernel,
        [sds((2 * HD, rows), F32)] + [sds((columns, rows), F32)] * 2,
        [*shared, norm, own_kv, dqt],
        scratch=[pltpu.VMEM((HD, lanes), F32)],
        smem=1,
        us=4,
    )
    width = HD // share
    dq_par, keep, *send = call(
        functools.partial(combine_kernel, share, len(came)),
        [sds(dq_par.shape, F32), sds((2 * width, rows), F32)]
        + [sds((2 * width, rows), BF16)] * (share - 1),
        [dq_par, own_dkv, *came],
        scratch=[pltpu.VMEM((2 * HD, rows), F32)],
        aliases={0: 0},
    )
    back = [
        lax.ppermute(part, "grp", [(i, i ^ (away + 1)) for i in range(grp)])
        for away, part in enumerate(send)
    ]
    grad_query, token = call(
        query_kernel,
        [sds((rows, columns), BF16), sds((8, 128), F32)],
        [dq_own, swap(dq_par)],
        us=2,
    )
    grad_key, grad_value = call(
        finish_kernel,
        [sds((width, rows), BF16)] * 2,
        [token, keep, *back],
        unread=[0],
    )
    return grad_query, grad_key.T, grad_value.T


def solution(mesh):
    in_specs = (P("srv", "grp"), P("srv", None), P("srv", None), P("srv", "grp"), P())
    out_specs = (P("srv", "grp"), P("srv", "grp"), P("srv", "grp"))
    return jax.shard_map(
        on_device, mesh=mesh, in_specs=in_specs, out_specs=out_specs, check_vma=False
    )
```

time: 46.9 us -> 40.5 us (0.86)
  waiting for transfers between devices: 18.9 us -> 15.4 us
  starting transfers between devices: 18.6 us -> 15.7 us
    ppermute x6, starting transfers between devices: 13.4 us -> 10.5 us  [trade(): return lax.ppermute(block, 'srv', [(i, i ^ 2 * away) for i in range(srv)])]
    ppermute x6, waiting for transfers between devices: 12.2 us -> 9.31 us  [trade(): return lax.ppermute(block, 'srv', [(i, i ^ 2 * away) for i in range(srv)])]
    concatenate x1 -> x0, local copies, waits for them, and re-layouts: 0.89 us -> none  [on_device(): own_kv = jnp.concatenate([key_rows, value_rows], axis=1)]
    unnamed x7 -> x10, local copies, waits for them, and re-layouts: 0.87 us -> 1.73 us
    ppermute x3, waiting for transfers between devices: 5.49 us -> 4.93 us  [on_device(): lax.ppermute(part, 'grp', [(i, i ^ away + 1) for i in range(grp)])]
    pallas_call x6 -> x9, Pallas kernels: 6.57 us -> 6.72 us  [call(): pl.pallas_call(kernel, out_shape=out_shape, in_specs=kinds, out_specs=res...]
    ppermute x4 -> x3, waiting for transfers between devices: 1.2 us -> 1.2 us  [swap(): return lax.ppermute(block, 'srv', [(i, i ^ 1) for i in range(srv)])]
  transfers between devices with their start and end apart: 13 -> 12, of which waited for: 8 -> 7; matrix products, arithmetic and copies ran while one was open for 4% -> 0% of each run, Pallas kernels for 3% -> 11%
where the time goes in v2:
time: 40.5 us; the launch traced here: 40.3 us
  starting transfers between devices  15.7 us (39%)
  waiting for transfers between devices  15.4 us (38%)
  Pallas kernels  6.72 us (17%)
  local copies, waits for them, and re-layouts  1.73 us (4%)
  between operations  0.76 us (2%)
    ppermute x6, starting transfers between devices, trade(): return lax.ppermute(block, 'srv', [(i, i ^ 2 * away) for i in range(srv)])  10.5 us
    ppermute x6, waiting for transfers between devices, trade(): return lax.ppermute(block, 'srv', [(i, i ^ 2 * away) for i in range(srv)])  9.31 us
    pallas_call x9, Pallas kernels, call(): pl.pallas_call(kernel, out_shape=out_shape, in_specs=kinds, out_specs=res...  6.72 us
    ppermute x3, waiting for transfers between devices, on_device(): lax.ppermute(part, 'grp', [(i, i ^ away + 1) for i in range(grp)])  4.93 us
    ppermute x3, starting transfers between devices, on_device(): lax.ppermute(part, 'grp', [(i, i ^ away + 1) for i in range(grp)])  4.45 us
    unnamed x10, local copies, waits for them, and re-layouts  1.73 us
    ppermute x3, waiting for transfers between devices, swap(): return lax.ppermute(block, 'srv', [(i, i ^ 1) for i in range(srv)])  1.2 us
  transfers between devices with their start and end apart: 12, of which 7 were waited for; matrix products, arithmetic and copies ran while one was open for 0% of the time, Pallas kernels for 11%

profile of v2, /device:TPU:0, one launch (start us, length us, event | category | flops | bytes accessed | tf_op | source)
XLA Modules:
  0.0 40.3 jit_solution(2718723371134198254)
XLA Ops:
  0.7 0.9 %copy-done.3 = bf16[256,128]{1,0:T(8,128)(2,1)S(1)} copy-done((bf16[256,128]{1,0:T(8,128)(2,1)S(1)}, bf16[256,128]{1,0:T(8,128)(2,1)}, u32[]{:S(2)}) %copy-start.3) | copy-done | bytes 65560
  1.5 0.8 %copy-done.4 = bf16[256,128]{1,0:T(8,128)(2,1)S(1)} copy-done((bf16[256,128]{1,0:T(8,128)(2,1)S(1)}, bf16[256,128]{1,0:T(8,128)(2,1)}, u32[]{:S(2)}) %copy-start.4) | copy-done | bytes 65560
  2.4 0.0 copy-start
  2.4 0.1 shard_map.77.qd_own
  2.6 0.5 %collective-permute-start = (bf16[256,512]{1,0:T(8,128)(2,1)S(1)}, bf16[256,512]{1,0:T(8,128)(2,1)S(1)}, u32[]{:S(2)}, u32[]{:S(2)}) collective-permute-start(bf16[256,512]{1,0:T(8,128)(2,1)S(1)} %shard_map.77.qd_own), channel_id=1, source_target_pairs={{0,1},{1,0},{2,3},{3,2},{4,5},{5,4},{6,7},{7,6},{8,9},{9,8},{10,11... | collective-permute-start | bytes 786440 | tf_op jit(solution)/shard_map/ppermute | solution.py:312
  3.1 3.5 %collective-permute-start.3 = (bf16[256,256]{1,0:T(8,128)(2,1)S(1)}, bf16[256,256]{1,0:T(8,128)(2,1)S(1)}, u32[]{:S(2)}, u32[]{:S(2)}) collective-permute-start(bf16[256,256]{1,0:T(8,128)(2,1)S(1)} %shard_map.76.after_ref.kv_ref), channel_id=1, source_target_pairs={{0,6},{1,7},{2,4},{3,5},{4,2},{5,3},{6,0},{7,1},{8,14},{9,15},{10,... | collective-permute-start | bytes 393224 | tf_op jit(solution)/shard_map/ppermute | solution.py:309
  6.6 0.5 %collective-permute-start.2 = (bf16[256,256]{1,0:T(8,128)(2,1)S(1)}, bf16[256,256]{1,0:T(8,128)(2,1)S(1)}, u32[]{:S(2)}, u32[]{:S(2)}) collective-permute-start(bf16[256,256]{1,0:T(8,128)(2,1)S(1)} %shard_map.76.after_ref.kv_ref), channel_id=1, source_target_pairs={{0,4},{1,5},{2,6},{3,7},{4,0},{5,1},{6,2},{7,3},{8,12},{9,13},{10,... | collective-permute-start | bytes 393224 | tf_op jit(solution)/shard_map/ppermute | solution.py:309
  7.1 0.1 collective-permute-start.1
  7.2 1.4 %shard_map.78.stats_in = f32[8,1024]{1,0:T(8,128)S(1)} custom-call(s32[2048]{0:T(1024)S(1)} %copy-done, s32[8,256]{1,0:T(8,128)S(1)} %reshape.9.docs_ref, bf16[256,512]{1,0:T(8,128)(2,1)S(1)} %shard_map.77.qd_own, bf16[256,512]{1,0:T(8,128)(2,1)S(1)} %collective-permute-done.qd_par, bf16[256,256]{1,0:T(8,128)(2,1)S(1)} %shard_map.76.after_ref.kv_ref), custom_call_target="tpu_custom_call" | custom-call | bytes 524288 | tf_op jit(solution)/shard_map/pallas_call | solution.py:276
  8.7 2.1 %collective-permute-done.3 = bf16[256,256]{1,0:T(8,128)(2,1)S(1)} collective-permute-done((bf16[256,256]{1,0:T(8,128)(2,1)S(1)}, bf16[256,256]{1,0:T(8,128)(2,1)S(1)}, u32[]{:S(2)}, u32[]{:S(2)}) %collective-permute-start.3) | collective-permute-done | bytes 131104 | tf_op jit(solution)/shard_map/ppermute | solution.py:309
  10.8 2.7 %collective-permute-done.2 = bf16[256,256]{1,0:T(8,128)(2,1)S(1)} collective-permute-done((bf16[256,256]{1,0:T(8,128)(2,1)S(1)}, bf16[256,256]{1,0:T(8,128)(2,1)S(1)}, u32[]{:S(2)}, u32[]{:S(2)}) %collective-permute-start.2) | collective-permute-done | bytes 131104 | tf_op jit(solution)/shard_map/ppermute | solution.py:309
  13.5 0.3 collective-permute-done.1
  13.8 0.7 %shard_map.79.stats_ref = f32[8,1024]{1,0:T(8,128)S(1)} custom-call(s32[2048]{0:T(1024)S(1)} %copy-done, s32[8,256]{1,0:T(8,128)S(1)} %reshape.9.docs_ref, bf16[256,512]{1,0:T(8,128)(2,1)S(1)} %shard_map.77.qd_own, bf16[256,512]{1,0:T(8,128)(2,1)S(1)} %collective-permute-done.qd_par, f32[8,1024]{1,0:T(8,128)S(1)} %shard_map.78.stats_in, ...), custom_call_target="tpu_custom_call" | custom-call | bytes 524288 | tf_op jit(solution)/shard_map/pallas_call | solution.py:276
  14.6 0.1 collective-permute-start.4
  14.6 1.2 %collective-permute-done.4.other_ref = f32[8,1024]{1,0:T(8,128)S(1)} collective-permute-done((f32[8,1024]{1,0:T(8,128)S(1)}, f32[8,1024]{1,0:T(8,128)S(1)}, u32[]{:S(2)}, u32[]{:S(2)}) %collective-permute-start.4) | collective-permute-done | bytes 32800 | tf_op jit(solution)/shard_map/ppermute | solution.py:312
  15.8 0.8 %shard_map.80 = (bf16[1,256,256]{2,1,0:T(8,128)(2,1)S(1)}, bf16[1,256,256]{2,1,0:T(8,128)(2,1)S(1)}, bf16[1,256,256]{2,1,0:T(8,128)(2,1)S(1)}, f32[128,1024]{1,0:T(8,128)S(1)}, f32[8,1024]{1,0:T(8,128)S(1)}) custom-call(s32[2048]{0:T(1024)S(1)} %copy-done, s32[8,256]{1,0:T(8,128)S(1)} %reshape.9.docs_ref, bf16[256,512]{1,0:T(8,128)(2,1)S(1)} %shard_map.77.qd_own, ...), custom_call_target="tpu_custom_call" | custom-call | bytes 524288 | tf_op jit(solution)/shard_map/pallas_call | solution.py:276
  16.6 1.6 %collective-permute-start.5 = (bf16[1,256,256]{2,1,0:T(8,128)(2,1)S(1)}, bf16[1,256,256]{2,1,0:T(8,128)(2,1)S(1)}, u32[]{:S(2)}, u32[]{:S(2)}) collective-permute-start(bf16[1,256,256]{2,1,0:T(8,128)(2,1)S(1)} %get-tuple-element.25), channel_id=1, source_target_pairs={{0,2},{1,3},{2,0},{3,1},{4,6},{5,7},{6,4},{7,5},{8,10},{9,11},{10,... | collective-permute-start | bytes 393224 | tf_op jit(solution)/shard_map/ppermute | solution.py:309
  18.2 4.8 %collective-permute-start.6 = (bf16[1,256,256]{2,1,0:T(8,128)(2,1)S(1)}, bf16[1,256,256]{2,1,0:T(8,128)(2,1)S(1)}, u32[]{:S(2)}, u32[]{:S(2)}) collective-permute-start(bf16[1,256,256]{2,1,0:T(8,128)(2,1)S(1)} %get-tuple-element.26), channel_id=1, source_target_pairs={{0,4},{1,5},{2,6},{3,7},{4,0},{5,1},{6,2},{7,3},{8,12},{9,13},{10,... | collective-permute-start | bytes 393224 | tf_op jit(solution)/shard_map/ppermute | solution.py:309
  23.0 0.0 collective-permute-start.7
  23.0 2.1 %shard_map.81 = (f32[256,256]{1,0:T(8,128)S(1)}, f32[256,256]{1,0:T(8,128)S(1)}, f32[256,256]{1,0:T(8,128)S(1)}) custom-call(s32[2048]{0:T(1024)S(1)} %copy-done, s32[8,256]{1,0:T(8,128)S(1)} %reshape.9.docs_ref, bf16[256,512]{1,0:T(8,128)(2,1)S(1)} %shard_map.77.qd_own, bf16[256,512]{1,0:T(8,128)(2,1)S(1)} %collective-permute-done.qd_par, ...), custom_call_target="tpu_custom_call" | custom-call | flops 4000000000 | bytes 524288 | tf_op jit(solution)/shard_map/pallas_call | solution.py:276
  25.2 0.0 collective-permute-done.5.rest_0_
  25.2 4.2 %collective-permute-done.6.rest_1_ = bf16[1,256,256]{2,1,0:T(8,128)(2,1)S(1)} collective-permute-done((bf16[1,256,256]{2,1,0:T(8,128)(2,1)S(1)}, bf16[1,256,256]{2,1,0:T(8,128)(2,1)S(1)}, u32[]{:S(2)}, u32[]{:S(2)}) %collective-permute-start.6) | collective-permute-done | bytes 131104 | tf_op jit(solution)/shard_map/ppermute | solution.py:309
  29.4 0.1 shard_map.82
  29.4 0.1 collective-permute-start.8
  29.5 1.9 %collective-permute-start.9 = (bf16[64,256]{1,0:T(8,128)(2,1)S(1)}, bf16[64,256]{1,0:T(8,128)(2,1)S(1)}, u32[]{:S(2)}, u32[]{:S(2)}) collective-permute-start(bf16[64,256]{1,0:T(8,128)(2,1)S(1)} %get-tuple-element.32), channel_id=1, source_target_pairs={{0,8},{8,0},{16,24},{24,16},{1,9},{9,1},{17,25},{25,17},{2,10},{10... | collective-permute-start | bytes 98312 | tf_op jit(solution)/shard_map/ppermute | solution.py:365
  31.4 2.6 %collective-permute-start.10 = (bf16[64,256]{1,0:T(8,128)(2,1)S(1)}, bf16[64,256]{1,0:T(8,128)(2,1)S(1)}, u32[]{:S(2)}, u32[]{:S(2)}) collective-permute-start(bf16[64,256]{1,0:T(8,128)(2,1)S(1)} %get-tuple-element.33), channel_id=1, source_target_pairs={{0,16},{8,24},{16,0},{24,8},{1,17},{9,25},{17,1},{25,9},{2,18},{10... | collective-permute-start | bytes 98312 | tf_op jit(solution)/shard_map/ppermute | solution.py:365
  34.0 0.0 collective-permute-start.11
  34.0 0.8 %shard_map.83 = (bf16[256,256]{1,0:T(8,128)(2,1)}, f32[8,128]{1,0:T(8,128)S(1)}) custom-call(f32[256,256]{1,0:T(8,128)S(1)} %get-tuple-element.22.dq_own, f32[256,256]{1,0:T(8,128)S(1)} %collective-permute-done.8.dq_far), custom_call_target="tpu_custom_call" | custom-call | flops 2000000000 | bytes 524288 | tf_op jit(solution)/shard_map/pallas_call | solution.py:276
  34.8 0.0 collective-permute-done.9.rest_0_
  34.8 2.0 %collective-permute-done.10.rest_1_ = bf16[64,256]{1,0:T(8,128)(2,1)S(1)} collective-permute-done((bf16[64,256]{1,0:T(8,128)(2,1)S(1)}, bf16[64,256]{1,0:T(8,128)(2,1)S(1)}, u32[]{:S(2)}, u32[]{:S(2)}) %collective-permute-start.10) | collective-permute-done | bytes 32800 | tf_op jit(solution)/shard_map/ppermute | solution.py:365
  36.8 2.9 %collective-permute-done.11.rest_2_ = bf16[64,256]{1,0:T(8,128)(2,1)S(1)} collective-permute-done((bf16[64,256]{1,0:T(8,128)(2,1)S(1)}, bf16[64,256]{1,0:T(8,128)(2,1)S(1)}, u32[]{:S(2)}, u32[]{:S(2)}) %collective-permute-start.11) | collective-permute-done | bytes 32800 | tf_op jit(solution)/shard_map/ppermute | solution.py:365
  39.7 0.6 %shard_map.84 = (bf16[32,256]{1,0:T(8,128)(2,1)}, bf16[32,256]{1,0:T(8,128)(2,1)}) custom-call(f32[8,128]{1,0:T(8,128)S(1)} %get-tuple-element.30.after_ref, f32[64,256]{1,0:T(8,128)S(1)} %get-tuple-element.31.keep_ref, bf16[64,256]{1,0:T(8,128)(2,1)S(1)} %collective-permute-done.9.rest_0_, bf16[64,256]{1,0:T(8,128)(2,1)S(1)} %collective-permute-done.10.rest_1_, ...), custom_call_target="tpu_custom_call" | custom-call | bytes 524288 | tf_op jit(solution)/shard_map/pallas_call | solution.py:276
  (12 shorter events, 0.0 us)
Async XLA Ops:
  0.6 1.8 %copy-start.2 = (bf16[256,256]{1,0:T(8,128)(2,1)S(1)}, bf16[256,256]{1,0:T(8,128)(2,1)}, u32[]{:S(2)}) copy-start(bf16[256,256]{1,0:T(8,128)(2,1)} %do_ref.1) | copy-start | bytes 393220
  0.6 1.8 %copy-start.1 = (bf16[256,256]{1,0:T(8,128)(2,1)S(1)}, bf16[256,256]{1,0:T(8,128)(2,1)}, u32[]{:S(2)}) copy-start(bf16[256,256]{1,0:T(8,128)(2,1)} %q_ref.1) | copy-start | bytes 393220
  0.7 0.9 %copy-start.3 = (bf16[256,128]{1,0:T(8,128)(2,1)S(1)}, bf16[256,128]{1,0:T(8,128)(2,1)}, u32[]{:S(2)}) copy-start(bf16[256,128]{1,0:T(8,128)(2,1)} %key_ref.1) | copy-start | bytes 196612
  1.5 0.8 %copy-start.4 = (bf16[256,128]{1,0:T(8,128)(2,1)S(1)}, bf16[256,128]{1,0:T(8,128)(2,1)}, u32[]{:S(2)}) copy-start(bf16[256,128]{1,0:T(8,128)(2,1)} %value_ref.1) | copy-start | bytes 196612
  2.4 4.8 %copy-start = (s32[2048]{0:T(1024)S(1)}, s32[2048]{0:T(1024)}, u32[]{:S(2)}) copy-start(s32[2048]{0:T(1024)} %ids_ref.7) | copy-start | bytes 24580
  2.6 4.7 %collective-permute-start = (bf16[256,512]{1,0:T(8,128)(2,1)S(1)}, bf16[256,512]{1,0:T(8,128)(2,1)S(1)}, u32[]{:S(2)}, u32[]{:S(2)}) collective-permute-start(bf16[256,512]{1,0:T(8,128)(2,1)S(1)} %shard_map.77.qd_own), channel_id=1, source_target_pairs={{0,1},{1,0},{2,3},{3,2},{4,5},{5,4},{6,7},{7,6},{8,9},{9,8},{10,11... | collective-permute-start | bytes 786440 | tf_op jit(solution)/shard_map/ppermute | solution.py:312
  3.1 7.7 %collective-permute-start.3 = (bf16[256,256]{1,0:T(8,128)(2,1)S(1)}, bf16[256,256]{1,0:T(8,128)(2,1)S(1)}, u32[]{:S(2)}, u32[]{:S(2)}) collective-permute-start(bf16[256,256]{1,0:T(8,128)(2,1)S(1)} %shard_map.76.after_ref.kv_ref), channel_id=1, source_target_pairs={{0,6},{1,7},{2,4},{3,5},{4,2},{5,3},{6,0},{7,1},{8,14},{9,15},{10,... | collective-permute-start | bytes 393224 | tf_op jit(solution)/shard_map/ppermute | solution.py:309
  6.6 6.9 %collective-permute-start.2 = (bf16[256,256]{1,0:T(8,128)(2,1)S(1)}, bf16[256,256]{1,0:T(8,128)(2,1)S(1)}, u32[]{:S(2)}, u32[]{:S(2)}) collective-permute-start(bf16[256,256]{1,0:T(8,128)(2,1)S(1)} %shard_map.76.after_ref.kv_ref), channel_id=1, source_target_pairs={{0,4},{1,5},{2,6},{3,7},{4,0},{5,1},{6,2},{7,3},{8,12},{9,13},{10,... | collective-permute-start | bytes 393224 | tf_op jit(solution)/shard_map/ppermute | solution.py:309
  7.1 6.7 %collective-permute-start.1 = (bf16[256,256]{1,0:T(8,128)(2,1)S(1)}, bf16[256,256]{1,0:T(8,128)(2,1)S(1)}, u32[]{:S(2)}, u32[]{:S(2)}) collective-permute-start(bf16[256,256]{1,0:T(8,128)(2,1)S(1)} %shard_map.76.after_ref.kv_ref), channel_id=1, source_target_pairs={{0,2},{1,3},{2,0},{3,1},{4,6},{5,7},{6,4},{7,5},{8,10},{9,11},{10,... | collective-permute-start | bytes 393224 | tf_op jit(solution)/shard_map/ppermute | solution.py:309
  14.6 1.3 %collective-permute-start.4 = (f32[8,1024]{1,0:T(8,128)S(1)}, f32[8,1024]{1,0:T(8,128)S(1)}, u32[]{:S(2)}, u32[]{:S(2)}) collective-permute-start(f32[8,1024]{1,0:T(8,128)S(1)} %shard_map.79.stats_ref), channel_id=1, source_target_pairs={{0,1},{1,0},{2,3},{3,2},{4,5},{5,4},{6,7},{7,6},{8,9},{9,8},{10,11... | collective-permute-start | bytes 98312 | tf_op jit(solution)/shard_map/ppermute | solution.py:312
  16.6 8.5 %collective-permute-start.5 = (bf16[1,256,256]{2,1,0:T(8,128)(2,1)S(1)}, bf16[1,256,256]{2,1,0:T(8,128)(2,1)S(1)}, u32[]{:S(2)}, u32[]{:S(2)}) collective-permute-start(bf16[1,256,256]{2,1,0:T(8,128)(2,1)S(1)} %get-tuple-element.25), channel_id=1, source_target_pairs={{0,2},{1,3},{2,0},{3,1},{4,6},{5,7},{6,4},{7,5},{8,10},{9,11},{10,... | collective-permute-start | bytes 393224 | tf_op jit(solution)/shard_map/ppermute | solution.py:309
  18.2 11.2 %collective-permute-start.6 = (bf16[1,256,256]{2,1,0:T(8,128)(2,1)S(1)}, bf16[1,256,256]{2,1,0:T(8,128)(2,1)S(1)}, u32[]{:S(2)}, u32[]{:S(2)}) collective-permute-start(bf16[1,256,256]{2,1,0:T(8,128)(2,1)S(1)} %get-tuple-element.26), channel_id=1, source_target_pairs={{0,4},{1,5},{2,6},{3,7},{4,0},{5,1},{6,2},{7,3},{8,12},{9,13},{10,... | collective-permute-start | bytes 393224 | tf_op jit(solution)/shard_map/ppermute | solution.py:309
  23.0 6.3 %collective-permute-start.7 = (bf16[1,256,256]{2,1,0:T(8,128)(2,1)S(1)}, bf16[1,256,256]{2,1,0:T(8,128)(2,1)S(1)}, u32[]{:S(2)}, u32[]{:S(2)}) collective-permute-start(bf16[1,256,256]{2,1,0:T(8,128)(2,1)S(1)} %get-tuple-element.27), channel_id=1, source_target_pairs={{0,6},{1,7},{2,4},{3,5},{4,2},{5,3},{6,0},{7,1},{8,14},{9,15},{10,... | collective-permute-start | bytes 393224 | tf_op jit(solution)/shard_map/ppermute | solution.py:309
  29.4 4.5 %collective-permute-start.8 = (f32[256,256]{1,0:T(8,128)S(1)}, f32[256,256]{1,0:T(8,128)S(1)}, u32[]{:S(2)}, u32[]{:S(2)}) collective-permute-start(f32[256,256]{1,0:T(8,128)S(1)} %get-tuple-element.28), channel_id=1, source_target_pairs={{0,1},{1,0},{2,3},{3,2},{4,5},{5,4},{6,7},{7,6},{8,9},{9,8},{10,11... | collective-permute-start | bytes 786440 | tf_op jit(solution)/shard_map/ppermute | solution.py:312
  29.5 5.2 %collective-permute-start.9 = (bf16[64,256]{1,0:T(8,128)(2,1)S(1)}, bf16[64,256]{1,0:T(8,128)(2,1)S(1)}, u32[]{:S(2)}, u32[]{:S(2)}) collective-permute-start(bf16[64,256]{1,0:T(8,128)(2,1)S(1)} %get-tuple-element.32), channel_id=1, source_target_pairs={{0,8},{8,0},{16,24},{24,16},{1,9},{9,1},{17,25},{25,17},{2,10},{10... | collective-permute-start | bytes 98312 | tf_op jit(solution)/shard_map/ppermute | solution.py:365
  31.4 5.4 %collective-permute-start.10 = (bf16[64,256]{1,0:T(8,128)(2,1)S(1)}, bf16[64,256]{1,0:T(8,128)(2,1)S(1)}, u32[]{:S(2)}, u32[]{:S(2)}) collective-permute-start(bf16[64,256]{1,0:T(8,128)(2,1)S(1)} %get-tuple-element.33), channel_id=1, source_target_pairs={{0,16},{8,24},{16,0},{24,8},{1,17},{9,25},{17,1},{25,9},{2,18},{10... | collective-permute-start | bytes 98312 | tf_op jit(solution)/shard_map/ppermute | solution.py:365
  34.0 5.7 %collective-permute-start.11 = (bf16[64,256]{1,0:T(8,128)(2,1)S(1)}, bf16[64,256]{1,0:T(8,128)(2,1)S(1)}, u32[]{:S(2)}, u32[]{:S(2)}) collective-permute-start(bf16[64,256]{1,0:T(8,128)(2,1)S(1)} %get-tuple-element.34), channel_id=1, source_target_pairs={{0,24},{8,16},{16,8},{24,0},{1,25},{9,17},{17,9},{25,1},{2,26},{10... | collective-permute-start | bytes 98312 | tf_op jit(solution)/shard_map/ppermute | solution.py:365

commit v3 on v2

--- a/solution.py
+++ b/solution.py
@@ -95,13 +95,20 @@
     return srv // 2, srv % 2
 
 
-def reaches(ids_ref, rows, key_block, row_block):
-    return ids_ref[key_block * rows + rows - 1] >= ids_ref[row_block * rows]
-
-
-def pack_kernel(key_ref, value_ref, kv_ref):
-    kv_ref[:, :HD] = key_ref[...]
-    kv_ref[:, HD:] = value_ref[...]
+def reaches(docs_ref, key_block, row_block):
+    last = docs_ref[pl.ds(key_block, 1), :][0, docs_ref.shape[1] - 1]
+    return last >= docs_ref[pl.ds(row_block, 1), :][0, 0]
+
+
+def pack_kernel(key_ref, value_ref, kv_ref, sems):
+    copies = [
+        pltpu.make_async_copy(ref, kv_ref.at[:, half * HD : (half + 1) * HD], sems.at[half])
+        for half, ref in enumerate((key_ref, value_ref))
+    ]
+    for copy in copies:
+        copy.start()
+    for copy in copies:
+        copy.wait()
 
 
 def turn_kernel(q_ref, do_ref, after_ref, qd_ref):
@@ -114,7 +121,7 @@
             ]
 
 
-def own_stats_kernel(ids_ref, docs_ref, qd_own, qd_par, kv_ref, stats_ref):
+def own_stats_kernel(docs_ref, qd_own, qd_par, kv_ref, stats_ref):
     rows = docs_ref.shape[1]
     chip, core = place()
     stats_ref[...] = jnp.zeros(stats_ref.shape, F32)
@@ -124,55 +131,40 @@
     add_stats(stats_ref, kv, qd_own, docs_ref, block, block, 0, True)
     other = chip * 2 + 1 - core
 
-    @pl.when((core == 0) & reaches(ids_ref, rows, block, other))
+    @pl.when((core == 0) & reaches(docs_ref, block, other))
     def _():
         add_stats(stats_ref, kv, qd_par, docs_ref, block, other, 1, False)
 
 
-def each_remote(groups, ids_ref, rows, body):
+def each_remote(first, count, docs_ref, body):
     chip, core = place()
 
-    def step(group, slot, away):
-        source = chip ^ away
+    def step(slot):
+        source = chip ^ (first + slot)
         key_block = source * 2 + core
         for side in range(2):
             row_block = chip * 2 + (core if side == 0 else 1 - core)
-            active = (source < chip) & reaches(ids_ref, rows, key_block, row_block)
-            pl.when(active)(functools.partial(body, group, slot, key_block, row_block, side))
-
-    first = 1
-    for group, amount in enumerate(groups):
-        if amount == 1:
-            step(group, 0, first)
-        else:
-            base = first
-
-            @pl.loop(0, amount)
-            def _(slot):
-                step(group, slot, base + slot)
-
-        first += amount
-
-
-def far_stats_kernel(groups, ids_ref, docs_ref, qd_own, qd_par, stats_in, *rest):
-    kv_refs, stats_ref = rest[:-1], rest[-1]
-    rows = docs_ref.shape[1]
+            active = (source < chip) & reaches(docs_ref, key_block, row_block)
+            pl.when(active)(functools.partial(body, slot, key_block, row_block, side))
+
+    if count == 1:
+        step(0)
+    else:
+        pl.loop(0, count)(step)
+
+
+def far_stats_kernel(first, docs_ref, qd_own, qd_par, stats_in, kv_ref, stats_ref):
     stats_ref[...] = stats_in[...]
 
-    def body(group, slot, key_block, row_block, side):
+    def body(slot, key_block, row_block, side):
         qd_ref = (qd_own, qd_par)[side]
-        kv = kv_refs[group][slot]
-        add_stats(stats_ref, kv, qd_ref, docs_ref, key_block, row_block, side, False)
-
-    each_remote(groups, ids_ref, rows, body)
-
-
-def far_grads_kernel(groups, ids_ref, docs_ref, qd_own, qd_par, stats_ref, other_ref, *rest):
-    count = len(groups)
-    kv_refs, out_refs = rest[:count], rest[count : 2 * count]
-    dqt_ref, norm_ref = rest[2 * count :]
-    rows = docs_ref.shape[1]
-    half = qd_own.shape[1]
+        add_stats(stats_ref, kv_ref[slot], qd_ref, docs_ref, key_block, row_block, side, False)
+
+    each_remote(first, kv_ref.shape[0], docs_ref, body)
+
+
+def norm_kernel(stats_ref, other_ref, norm_ref):
+    half = stats_ref.shape[1] // 2
     mine = stats_ref[...]
     other = other_ref[...]
     other = jnp.concatenate([other[:, half:], other[:, :half]], axis=1)
@@ -183,38 +175,38 @@
     norm_ref[...] = jnp.zeros(norm_ref.shape, F32)
     norm_ref[0:1, :] = top + jnp.log2(total)
     norm_ref[1:2, :] = (mine[2:3] * mine_by + other[2:3] * other_by) / total
+
+
+def far_grads_kernel(first, docs_ref, qd_own, qd_par, norm_ref, kv_ref, out_ref, dqt_ref):
     dqt_ref[...] = jnp.zeros(dqt_ref.shape, F32)
-    for out_ref in out_refs:
-        out_ref[...] = jnp.zeros(out_ref.shape, BF16)
-
-    def body(group, slot, key_block, row_block, side):
+    out_ref[...] = jnp.zeros(out_ref.shape, BF16)
+
+    def body(slot, key_block, row_block, side):
         qd_ref = (qd_own, qd_par)[side]
-        kv = kv_refs[group][slot]
         dkt, dvt = add_grads(
-            kv, qd_ref, docs_ref, key_block, row_block, side, False, norm_ref, dqt_ref
+            kv_ref[slot], qd_ref, docs_ref, key_block, row_block, side, False, norm_ref, dqt_ref
         )
         both = jnp.concatenate([dkt * SCALE, dvt], axis=0)
         if side == 1:
-            both = both + out_refs[group][slot].astype(F32)
-        out_refs[group][slot] = both.astype(BF16)
-
-    each_remote(groups, ids_ref, rows, body)
-
-
-def own_grads_kernel(
-    ids_ref, docs_ref, qd_own, qd_par, norm_ref, kv_ref, dqt_in, dkv_ref, dq_own, dq_par, dqt_ref
-):
+            both = both + out_ref[slot].astype(F32)
+        out_ref[slot] = both.astype(BF16)
+
+    each_remote(first, kv_ref.shape[0], docs_ref, body)
+
+
+def own_grads_kernel(docs_ref, qd_own, qd_par, norm_ref, kv_ref, *rest):
+    dqt_in, (dkv_ref, dq_own, dq_par, dqt_ref) = rest[:-4], rest[-4:]
     rows = docs_ref.shape[1]
     heads = qd_own.shape[1] // rows
     chip, core = place()
     block = chip * 2 + core
     other = chip * 2 + 1 - core
-    dqt_ref[...] = dqt_in[...]
+    dqt_ref[...] = sum(part[...] for part in dqt_in)
     kv = kv_ref[...]
     dkt, dvt = add_grads(kv, qd_own, docs_ref, block, block, 0, True, norm_ref, dqt_ref)
     dkv_ref[...] = jnp.concatenate([dkt * SCALE, dvt], axis=0)
 
-    @pl.when((core == 0) & reaches(ids_ref, rows, block, other))
+    @pl.when((core == 0) & reaches(docs_ref, block, other))
     def _():
         dkt, dvt = add_grads(kv, qd_par, docs_ref, block, other, 1, False, norm_ref, dqt_ref)
         dkv_ref[...] += jnp.concatenate([dkt * SCALE, dvt], axis=0)
@@ -238,11 +230,10 @@
     width = HD // share
     total = own_ref[...]
     for part in parts:
-        for slot in range(part.shape[0]):
-            total = total + part[slot].astype(F32)
+        total = total + part[...].astype(F32)
     sum_ref[...] = total
     member = lax.axis_index("grp") % share
-    for away, out_ref in enumerate((keep_ref, *send_refs)):
+    for away, out_ref in zip((0, *range(share - 1, 0, -1)), (keep_ref, *send_refs)):
         first = pl.multiple_of((member ^ away) * width, width)
         for half in range(2):
             piece = sum_ref[pl.ds(half * HD + first, width), :]
@@ -259,13 +250,15 @@
     dv_ref[...] = total[width:].astype(BF16)
 
 
-SMEM = pl.BlockSpec(memory_space=pltpu.SMEM)
 VMEM = pl.BlockSpec(memory_space=pltpu.VMEM)
 ANY = pl.BlockSpec(memory_space=pl.ANY)
 
 
-def call(kernel, out_shape, operands, scratch=(), smem=0, unread=(), aliases={}, us=0):
-    kinds = [SMEM] * smem + [VMEM] * (len(operands) - smem)
+HBM = pl.BlockSpec(memory_space=pltpu.HBM)
+
+
+def call(kernel, out_shape, operands, scratch=(), unread=(), aliases={}, us=0, hbm=0, vmem=24):
+    kinds = [HBM] * hbm + [VMEM] * (len(operands) - hbm)
     results = [VMEM] * len(out_shape)
     for place_of in unread:
         kinds[place_of] = ANY
@@ -281,7 +274,7 @@
         scratch_shapes=list(scratch),
         input_output_aliases=aliases,
         cost_estimate=cost,
-        compiler_params=pltpu.CompilerParams(vmem_limit_bytes=24 << 20),
+        compiler_params=pltpu.CompilerParams(vmem_limit_bytes=vmem << 20),
     )(*operands)
 
 
@@ -302,7 +295,14 @@
         first = lax.axis_index("grp") // share * HD
         key_rows = lax.dynamic_slice_in_dim(key_rows, first, HD, 1)
         value_rows = lax.dynamic_slice_in_dim(value_rows, first, HD, 1)
-    (own_kv,) = call(pack_kernel, [sds((rows, 2 * HD), BF16)], [key_rows, value_rows])
+    (own_kv,) = call(
+        pack_kernel,
+        [sds((rows, 2 * HD), BF16)],
+        [key_rows, value_rows],
+        scratch=[pltpu.SemaphoreType.DMA((2,))],
+        hbm=2,
+        vmem=60,
+    )
     docs = doc_ids.reshape(srv, rows)
 
     def trade(block, away):
@@ -311,11 +311,10 @@
     def swap(block):
         return lax.ppermute(block, "srv", [(i, i ^ 1) for i in range(srv)])
 
-    far_kv = [trade(own_kv, away)[None] for away in range(chips - 1, 0, -1)][::-1]
-    groups = [1] * len(far_kv)
+    order = list(range(chips - 1, 0, -1))
+    far_kv = {away: trade(own_kv, away)[None] for away in order}
     if chips > 4:
-        groups = [len(far_kv)]
-        far_kv = [jnp.concatenate(far_kv, axis=0)]
+        far_kv = {1: jnp.concatenate([far_kv[away] for away in order[::-1]], axis=0)}
     (qd_own,) = call(
         turn_kernel,
         [sds((2 * HD, heads * rows), BF16)],
@@ -323,33 +322,31 @@
         unread=[2],
     )
     qd_par = swap(qd_own)
-    shared = [doc_ids, docs, qd_own, qd_par]
+    shared = [docs, qd_own, qd_par]
     (stats,) = call(
-        own_stats_kernel, [sds((8, lanes), F32)], [*shared, own_kv], smem=1
-    )
-    (stats,) = call(
-        functools.partial(far_stats_kernel, groups),
-        [sds((8, lanes), F32)],
-        [*shared, stats, *far_kv],
-        smem=1,
-    )
-    other_stats = swap(stats)
-    *far_dkv, dqt, norm = call(
-        functools.partial(far_grads_kernel, groups),
-        [sds((amount, 2 * HD, rows), BF16) for amount in groups]
-        + [sds((HD, lanes), F32), sds((8, lanes), F32)],
-        [*shared, stats, other_stats, *far_kv],
-        smem=1,
-    )
-    if chips > 4:
-        far_dkv = [far_dkv[0][i : i + 1] for i in range(chips - 1)]
-    came = [trade(part, away + 1) for away, part in enumerate(far_dkv)]
+        own_stats_kernel, [sds((8, lanes), F32)], [*shared, own_kv]
+    )
+    for first, kv in far_kv.items():
+        (stats,) = call(
+            functools.partial(far_stats_kernel, first),
+            [sds((8, lanes), F32)],
+            [*shared, stats, kv],
+            )
+    (norm,) = call(norm_kernel, [sds((8, lanes), F32)], [stats, swap(stats)])
+    came, dqt = [], []
+    for first, kv in far_kv.items():
+        part, dqt_part = call(
+            functools.partial(far_grads_kernel, first),
+            [sds(kv.shape[:1] + (2 * HD, rows), BF16), sds((HD, lanes), F32)],
+            [*shared, norm, kv],
+            )
+        dqt.append(dqt_part)
+        came += [trade(part[slot], first + slot) for slot in range(kv.shape[0])]
     own_dkv, dq_own, dq_par = call(
         own_grads_kernel,
         [sds((2 * HD, rows), F32)] + [sds((columns, rows), F32)] * 2,
-        [*shared, norm, own_kv, dqt],
+        [*shared, norm, own_kv, *dqt],
         scratch=[pltpu.VMEM((HD, lanes), F32)],
-        smem=1,
         us=4,
     )
     width = HD // share
@@ -362,8 +359,8 @@
         aliases={0: 0},
     )
     back = [
-        lax.ppermute(part, "grp", [(i, i ^ (away + 1)) for i in range(grp)])
-        for away, part in enumerate(send)
+        lax.ppermute(part, "grp", [(i, i ^ away) for i in range(grp)])
+        for away, part in zip(range(share - 1, 0, -1), send)
     ]
     grad_query, token = call(
         query_kernel,

time: 40.5 us -> 36.9 us (0.911); the launches traced: 40.3 us -> 37.2 us
  waiting for transfers between devices: 15.4 us -> 12.9 us
  Pallas kernels: 6.72 us -> 8.68 us
  local copies, waits for them, and re-layouts: 1.73 us -> 0.02 us
  starting transfers between devices: 15.7 us -> 14.8 us
    pallas_call x9 -> x14, Pallas kernels: 6.72 us -> 8.68 us  [call(): pl.pallas_call(kernel, out_shape=out_shape, in_specs=kinds, out_specs=res...]
    unnamed x10 -> x6, local copies, waits for them, and re-layouts: 1.73 us -> 0.01 us
    ppermute x3, waiting for transfers between devices: 4.93 us -> 3.25 us  [on_device(): lax.ppermute(part, 'grp', [(i, i ^ away) for i in range(grp)])]
    ppermute x6, starting transfers between devices: 10.5 us -> 9.66 us  [trade(): return lax.ppermute(block, 'srv', [(i, i ^ 2 * away) for i in range(srv)])]
    ppermute x6, waiting for transfers between devices: 9.31 us -> 8.5 us  [trade(): return lax.ppermute(block, 'srv', [(i, i ^ 2 * away) for i in range(srv)])]
  transfers between devices with their start and end apart: 12 -> 12, of which waited for: 7 -> 7; matrix products, arithmetic and copies ran while one was open for 0% -> 0% of each run, Pallas kernels for 11% -> 16%
where the time goes in v3:
time: 36.9 us; the launch traced here: 37.2 us
  starting transfers between devices  14.8 us (40%)
  waiting for transfers between devices  12.9 us (35%)
  Pallas kernels  8.68 us (24%)
  between operations  0.79 us (2%)
    ppermute x6, starting transfers between devices, trade(): return lax.ppermute(block, 'srv', [(i, i ^ 2 * away) for i in range(srv)])  9.66 us
    pallas_call x14, Pallas kernels, call(): pl.pallas_call(kernel, out_shape=out_shape, in_specs=kinds, out_specs=res...  8.68 us
    ppermute x6, waiting for transfers between devices, trade(): return lax.ppermute(block, 'srv', [(i, i ^ 2 * away) for i in range(srv)])  8.5 us
    ppermute x3, starting transfers between devices, on_device(): lax.ppermute(part, 'grp', [(i, i ^ away) for i in range(grp)])  4.45 us
    ppermute x3, waiting for transfers between devices, on_device(): lax.ppermute(part, 'grp', [(i, i ^ away) for i in range(grp)])  3.25 us
    ppermute x3, waiting for transfers between devices, swap(): return lax.ppermute(block, 'srv', [(i, i ^ 1) for i in range(srv)])  1.2 us
  transfers between devices with their start and end apart: 12, of which 7 were waited for; matrix products, arithmetic and copies ran while one was open for 0% of the time, Pallas kernels for 16%

profile of v3, /device:TPU:0, one launch (start us, length us, event | category | flops | bytes accessed | tf_op | source)
XLA Modules:
  0.0 37.2 jit_solution(15993176786156040478)
XLA Ops:
  0.7 1.6 %shard_map.76.after_ref.kv_ref = bf16[256,256]{1,0:T(8,128)(2,1)} custom-call(bf16[256,128]{1,0:T(8,128)(2,1)} %key_ref.1, bf16[256,128]{1,0:T(8,128)(2,1)} %value_ref.1), custom_call_target="tpu_custom_call" | custom-call | bytes 524288 | tf_op jit(solution)/shard_map/pallas_call | solution.py:269
  2.3 0.0 copy-start.2
  2.3 0.1 shard_map.77.qd_own
  2.4 0.5 %collective-permute-start = (bf16[256,512]{1,0:T(8,128)(2,1)S(1)}, bf16[256,512]{1,0:T(8,128)(2,1)S(1)}, u32[]{:S(2)}, u32[]{:S(2)}) collective-permute-start(bf16[256,512]{1,0:T(8,128)(2,1)S(1)} %shard_map.77.qd_own), channel_id=1, source_target_pairs={{0,1},{1,0},{2,3},{3,2},{4,5},{5,4},{6,7},{7,6},{8,9},{9,8},{10,11... | collective-permute-start | bytes 786440 | tf_op jit(solution)/shard_map/ppermute | solution.py:312
  2.9 3.5 %collective-permute-start.1 = (bf16[256,256]{1,0:T(8,128)(2,1)}, bf16[256,256]{1,0:T(8,128)(2,1)S(1)}, u32[]{:S(2)}, u32[]{:S(2)}) collective-permute-start(bf16[256,256]{1,0:T(8,128)(2,1)} %shard_map.76.after_ref.kv_ref), channel_id=1, source_target_pairs={{0,6},{1,7},{2,4},{3,5},{4,2},{5,3},{6,0},{7,1},{8,14},{9,15},{10,... | collective-permute-start | bytes 393224 | tf_op jit(solution)/shard_map/ppermute | solution.py:309
  6.4 0.5 %collective-permute-start.2 = (bf16[256,256]{1,0:T(8,128)(2,1)}, bf16[256,256]{1,0:T(8,128)(2,1)S(1)}, u32[]{:S(2)}, u32[]{:S(2)}) collective-permute-start(bf16[256,256]{1,0:T(8,128)(2,1)} %shard_map.76.after_ref.kv_ref), channel_id=1, source_target_pairs={{0,4},{1,5},{2,6},{3,7},{4,0},{5,1},{6,2},{7,3},{8,12},{9,13},{10,... | collective-permute-start | bytes 393224 | tf_op jit(solution)/shard_map/ppermute | solution.py:309
  6.9 0.1 collective-permute-start.3
  7.1 1.7 %shard_map.78.stats_in = f32[8,1024]{1,0:T(8,128)S(1)} custom-call(s32[8,256]{1,0:T(8,128)S(1)} %reshape.9.docs_ref, bf16[256,512]{1,0:T(8,128)(2,1)S(1)} %shard_map.77.qd_own, bf16[256,512]{1,0:T(8,128)(2,1)S(1)} %collective-permute-done.qd_par, bf16[256,256]{1,0:T(8,128)(2,1)} %shard_map.76.after_ref.kv_ref), custom_call_target="tpu_custom_call" | custom-call | bytes 524288 | tf_op jit(solution)/shard_map/pallas_call | solution.py:269
  8.8 2.0 %collective-permute-done.1 = bf16[256,256]{1,0:T(8,128)(2,1)S(1)} collective-permute-done((bf16[256,256]{1,0:T(8,128)(2,1)}, bf16[256,256]{1,0:T(8,128)(2,1)S(1)}, u32[]{:S(2)}, u32[]{:S(2)}) %collective-permute-start.1) | collective-permute-done | bytes 131104 | tf_op jit(solution)/shard_map/ppermute | solution.py:309
  10.8 0.2 shard_map.79.stats_in
  11.1 2.5 %collective-permute-done.2 = bf16[256,256]{1,0:T(8,128)(2,1)S(1)} collective-permute-done((bf16[256,256]{1,0:T(8,128)(2,1)}, bf16[256,256]{1,0:T(8,128)(2,1)S(1)}, u32[]{:S(2)}, u32[]{:S(2)}) %collective-permute-start.2) | collective-permute-done | bytes 131104 | tf_op jit(solution)/shard_map/ppermute | solution.py:309
  13.5 0.2 shard_map.80.stats_in
  13.8 0.1 collective-permute-done.3
  13.9 0.2 shard_map.81.stats_ref
  14.1 0.1 collective-permute-start.4
  14.2 1.2 %collective-permute-done.4.other_ref = f32[8,1024]{1,0:T(8,128)S(1)} collective-permute-done((f32[8,1024]{1,0:T(8,128)S(1)}, f32[8,1024]{1,0:T(8,128)S(1)}, u32[]{:S(2)}, u32[]{:S(2)}) %collective-permute-start.4) | collective-permute-done | bytes 32800 | tf_op jit(solution)/shard_map/ppermute | solution.py:312
  15.4 0.2 shard_map.85
  15.6 3.9 %collective-permute-start.7 = (bf16[256,256]{1,0:T(8,128)(2,1)S(1)}, bf16[256,256]{1,0:T(8,128)(2,1)S(1)}, u32[]{:S(2)}, u32[]{:S(2)}) collective-permute-start(bf16[256,256]{1,0:T(8,128)(2,1)S(1)} %bitcast.14), channel_id=1, source_target_pairs={{0,2},{1,3},{2,0},{3,1},{4,6},{5,7},{6,4},{7,5},{8,10},{9,11},{10,... | collective-permute-start | bytes 393224 | tf_op jit(solution)/shard_map/ppermute | solution.py:309
  19.5 0.2 shard_map.84
  19.8 0.1 collective-permute-start.6
  19.9 0.2 shard_map.83
  20.1 1.5 %collective-permute-start.5 = (bf16[256,256]{1,0:T(8,128)(2,1)S(1)}, bf16[256,256]{1,0:T(8,128)(2,1)S(1)}, u32[]{:S(2)}, u32[]{:S(2)}) collective-permute-start(bf16[256,256]{1,0:T(8,128)(2,1)S(1)} %bitcast.16), channel_id=1, source_target_pairs={{0,6},{1,7},{2,4},{3,5},{4,2},{5,3},{6,0},{7,1},{8,14},{9,15},{10,... | collective-permute-start | bytes 393224 | tf_op jit(solution)/shard_map/ppermute | solution.py:309
  21.6 2.4 %shard_map.86 = (f32[256,256]{1,0:T(8,128)S(1)}, f32[256,256]{1,0:T(8,128)S(1)}, f32[256,256]{1,0:T(8,128)S(1)}) custom-call(s32[8,256]{1,0:T(8,128)S(1)} %reshape.9.docs_ref, bf16[256,512]{1,0:T(8,128)(2,1)S(1)} %shard_map.77.qd_own, bf16[256,512]{1,0:T(8,128)(2,1)S(1)} %collective-permute-done.qd_par, f32[8,1024]{1,0:T(8,128)S(1)} %shard_map.82.norm_ref, ...), custom_call_target="tpu_custom_call" | custom-call | flops 4000000000 | bytes 524288 | tf_op jit(solution)/shard_map/pallas_call | solution.py:269
  24.0 3.9 %collective-permute-done.6.rest_1_ = bf16[256,256]{1,0:T(8,128)(2,1)S(1)} collective-permute-done((bf16[256,256]{1,0:T(8,128)(2,1)S(1)}, bf16[256,256]{1,0:T(8,128)(2,1)S(1)}, u32[]{:S(2)}, u32[]{:S(2)}) %collective-permute-start.6) | collective-permute-done | bytes 131104 | tf_op jit(solution)/shard_map/ppermute | solution.py:309
  27.9 0.1 shard_map.87
  28.0 0.1 collective-permute-start.8
  28.1 3.7 %collective-permute-start.9 = (bf16[64,256]{1,0:T(8,128)(2,1)S(1)}, bf16[64,256]{1,0:T(8,128)(2,1)S(1)}, u32[]{:S(2)}, u32[]{:S(2)}) collective-permute-start(bf16[64,256]{1,0:T(8,128)(2,1)S(1)} %get-tuple-element.34), channel_id=1, source_target_pairs={{0,24},{8,16},{16,8},{24,0},{1,25},{9,17},{17,9},{25,1},{2,26},{10... | collective-permute-start | bytes 98312 | tf_op jit(solution)/shard_map/ppermute | solution.py:362
  31.8 0.8 %collective-permute-start.11 = (bf16[64,256]{1,0:T(8,128)(2,1)S(1)}, bf16[64,256]{1,0:T(8,128)(2,1)S(1)}, u32[]{:S(2)}, u32[]{:S(2)}) collective-permute-start(bf16[64,256]{1,0:T(8,128)(2,1)S(1)} %get-tuple-element.36), channel_id=1, source_target_pairs={{0,8},{8,0},{16,24},{24,16},{1,9},{9,1},{17,25},{25,17},{2,10},{10... | collective-permute-start | bytes 98312 | tf_op jit(solution)/shard_map/ppermute | solution.py:362
  32.6 0.8 %shard_map.88 = (bf16[256,256]{1,0:T(8,128)(2,1)}, f32[8,128]{1,0:T(8,128)S(1)}) custom-call(f32[256,256]{1,0:T(8,128)S(1)} %get-tuple-element.24.dq_own, f32[256,256]{1,0:T(8,128)S(1)} %collective-permute-done.8.dq_far), custom_call_target="tpu_custom_call" | custom-call | flops 2000000000 | bytes 524288 | tf_op jit(solution)/shard_map/pallas_call | solution.py:269
  33.3 0.6 %collective-permute-done.9.rest_0_ = bf16[64,256]{1,0:T(8,128)(2,1)S(1)} collective-permute-done((bf16[64,256]{1,0:T(8,128)(2,1)S(1)}, bf16[64,256]{1,0:T(8,128)(2,1)S(1)}, u32[]{:S(2)}, u32[]{:S(2)}) %collective-permute-start.9) | collective-permute-done | bytes 32800 | tf_op jit(solution)/shard_map/ppermute | solution.py:362
  33.9 2.7 %collective-permute-done.10.rest_1_ = bf16[64,256]{1,0:T(8,128)(2,1)S(1)} collective-permute-done((bf16[64,256]{1,0:T(8,128)(2,1)S(1)}, bf16[64,256]{1,0:T(8,128)(2,1)S(1)}, u32[]{:S(2)}, u32[]{:S(2)}) %collective-permute-start.10) | collective-permute-done | bytes 32800 | tf_op jit(solution)/shard_map/ppermute | solution.py:362
  36.6 0.6 %shard_map.89 = (bf16[32,256]{1,0:T(8,128)(2,1)}, bf16[32,256]{1,0:T(8,128)(2,1)}) custom-call(f32[8,128]{1,0:T(8,128)S(1)} %get-tuple-element.32.after_ref, f32[64,256]{1,0:T(8,128)S(1)} %get-tuple-element.33.keep_ref, bf16[64,256]{1,0:T(8,128)(2,1)S(1)} %collective-permute-done.9.rest_0_, bf16[64,256]{1,0:T(8,128)(2,1)S(1)} %collective-permute-done.10.rest_1_, ...), custom_call_target="tpu_custom_call" | custom-call | bytes 524288 | tf_op jit(solution)/shard_map/pallas_call | solution.py:269
  (13 shorter events, 0.1 us)
Async XLA Ops:
  0.6 1.6 %copy-start.1 = (bf16[256,256]{1,0:T(8,128)(2,1)S(1)}, bf16[256,256]{1,0:T(8,128)(2,1)}, u32[]{:S(2)}) copy-start(bf16[256,256]{1,0:T(8,128)(2,1)} %do_ref.1) | copy-start | bytes 393220
  0.6 1.6 %copy-start = (bf16[256,256]{1,0:T(8,128)(2,1)S(1)}, bf16[256,256]{1,0:T(8,128)(2,1)}, u32[]{:S(2)}) copy-start(bf16[256,256]{1,0:T(8,128)(2,1)} %q_ref.1) | copy-start | bytes 393220
  2.3 4.8 %copy-start.2 = (s32[2048]{0:T(1024)S(1)}, s32[2048]{0:T(1024)}, u32[]{:S(2)}) copy-start(s32[2048]{0:T(1024)} %param.9) | copy-start | bytes 24580
  2.4 4.7 %collective-permute-start = (bf16[256,512]{1,0:T(8,128)(2,1)S(1)}, bf16[256,512]{1,0:T(8,128)(2,1)S(1)}, u32[]{:S(2)}, u32[]{:S(2)}) collective-permute-start(bf16[256,512]{1,0:T(8,128)(2,1)S(1)} %shard_map.77.qd_own), channel_id=1, source_target_pairs={{0,1},{1,0},{2,3},{3,2},{4,5},{5,4},{6,7},{7,6},{8,9},{9,8},{10,11... | collective-permute-start | bytes 786440 | tf_op jit(solution)/shard_map/ppermute | solution.py:312
  2.9 7.9 %collective-permute-start.1 = (bf16[256,256]{1,0:T(8,128)(2,1)}, bf16[256,256]{1,0:T(8,128)(2,1)S(1)}, u32[]{:S(2)}, u32[]{:S(2)}) collective-permute-start(bf16[256,256]{1,0:T(8,128)(2,1)} %shard_map.76.after_ref.kv_ref), channel_id=1, source_target_pairs={{0,6},{1,7},{2,4},{3,5},{4,2},{5,3},{6,0},{7,1},{8,14},{9,15},{10,... | collective-permute-start | bytes 393224 | tf_op jit(solution)/shard_map/ppermute | solution.py:309
  6.4 7.1 %collective-permute-start.2 = (bf16[256,256]{1,0:T(8,128)(2,1)}, bf16[256,256]{1,0:T(8,128)(2,1)S(1)}, u32[]{:S(2)}, u32[]{:S(2)}) collective-permute-start(bf16[256,256]{1,0:T(8,128)(2,1)} %shard_map.76.after_ref.kv_ref), channel_id=1, source_target_pairs={{0,4},{1,5},{2,6},{3,7},{4,0},{5,1},{6,2},{7,3},{8,12},{9,13},{10,... | collective-permute-start | bytes 393224 | tf_op jit(solution)/shard_map/ppermute | solution.py:309
  6.9 6.9 %collective-permute-start.3 = (bf16[256,256]{1,0:T(8,128)(2,1)}, bf16[256,256]{1,0:T(8,128)(2,1)S(1)}, u32[]{:S(2)}, u32[]{:S(2)}) collective-permute-start(bf16[256,256]{1,0:T(8,128)(2,1)} %shard_map.76.after_ref.kv_ref), channel_id=1, source_target_pairs={{0,2},{1,3},{2,0},{3,1},{4,6},{5,7},{6,4},{7,5},{8,10},{9,11},{10,... | collective-permute-start | bytes 393224 | tf_op jit(solution)/shard_map/ppermute | solution.py:309
  14.1 1.3 %collective-permute-start.4 = (f32[8,1024]{1,0:T(8,128)S(1)}, f32[8,1024]{1,0:T(8,128)S(1)}, u32[]{:S(2)}, u32[]{:S(2)}) collective-permute-start(f32[8,1024]{1,0:T(8,128)S(1)} %shard_map.81.stats_ref), channel_id=1, source_target_pairs={{0,1},{1,0},{2,3},{3,2},{4,5},{5,4},{6,7},{7,6},{8,9},{9,8},{10,11... | collective-permute-start | bytes 98312 | tf_op jit(solution)/shard_map/ppermute | solution.py:312
  15.6 8.4 %collective-permute-start.7 = (bf16[256,256]{1,0:T(8,128)(2,1)S(1)}, bf16[256,256]{1,0:T(8,128)(2,1)S(1)}, u32[]{:S(2)}, u32[]{:S(2)}) collective-permute-start(bf16[256,256]{1,0:T(8,128)(2,1)S(1)} %bitcast.14), channel_id=1, source_target_pairs={{0,2},{1,3},{2,0},{3,1},{4,6},{5,7},{6,4},{7,5},{8,10},{9,11},{10,... | collective-permute-start | bytes 393224 | tf_op jit(solution)/shard_map/ppermute | solution.py:309
  19.8 8.2 %collective-permute-start.6 = (bf16[256,256]{1,0:T(8,128)(2,1)S(1)}, bf16[256,256]{1,0:T(8,128)(2,1)S(1)}, u32[]{:S(2)}, u32[]{:S(2)}) collective-permute-start(bf16[256,256]{1,0:T(8,128)(2,1)S(1)} %bitcast.15), channel_id=1, source_target_pairs={{0,4},{1,5},{2,6},{3,7},{4,0},{5,1},{6,2},{7,3},{8,12},{9,13},{10,... | collective-permute-start | bytes 393224 | tf_op jit(solution)/shard_map/ppermute | solution.py:309
  20.1 7.8 %collective-permute-start.5 = (bf16[256,256]{1,0:T(8,128)(2,1)S(1)}, bf16[256,256]{1,0:T(8,128)(2,1)S(1)}, u32[]{:S(2)}, u32[]{:S(2)}) collective-permute-start(bf16[256,256]{1,0:T(8,128)(2,1)S(1)} %bitcast.16), channel_id=1, source_target_pairs={{0,6},{1,7},{2,4},{3,5},{4,2},{5,3},{6,0},{7,1},{8,14},{9,15},{10,... | collective-permute-start | bytes 393224 | tf_op jit(solution)/shard_map/ppermute | solution.py:309
  28.0 4.5 %collective-permute-start.8 = (f32[256,256]{1,0:T(8,128)S(1)}, f32[256,256]{1,0:T(8,128)S(1)}, u32[]{:S(2)}, u32[]{:S(2)}) collective-permute-start(f32[256,256]{1,0:T(8,128)S(1)} %get-tuple-element.30), channel_id=1, source_target_pairs={{0,1},{1,0},{2,3},{3,2},{4,5},{5,4},{6,7},{7,6},{8,9},{9,8},{10,11... | collective-permute-start | bytes 786440 | tf_op jit(solution)/shard_map/ppermute | solution.py:312
  28.1 5.8 %collective-permute-start.9 = (bf16[64,256]{1,0:T(8,128)(2,1)S(1)}, bf16[64,256]{1,0:T(8,128)(2,1)S(1)}, u32[]{:S(2)}, u32[]{:S(2)}) collective-permute-start(bf16[64,256]{1,0:T(8,128)(2,1)S(1)} %get-tuple-element.34), channel_id=1, source_target_pairs={{0,24},{8,16},{16,8},{24,0},{1,25},{9,17},{17,9},{25,1},{2,26},{10... | collective-permute-start | bytes 98312 | tf_op jit(solution)/shard_map/ppermute | solution.py:362
  31.8 4.8 %collective-permute-start.10 = (bf16[64,256]{1,0:T(8,128)(2,1)S(1)}, bf16[64,256]{1,0:T(8,128)(2,1)S(1)}, u32[]{:S(2)}, u32[]{:S(2)}) collective-permute-start(bf16[64,256]{1,0:T(8,128)(2,1)S(1)} %get-tuple-element.35), channel_id=1, source_target_pairs={{0,16},{8,24},{16,0},{24,8},{1,17},{9,25},{17,1},{25,9},{2,18},{10... | collective-permute-start | bytes 98312 | tf_op jit(solution)/shard_map/ppermute | solution.py:362
  31.8 4.8 %collective-permute-start.11 = (bf16[64,256]{1,0:T(8,128)(2,1)S(1)}, bf16[64,256]{1,0:T(8,128)(2,1)S(1)}, u32[]{:S(2)}, u32[]{:S(2)}) collective-permute-start(bf16[64,256]{1,0:T(8,128)(2,1)S(1)} %get-tuple-element.36), channel_id=1, source_target_pairs={{0,8},{8,0},{16,24},{24,16},{1,9},{9,1},{17,25},{25,17},{2,10},{10... | collective-permute-start | bytes 98312 | tf_op jit(solution)/shard_map/ppermute | solution.py:362

commit v4 on v3

v4 whole, which is shorter than its diff:
```python
import functools

import jax
import jax.numpy as jnp
from jax import lax
from jax.experimental import pallas as pl
from jax.experimental.pallas import tpu as pltpu
from jax.sharding import PartitionSpec as P

HD = 128
SCALE = HD**-0.5
LOG2E = 1.4426950408889634
MASKED = -1.0e30
LOWEST = -1.0e20
F32 = jnp.float32
BF16 = jnp.bfloat16


def nn(a, b):
    return lax.dot_general(a, b, (((1,), (0,)), ((), ())), preferred_element_type=F32)


def nt(a, b):
    return lax.dot_general(a, b, (((1,), (1,)), ((), ())), preferred_element_type=F32)


def tn(a, b):
    return lax.dot_general(a, b, (((0,), (0,)), ((), ())), preferred_element_type=F32)


def place():
    srv = lax.axis_index("srv")
    return srv // 2, srv % 2


def hot_kernel(docs_ref, khot_ref, rhot_ref):
    rows = docs_ref.shape[1]
    chip, core = place()
    kind = lax.broadcasted_iota(jnp.int32, (HD, rows), 0)
    for source in range(khot_ref.shape[0]):
        hot = kind == docs_ref[pl.ds(source * 2 + core, 1), :]
        khot_ref[source] = jnp.transpose(hot.astype(F32)).astype(BF16)
    for side in range(2):
        row_block = chip * 2 + (core if side == 0 else 1 - core)
        hot = kind == docs_ref[pl.ds(row_block, 1), :]
        rhot_ref[:, side * rows : (side + 1) * rows] = jnp.where(hot, 0.0, MASKED).astype(BF16)


def chunks_of(sides, qds, rhot_ref):
    rows = rhot_ref.shape[1] // 2
    heads = qds[0].shape[1] // rows
    for side in sides:
        for head in range(heads):
            local = slice(head * rows, (head + 1) * rows)
            chunk = side * heads + head
            lanes = slice(chunk * rows, (chunk + 1) * rows)
            penalty = rhot_ref[:, side * rows : (side + 1) * rows]
            yield lanes, qds[side][:HD, local], qds[side][HD:, local], penalty


def scores_of(kv, khot, qt, penalty, causal):
    keys = jnp.concatenate([kv[:, :HD], khot], axis=1)
    scores = nn(keys, jnp.concatenate([qt, penalty], axis=0))
    if causal:
        key_pos = lax.broadcasted_iota(jnp.int32, scores.shape, 0)
        row_pos = lax.broadcasted_iota(jnp.int32, scores.shape, 1)
        scores = jnp.where(key_pos <= row_pos, scores, MASKED)
    return scores


def add_stats(stats_ref, kv, khot, qds, rhot_ref, sides, causal):
    for lanes, qt, dot, penalty in chunks_of(sides, qds, rhot_ref):
        scores = scores_of(kv, khot, qt, penalty, causal)
        grad_probs = nn(kv[:, HD:], dot)
        old = stats_ref[0:1, lanes]
        new = jnp.maximum(old, jnp.max(scores, axis=0, keepdims=True) * (SCALE * LOG2E))
        factor = jnp.exp2(old - new)
        weights = jnp.exp2(scores * (SCALE * LOG2E) - new)
        stats_ref[0:1, lanes] = new
        stats_ref[1:2, lanes] = stats_ref[1:2, lanes] * factor + jnp.sum(
            weights, axis=0, keepdims=True
        )
        stats_ref[2:3, lanes] = stats_ref[2:3, lanes] * factor + jnp.sum(
            weights * grad_probs, axis=0, keepdims=True
        )


def add_grads(kv, khot, qds, rhot_ref, sides, causal, norm_ref, dqt_ref, fresh):
    qts, dots, lows, grads = [], [], [], []
    for lanes, qt, dot, penalty in chunks_of(sides, qds, rhot_ref):
        scores = scores_of(kv, khot, qt, penalty, causal)
        weights = jnp.exp2(scores * (SCALE * LOG2E) - norm_ref[0:1, lanes])
        grad_probs = nn(kv[:, HD:], dot)
        grad_scores = (weights * (grad_probs - norm_ref[1:2, lanes])).astype(BF16)
        change = tn(kv[:, :HD], grad_scores)
        if fresh:
            dqt_ref[:, lanes] = change
        else:
            dqt_ref[:, lanes] += change
        qts.append(qt)
        dots.append(dot)
        lows.append(weights.astype(BF16))
        grads.append(grad_scores)

    def joined(parts):
        return jnp.concatenate(parts, axis=1)

    dkt = nt(joined(qts), joined(grads)) * SCALE
    dvt = nt(joined(dots), joined(lows))
    return jnp.concatenate([dkt, dvt], axis=0)


def reaches(docs_ref, key_block, row_block):
    last = docs_ref[pl.ds(key_block, 1), :][0, docs_ref.shape[1] - 1]
    return last >= docs_ref[pl.ds(row_block, 1), :][0, 0]


def blank_kernel(stats_ref):
    stats_ref[...] = jnp.zeros(stats_ref.shape, F32)
    stats_ref[0:1, :] = jnp.full((1, stats_ref.shape[1]), LOWEST, F32)


def pack_kernel(after_ref, key_ref, value_ref, kv_ref):
    kv_ref[:, :HD] = key_ref[...]
    kv_ref[:, HD:] = value_ref[...]


def turn_kernel(q_own, do_own, q_par, do_par, qd_own, qd_par):
    rows, columns = q_own.shape
    for q_ref, do_ref, qd_ref in ((q_own, do_own, qd_own), (q_par, do_par, qd_par)):
        for top, ref in ((0, q_ref), (HD, do_ref)):
            turned = jnp.transpose(ref[...])
            for head in range(columns // HD):
                qd_ref[top : top + HD, head * rows : (head + 1) * rows] = turned[
                    head * HD : (head + 1) * HD, :
                ]


def own_stats_kernel(khot_ref, rhot_ref, qd_own, qd_par, kv_ref, stats_in, stats_ref):
    chip, core = place()
    stats_ref[...] = stats_in[...]
    kv, khot, qds = kv_ref[...], khot_ref[chip], (qd_own, qd_par)
    add_stats(stats_ref, kv, khot, qds, rhot_ref, (0,), True)

    @pl.when(core == 0)
    def _():
        add_stats(stats_ref, kv, khot, qds, rhot_ref, (1,), False)


def each_remote(first, kv_ref, docs_ref, body, rest):
    chip, core = place()
    count = kv_ref.shape[0]

    def step(slot):
        source = chip ^ (first + slot)

        @pl.when(source < chip)
        def _():
            active = reaches(docs_ref, source * 2 + core, chip * 2)
            pl.when(active)(functools.partial(body, slot, source))
            if rest is not None:
                pl.when(jnp.logical_not(active))(rest)

        if rest is not None:
            pl.when(source > chip)(rest)

    if count == 1:
        step(0)
    else:
        pl.loop(0, count)(step)


def far_stats_kernel(firsts, docs_ref, khot_ref, rhot_ref, qd_own, qd_par, stats_in, *rest):
    kv_refs, stats_ref = rest[:-1], rest[-1]
    stats_ref[...] = stats_in[...]
    qds = qd_own, qd_par
    for first, kv_ref in zip(firsts, kv_refs):

        def body(slot, source, kv_ref=kv_ref):
            add_stats(stats_ref, kv_ref[slot], khot_ref[source], qds, rhot_ref, (0, 1), False)

        each_remote(first, kv_ref, docs_ref, body, None)


def norm_kernel(stats_ref, other_ref, norm_ref):
    half = stats_ref.shape[1] // 2
    mine = stats_ref[...]
    other = other_ref[...]
    other = jnp.concatenate([other[:, half:], other[:, :half]], axis=1)
    top = jnp.maximum(mine[0:1], other[0:1])
    mine_by = jnp.exp2(mine[0:1] - top)
    other_by = jnp.exp2(other[0:1] - top)
    total = mine[1:2] * mine_by + other[1:2] * other_by
    norm_ref[...] = jnp.zeros(norm_ref.shape, F32)
    norm_ref[0:1, :] = top + jnp.log2(total)
    norm_ref[1:2, :] = (mine[2:3] * mine_by + other[2:3] * other_by) / total


def far_grads_kernel(
    first, docs_ref, khot_ref, rhot_ref, qd_own, qd_par, norm_ref, kv_ref, out_ref, dqt_ref
):
    alone = kv_ref.shape[0] == 1
    qds = qd_own, qd_par

    def clear():
        dqt_ref[...] = jnp.zeros(dqt_ref.shape, F32)
        out_ref[...] = jnp.zeros(out_ref.shape, BF16)

    if not alone:
        clear()

    def body(slot, source):
        part = add_grads(
            kv_ref[slot], khot_ref[source], qds, rhot_ref, (0, 1), False, norm_ref, dqt_ref, alone
        )
        out_ref[slot] = part.astype(BF16)

    each_remote(first, kv_ref, docs_ref, body, clear if alone else None)


def own_grads_kernel(after_ref, khot_ref, rhot_ref, qd_own, qd_par, norm_ref, kv_ref, *rest):
    dqt_in, (dkv_ref, dq_own, dq_par, dqt_ref) = rest[:-4], rest[-4:]
    rows = kv_ref.shape[0]
    heads = qd_own.shape[1] // rows
    chip, core = place()
    dqt_ref[...] = sum(part[...] for part in dqt_in)
    kv, khot, qds = kv_ref[...], khot_ref[chip], (qd_own, qd_par)
    dkv_ref[...] = add_grads(kv, khot, qds, rhot_ref, (0,), True, norm_ref, dqt_ref, False)

    @pl.when(core == 0)
    def _():
        dkv_ref[...] += add_grads(kv, khot, qds, rhot_ref, (1,), False, norm_ref, dqt_ref, False)

    for side, out_ref in enumerate((dq_own, dq_par)):
        for head in range(heads):
            chunk = side * heads + head
            out_ref[head * HD : (head + 1) * HD, :] = (
                dqt_ref[:, chunk * rows : (chunk + 1) * rows] * SCALE
            )


def query_kernel(dq_own, dq_far, dq_ref, token_ref):
    token_ref[...] = jnp.zeros(token_ref.shape, F32)
    dq_ref[...] = jnp.transpose(dq_own[...] + dq_far[...]).astype(BF16)


def combine_kernel(share, count, dq_in, own_ref, *rest):
    parts, outs = rest[:count], rest[count:]
    keep_ref, send_refs, sum_ref = outs[1], outs[2:-1], outs[-1]
    width = HD // share
    total = own_ref[...]
    for part in parts:
        total = total + part[...].astype(F32)
    sum_ref[...] = total
    member = lax.axis_index("grp") % share
    for away, out_ref in zip((0, *range(share - 1, 0, -1)), (keep_ref, *send_refs)):
        first = pl.multiple_of((member ^ away) * width, width)
        for half in range(2):
            piece = sum_ref[pl.ds(half * HD + first, width), :]
            out_ref[half * width : (half + 1) * width, :] = piece.astype(out_ref.dtype)


def finish_kernel(after_ref, keep_ref, *rest):
    parts, (dk_ref, dv_ref) = rest[:-2], rest[-2:]
    total = keep_ref[...]
    for part in parts:
        total = total + part[...].astype(F32)
    width = total.shape[0] // 2
    dk_ref[...] = total[:width].astype(BF16)
    dv_ref[...] = total[width:].astype(BF16)


VMEM = pl.BlockSpec(memory_space=pltpu.VMEM)
ANY = pl.BlockSpec(memory_space=pl.ANY)


HBM = pl.BlockSpec(memory_space=pltpu.HBM)


def call(kernel, out_shape, operands, scratch=(), unread=(), aliases={}, us=0, hbm=0, vmem=24):
    kinds = [HBM] * hbm + [VMEM] * (len(operands) - hbm)
    results = [VMEM] * len(out_shape)
    for place_of in unread:
        kinds[place_of] = ANY
    for source, target in aliases.items():
        kinds[source] = ANY
        results[target] = ANY
    cost = pl.CostEstimate(flops=us * 10**9, bytes_accessed=1 << 19, transcendentals=0)
    return pl.pallas_call(
        kernel,
        out_shape=out_shape,
        in_specs=kinds,
        out_specs=results,
        scratch_shapes=list(scratch),
        input_output_aliases=aliases,
        cost_estimate=cost,
        compiler_params=pltpu.CompilerParams(vmem_limit_bytes=vmem << 20),
    )(*operands)


def sds(shape, dtype):
    return jax.ShapeDtypeStruct(shape, dtype)


def on_device(queries, key_rows, value_rows, grad_output, doc_ids):
    rows, columns = queries.shape
    heads = columns // HD
    srv = lax.axis_size("srv")
    chips = srv // 2
    grp = lax.axis_size("grp")
    kv_heads = key_rows.shape[1] // HD
    share = grp // kv_heads
    lanes = 2 * heads * rows
    if kv_heads > 1:
        first = lax.axis_index("grp") // share * HD
        key_rows = lax.dynamic_slice_in_dim(key_rows, first, HD, 1)
        value_rows = lax.dynamic_slice_in_dim(value_rows, first, HD, 1)
    (blank,) = call(blank_kernel, [sds((8, lanes), F32)], [], us=5)
    (own_kv,) = call(
        pack_kernel,
        [sds((rows, 2 * HD), BF16)],
        [blank, key_rows, value_rows],
        unread=[0],
    )
    docs = doc_ids.reshape(srv, rows)

    def trade(block, away):
        return lax.ppermute(block, "srv", [(i, i ^ 2 * away) for i in range(srv)])

    def swap(block):
        return lax.ppermute(block, "srv", [(i, i ^ 1) for i in range(srv)])

    order = list(range(chips - 1, 0, -1))
    far_kv = {away: trade(own_kv, away)[None] for away in order}
    if chips > 4:
        far_kv = {1: jnp.concatenate([far_kv[away] for away in order[::-1]], axis=0)}
    qd_own, qd_par = call(
        turn_kernel,
        [sds((2 * HD, heads * rows), BF16)] * 2,
        [queries, grad_output, swap(queries), swap(grad_output)],
    )
    khot, rhot = call(
        hot_kernel,
        [sds((chips, rows, HD), BF16), sds((HD, 2 * rows), BF16)],
        [docs],
    )
    shared = [docs, khot, rhot, qd_own, qd_par]
    (stats,) = call(
        own_stats_kernel, [sds((8, lanes), F32)], [*shared[1:], own_kv, blank]
    )
    for firsts in (list(far_kv)[:1], list(far_kv)[1:]):
        if firsts:
            (stats,) = call(
                functools.partial(far_stats_kernel, firsts),
                [sds((8, lanes), F32)],
                [*shared, stats, *[far_kv[first] for first in firsts]],
            )
    (norm,) = call(norm_kernel, [sds((8, lanes), F32)], [stats, swap(stats)])
    came, dqt = [], []
    for first, kv in reversed(far_kv.items()):
        part, dqt_part = call(
            functools.partial(far_grads_kernel, first),
            [sds(kv.shape[:1] + (2 * HD, rows), BF16), sds((HD, lanes), F32)],
            [*shared, norm, kv],
            )
        dqt.append(dqt_part)
        came += [trade(part[slot], first + slot) for slot in range(kv.shape[0])]
    own_dkv, dq_own, dq_par = call(
        own_grads_kernel,
        [sds((2 * HD, rows), F32)] + [sds((columns, rows), F32)] * 2,
        [came[-1], *shared[1:], norm, own_kv, *dqt],
        scratch=[pltpu.VMEM((HD, lanes), F32)],
        unread=[0],
        us=4,
    )
    width = HD // share
    dq_par, keep, *send = call(
        functools.partial(combine_kernel, share, len(came)),
        [sds(dq_par.shape, F32), sds((2 * width, rows), F32)]
        + [sds((2 * width, rows), BF16)] * (share - 1),
        [dq_par, own_dkv, *came],
        scratch=[pltpu.VMEM((2 * HD, rows), F32)],
        aliases={0: 0},
    )
    back = [
        lax.ppermute(part, "grp", [(i, i ^ away) for i in range(grp)])
        for away, part in zip(range(share - 1, 0, -1), send)
    ]
    grad_query, token = call(
        query_kernel,
        [sds((rows, columns), BF16), sds((8, 128), F32)],
        [dq_own, swap(dq_par)],
        us=2,
    )
    grad_key, grad_value = call(
        finish_kernel,
        [sds((width, rows), BF16)] * 2,
        [token, keep, *back],
        unread=[0],
    )
    return grad_query, grad_key.T, grad_value.T


def solution(mesh):
    in_specs = (P("srv", "grp"), P("srv", None), P("srv", None), P("srv", "grp"), P())
    out_specs = (P("srv", "grp"), P("srv", "grp"), P("srv", "grp"))
    return jax.shard_map(
        on_device, mesh=mesh, in_specs=in_specs, out_specs=out_specs, check_vma=False
    )
```

time: 36.9 us -> 33.5 us (0.908); the launches traced: 37.2 us -> 33 us
  Pallas kernels: 8.68 us -> 4.44 us
  waiting for transfers between devices: 12.9 us -> 12.1 us
  starting transfers between devices: 14.8 us -> 15.4 us
    pallas_call x14 -> x15, Pallas kernels: 8.68 us -> 4.44 us  [call(): pl.pallas_call(kernel, out_shape=out_shape, in_specs=kinds, out_specs=res...]
    ppermute x6, waiting for transfers between devices: 8.5 us -> 7.64 us  [trade(): return lax.ppermute(block, 'srv', [(i, i ^ 2 * away) for i in range(srv)])]
    ppermute x6, starting transfers between devices: 9.66 us -> 10.2 us  [trade(): return lax.ppermute(block, 'srv', [(i, i ^ 2 * away) for i in range(srv)])]
    ppermute x3 -> x4, starting transfers between devices: 0.66 us -> 0.78 us  [swap(): return lax.ppermute(block, 'srv', [(i, i ^ 1) for i in range(srv)])]
    ppermute x3 -> x4, waiting for transfers between devices: 1.2 us -> 1.21 us  [swap(): return lax.ppermute(block, 'srv', [(i, i ^ 1) for i in range(srv)])]
  transfers between devices with their start and end apart: 12 -> 13, of which waited for: 7 -> 7; matrix products, arithmetic and copies ran while one was open for 0% -> 0% of each run, Pallas kernels for 16% -> 11%
where the time goes in v4:
time: 33.5 us; the launch traced here: 33 us
  starting transfers between devices  15.4 us (46%)
  waiting for transfers between devices  12.1 us (36%)
  Pallas kernels  4.44 us (13%)
  between operations  0.76 us (2%)
    ppermute x6, starting transfers between devices, trade(): return lax.ppermute(block, 'srv', [(i, i ^ 2 * away) for i in range(srv)])  10.2 us
    ppermute x6, waiting for transfers between devices, trade(): return lax.ppermute(block, 'srv', [(i, i ^ 2 * away) for i in range(srv)])  7.64 us
    pallas_call x15, Pallas kernels, call(): pl.pallas_call(kernel, out_shape=out_shape, in_specs=kinds, out_specs=res...  4.44 us
    ppermute x3, starting transfers between devices, on_device(): lax.ppermute(part, 'grp', [(i, i ^ away) for i in range(grp)])  4.39 us
    ppermute x3, waiting for transfers between devices, on_device(): lax.ppermute(part, 'grp', [(i, i ^ away) for i in range(grp)])  3.26 us
    ppermute x4, waiting for transfers between devices, swap(): return lax.ppermute(block, 'srv', [(i, i ^ 1) for i in range(srv)])  1.21 us
    ppermute x4, starting transfers between devices, swap(): return lax.ppermute(block, 'srv', [(i, i ^ 1) for i in range(srv)])  0.78 us
  transfers between devices with their start and end apart: 13, of which 7 were waited for; matrix products, arithmetic and copies ran while one was open for 0% of the time, Pallas kernels for 11%

profile of v4, /device:TPU:0, one launch (start us, length us, event | category | flops | bytes accessed | tf_op | source)
XLA Modules:
  0.0 33.0 jit_solution(6064607804465277783)
XLA Ops:
  0.7 0.5 %collective-permute-start = (bf16[256,256]{1,0:T(8,128)(2,1)}, bf16[256,256]{1,0:T(8,128)(2,1)S(1)}, u32[]{:S(2)}, u32[]{:S(2)}) collective-permute-start(bf16[256,256]{1,0:T(8,128)(2,1)} %q_own.1), channel_id=1, source_target_pairs={{0,1},{1,0},{2,3},{3,2},{4,5},{5,4},{6,7},{7,6},{8,9},{9,8},{10,11... | collective-permute-start | bytes 393224 | tf_op jit(solution)/shard_map/ppermute | solution.py:331
  1.2 0.1 collective-permute-start.1
  1.3 0.2 copy-done.3
  1.5 0.0 copy-done.2
  1.5 4.0 %collective-permute-start.2 = (bf16[256,256]{1,0:T(8,128)(2,1)S(1)}, bf16[256,256]{1,0:T(8,128)(2,1)S(1)}, u32[]{:S(2)}, u32[]{:S(2)}) collective-permute-start(bf16[256,256]{1,0:T(8,128)(2,1)S(1)} %shard_map.79.kv_ref), channel_id=1, source_target_pairs={{0,6},{1,7},{2,4},{3,5},{4,2},{5,3},{6,0},{7,1},{8,14},{9,15},{10,... | collective-permute-start | bytes 393224 | tf_op jit(solution)/shard_map/ppermute | solution.py:328
  5.5 0.5 %collective-permute-start.4 = (bf16[256,256]{1,0:T(8,128)(2,1)S(1)}, bf16[256,256]{1,0:T(8,128)(2,1)S(1)}, u32[]{:S(2)}, u32[]{:S(2)}) collective-permute-start(bf16[256,256]{1,0:T(8,128)(2,1)S(1)} %shard_map.79.kv_ref), channel_id=1, source_target_pairs={{0,2},{1,3},{2,0},{3,1},{4,6},{5,7},{6,4},{7,5},{8,10},{9,11},{10,... | collective-permute-start | bytes 393224 | tf_op jit(solution)/shard_map/ppermute | solution.py:328
  6.0 0.1 collective-permute-start.3
  6.1 0.2 shard_map.76
  6.3 0.0 collective-permute-done.1.do_par
  6.3 0.2 shard_map.77
  6.5 0.8 %shard_map.80.stats_in = f32[8,1024]{1,0:T(8,128)S(1)} custom-call(bf16[4,256,128]{2,1,0:T(8,128)(2,1)S(1)} %get-tuple-element.25.khot_ref, bf16[128,512]{1,0:T(8,128)(2,1)S(1)} %get-tuple-element.26.rhot_ref, bf16[256,512]{1,0:T(8,128)(2,1)S(1)} %get-tuple-element.27.qd_own, bf16[256,512]{1,0:T(8,128)(2,1)S(1)} %get-tuple-element.28.qd_par, ...), custom_call_target="tpu_custom_call" | custom-call | bytes 524288 | tf_op jit(solution)/shard_map/pallas_call | solution.py:289
  7.3 2.5 %collective-permute-done.2 = bf16[256,256]{1,0:T(8,128)(2,1)S(1)} collective-permute-done((bf16[256,256]{1,0:T(8,128)(2,1)S(1)}, bf16[256,256]{1,0:T(8,128)(2,1)S(1)}, u32[]{:S(2)}, u32[]{:S(2)}) %collective-permute-start.2) | collective-permute-done | bytes 131104 | tf_op jit(solution)/shard_map/ppermute | solution.py:328
  9.8 2.2 %collective-permute-done.4 = bf16[256,256]{1,0:T(8,128)(2,1)S(1)} collective-permute-done((bf16[256,256]{1,0:T(8,128)(2,1)S(1)}, bf16[256,256]{1,0:T(8,128)(2,1)S(1)}, u32[]{:S(2)}, u32[]{:S(2)}) %collective-permute-start.4) | collective-permute-done | bytes 131104 | tf_op jit(solution)/shard_map/ppermute | solution.py:328
  12.1 0.0 collective-permute-done.3
  12.1 0.0 collective-permute-start.5
  12.1 1.2 %collective-permute-done.5.other_ref = f32[8,1024]{1,0:T(8,128)S(1)} collective-permute-done((f32[8,1024]{1,0:T(8,128)S(1)}, f32[8,1024]{1,0:T(8,128)S(1)}, u32[]{:S(2)}, u32[]{:S(2)}) %collective-permute-start.5) | collective-permute-done | bytes 32800 | tf_op jit(solution)/shard_map/ppermute | solution.py:331
  13.3 0.1 shard_map.84
  13.4 3.5 %collective-permute-start.6 = (bf16[256,256]{1,0:T(8,128)(2,1)S(1)}, bf16[256,256]{1,0:T(8,128)(2,1)S(1)}, u32[]{:S(2)}, u32[]{:S(2)}) collective-permute-start(bf16[256,256]{1,0:T(8,128)(2,1)S(1)} %bitcast.16), channel_id=1, source_target_pairs={{0,6},{1,7},{2,4},{3,5},{4,2},{5,3},{6,0},{7,1},{8,14},{9,15},{10,... | collective-permute-start | bytes 393224 | tf_op jit(solution)/shard_map/ppermute | solution.py:328
  16.9 0.1 shard_map.85
  17.0 0.1 collective-permute-start.8
  17.1 2.1 %collective-permute-start.7 = (bf16[256,256]{1,0:T(8,128)(2,1)S(1)}, bf16[256,256]{1,0:T(8,128)(2,1)S(1)}, u32[]{:S(2)}, u32[]{:S(2)}) collective-permute-start(bf16[256,256]{1,0:T(8,128)(2,1)S(1)} %bitcast.15), channel_id=1, source_target_pairs={{0,2},{1,3},{2,0},{3,1},{4,6},{5,7},{6,4},{7,5},{8,10},{9,11},{10,... | collective-permute-start | bytes 393224 | tf_op jit(solution)/shard_map/ppermute | solution.py:328
  19.2 1.8 %collective-permute-done.6.after_ref.rest_2_ = bf16[256,256]{1,0:T(8,128)(2,1)S(1)} collective-permute-done((bf16[256,256]{1,0:T(8,128)(2,1)S(1)}, bf16[256,256]{1,0:T(8,128)(2,1)S(1)}, u32[]{:S(2)}, u32[]{:S(2)}) %collective-permute-start.6) | collective-permute-done | bytes 131104 | tf_op jit(solution)/shard_map/ppermute | solution.py:328
  21.0 1.6 %shard_map.87 = (f32[256,256]{1,0:T(8,128)S(1)}, f32[256,256]{1,0:T(8,128)S(1)}, f32[256,256]{1,0:T(8,128)S(1)}) custom-call(bf16[256,256]{1,0:T(8,128)(2,1)S(1)} %collective-permute-done.6.after_ref.rest_2_, bf16[4,256,128]{2,1,0:T(8,128)(2,1)S(1)} %get-tuple-element.25.khot_ref, bf16[128,512]{1,0:T(8,128)(2,1)S(1)} %get-tuple-element.26.rhot_ref, ...), custom_call_target="tpu_custom_call" | custom-call | flops 4000000000 | bytes 524288 | tf_op jit(solution)/shard_map/pallas_call | solution.py:289
  22.6 1.1 %collective-permute-done.8.rest_1_ = bf16[256,256]{1,0:T(8,128)(2,1)S(1)} collective-permute-done((bf16[256,256]{1,0:T(8,128)(2,1)S(1)}, bf16[256,256]{1,0:T(8,128)(2,1)S(1)}, u32[]{:S(2)}, u32[]{:S(2)}) %collective-permute-start.8) | collective-permute-done | bytes 131104 | tf_op jit(solution)/shard_map/ppermute | solution.py:328
  23.7 0.1 shard_map.88
  23.8 0.2 collective-permute-start.9
  23.9 3.6 %collective-permute-start.10 = (bf16[64,256]{1,0:T(8,128)(2,1)S(1)}, bf16[64,256]{1,0:T(8,128)(2,1)S(1)}, u32[]{:S(2)}, u32[]{:S(2)}) collective-permute-start(bf16[64,256]{1,0:T(8,128)(2,1)S(1)} %get-tuple-element.42), channel_id=1, source_target_pairs={{0,24},{8,16},{16,8},{24,0},{1,25},{9,17},{17,9},{25,1},{2,26},{10... | collective-permute-start | bytes 98312 | tf_op jit(solution)/shard_map/ppermute | solution.py:386
  27.5 0.8 %collective-permute-start.12 = (bf16[64,256]{1,0:T(8,128)(2,1)S(1)}, bf16[64,256]{1,0:T(8,128)(2,1)S(1)}, u32[]{:S(2)}, u32[]{:S(2)}) collective-permute-start(bf16[64,256]{1,0:T(8,128)(2,1)S(1)} %get-tuple-element.44), channel_id=1, source_target_pairs={{0,8},{8,0},{16,24},{24,16},{1,9},{9,1},{17,25},{25,17},{2,10},{10... | collective-permute-start | bytes 98312 | tf_op jit(solution)/shard_map/ppermute | solution.py:386
  28.3 0.8 %shard_map.89 = (bf16[256,256]{1,0:T(8,128)(2,1)}, f32[8,128]{1,0:T(8,128)S(1)}) custom-call(f32[256,256]{1,0:T(8,128)S(1)} %get-tuple-element.33.dq_own, f32[256,256]{1,0:T(8,128)S(1)} %collective-permute-done.9.dq_far), custom_call_target="tpu_custom_call" | custom-call | flops 2000000000 | bytes 524288 | tf_op jit(solution)/shard_map/pallas_call | solution.py:289
  29.1 0.6 %collective-permute-done.10.rest_0_ = bf16[64,256]{1,0:T(8,128)(2,1)S(1)} collective-permute-done((bf16[64,256]{1,0:T(8,128)(2,1)S(1)}, bf16[64,256]{1,0:T(8,128)(2,1)S(1)}, u32[]{:S(2)}, u32[]{:S(2)}) %collective-permute-start.10) | collective-permute-done | bytes 32800 | tf_op jit(solution)/shard_map/ppermute | solution.py:386
  29.7 2.7 %collective-permute-done.11.rest_1_ = bf16[64,256]{1,0:T(8,128)(2,1)S(1)} collective-permute-done((bf16[64,256]{1,0:T(8,128)(2,1)S(1)}, bf16[64,256]{1,0:T(8,128)(2,1)S(1)}, u32[]{:S(2)}, u32[]{:S(2)}) %collective-permute-start.11) | collective-permute-done | bytes 32800 | tf_op jit(solution)/shard_map/ppermute | solution.py:386
  32.4 0.6 %shard_map.90 = (bf16[32,256]{1,0:T(8,128)(2,1)}, bf16[32,256]{1,0:T(8,128)(2,1)}) custom-call(f32[8,128]{1,0:T(8,128)S(1)} %get-tuple-element.40.after_ref, f32[64,256]{1,0:T(8,128)S(1)} %get-tuple-element.41.keep_ref, bf16[64,256]{1,0:T(8,128)(2,1)S(1)} %collective-permute-done.10.rest_0_, bf16[64,256]{1,0:T(8,128)(2,1)S(1)} %collective-permute-done.11.rest_1_, ...), custom_call_target="tpu_custom_call" | custom-call | bytes 524288 | tf_op jit(solution)/shard_map/pallas_call | solution.py:289
  (20 shorter events, 0.1 us)
Async XLA Ops:
  0.6 0.8 %copy-start.3 = (bf16[256,128]{1,0:T(8,128)(2,1)S(1)}, bf16[256,128]{1,0:T(8,128)(2,1)}, u32[]{:S(2)}) copy-start(bf16[256,128]{1,0:T(8,128)(2,1)} %value_ref.1) | copy-start | bytes 196612
  0.6 0.9 %copy-start.2 = (bf16[256,128]{1,0:T(8,128)(2,1)S(1)}, bf16[256,128]{1,0:T(8,128)(2,1)}, u32[]{:S(2)}) copy-start(bf16[256,128]{1,0:T(8,128)(2,1)} %key_ref.1) | copy-start | bytes 196612
  0.7 5.7 %collective-permute-start = (bf16[256,256]{1,0:T(8,128)(2,1)}, bf16[256,256]{1,0:T(8,128)(2,1)S(1)}, u32[]{:S(2)}, u32[]{:S(2)}) collective-permute-start(bf16[256,256]{1,0:T(8,128)(2,1)} %q_own.1), channel_id=1, source_target_pairs={{0,1},{1,0},{2,3},{3,2},{4,5},{5,4},{6,7},{7,6},{8,9},{9,8},{10,11... | collective-permute-start | bytes 393224 | tf_op jit(solution)/shard_map/ppermute | solution.py:331
  1.2 5.2 %collective-permute-start.1 = (bf16[256,256]{1,0:T(8,128)(2,1)}, bf16[256,256]{1,0:T(8,128)(2,1)S(1)}, u32[]{:S(2)}, u32[]{:S(2)}) collective-permute-start(bf16[256,256]{1,0:T(8,128)(2,1)} %do_own.1), channel_id=1, source_target_pairs={{0,1},{1,0},{2,3},{3,2},{4,5},{5,4},{6,7},{7,6},{8,9},{9,8},{10,11... | collective-permute-start | bytes 393224 | tf_op jit(solution)/shard_map/ppermute | solution.py:331
  1.5 4.6 %copy-start.4 = (s32[2048]{0:T(1024)S(1)}, s32[2048]{0:T(1024)}, u32[]{:S(2)}) copy-start(s32[2048]{0:T(1024)} %param.9) | copy-start | bytes 24580
  1.5 4.8 %copy-start = (bf16[256,256]{1,0:T(8,128)(2,1)S(1)}, bf16[256,256]{1,0:T(8,128)(2,1)}, u32[]{:S(2)}) copy-start(bf16[256,256]{1,0:T(8,128)(2,1)} %q_own.1) | copy-start | bytes 393220
  1.5 4.8 %copy-start.1 = (bf16[256,256]{1,0:T(8,128)(2,1)S(1)}, bf16[256,256]{1,0:T(8,128)(2,1)}, u32[]{:S(2)}) copy-start(bf16[256,256]{1,0:T(8,128)(2,1)} %do_own.1) | copy-start | bytes 393220
  1.5 8.3 %collective-permute-start.2 = (bf16[256,256]{1,0:T(8,128)(2,1)S(1)}, bf16[256,256]{1,0:T(8,128)(2,1)S(1)}, u32[]{:S(2)}, u32[]{:S(2)}) collective-permute-start(bf16[256,256]{1,0:T(8,128)(2,1)S(1)} %shard_map.79.kv_ref), channel_id=1, source_target_pairs={{0,6},{1,7},{2,4},{3,5},{4,2},{5,3},{6,0},{7,1},{8,14},{9,15},{10,... | collective-permute-start | bytes 393224 | tf_op jit(solution)/shard_map/ppermute | solution.py:328
  5.5 6.6 %collective-permute-start.4 = (bf16[256,256]{1,0:T(8,128)(2,1)S(1)}, bf16[256,256]{1,0:T(8,128)(2,1)S(1)}, u32[]{:S(2)}, u32[]{:S(2)}) collective-permute-start(bf16[256,256]{1,0:T(8,128)(2,1)S(1)} %shard_map.79.kv_ref), channel_id=1, source_target_pairs={{0,2},{1,3},{2,0},{3,1},{4,6},{5,7},{6,4},{7,5},{8,10},{9,11},{10,... | collective-permute-start | bytes 393224 | tf_op jit(solution)/shard_map/ppermute | solution.py:328
  6.0 6.0 %collective-permute-start.3 = (bf16[256,256]{1,0:T(8,128)(2,1)S(1)}, bf16[256,256]{1,0:T(8,128)(2,1)S(1)}, u32[]{:S(2)}, u32[]{:S(2)}) collective-permute-start(bf16[256,256]{1,0:T(8,128)(2,1)S(1)} %shard_map.79.kv_ref), channel_id=1, source_target_pairs={{0,4},{1,5},{2,6},{3,7},{4,0},{5,1},{6,2},{7,3},{8,12},{9,13},{10,... | collective-permute-start | bytes 393224 | tf_op jit(solution)/shard_map/ppermute | solution.py:328
  12.1 1.2 %collective-permute-start.5 = (f32[8,1024]{1,0:T(8,128)S(1)}, f32[8,1024]{1,0:T(8,128)S(1)}, u32[]{:S(2)}, u32[]{:S(2)}) collective-permute-start(f32[8,1024]{1,0:T(8,128)S(1)} %shard_map.82.stats_ref), channel_id=1, source_target_pairs={{0,1},{1,0},{2,3},{3,2},{4,5},{5,4},{6,7},{7,6},{8,9},{9,8},{10,11... | collective-permute-start | bytes 98312 | tf_op jit(solution)/shard_map/ppermute | solution.py:331
  13.4 7.6 %collective-permute-start.6 = (bf16[256,256]{1,0:T(8,128)(2,1)S(1)}, bf16[256,256]{1,0:T(8,128)(2,1)S(1)}, u32[]{:S(2)}, u32[]{:S(2)}) collective-permute-start(bf16[256,256]{1,0:T(8,128)(2,1)S(1)} %bitcast.16), channel_id=1, source_target_pairs={{0,6},{1,7},{2,4},{3,5},{4,2},{5,3},{6,0},{7,1},{8,14},{9,15},{10,... | collective-permute-start | bytes 393224 | tf_op jit(solution)/shard_map/ppermute | solution.py:328
  17.0 6.7 %collective-permute-start.8 = (bf16[256,256]{1,0:T(8,128)(2,1)S(1)}, bf16[256,256]{1,0:T(8,128)(2,1)S(1)}, u32[]{:S(2)}, u32[]{:S(2)}) collective-permute-start(bf16[256,256]{1,0:T(8,128)(2,1)S(1)} %bitcast.14), channel_id=1, source_target_pairs={{0,4},{1,5},{2,6},{3,7},{4,0},{5,1},{6,2},{7,3},{8,12},{9,13},{10,... | collective-permute-start | bytes 393224 | tf_op jit(solution)/shard_map/ppermute | solution.py:328
  17.1 6.6 %collective-permute-start.7 = (bf16[256,256]{1,0:T(8,128)(2,1)S(1)}, bf16[256,256]{1,0:T(8,128)(2,1)S(1)}, u32[]{:S(2)}, u32[]{:S(2)}) collective-permute-start(bf16[256,256]{1,0:T(8,128)(2,1)S(1)} %bitcast.15), channel_id=1, source_target_pairs={{0,2},{1,3},{2,0},{3,1},{4,6},{5,7},{6,4},{7,5},{8,10},{9,11},{10,... | collective-permute-start | bytes 393224 | tf_op jit(solution)/shard_map/ppermute | solution.py:328
  23.8 4.6 %collective-permute-start.9 = (f32[256,256]{1,0:T(8,128)S(1)}, f32[256,256]{1,0:T(8,128)S(1)}, u32[]{:S(2)}, u32[]{:S(2)}) collective-permute-start(f32[256,256]{1,0:T(8,128)S(1)} %get-tuple-element.38), channel_id=1, source_target_pairs={{0,1},{1,0},{2,3},{3,2},{4,5},{5,4},{6,7},{7,6},{8,9},{9,8},{10,11... | collective-permute-start | bytes 786440 | tf_op jit(solution)/shard_map/ppermute | solution.py:331
  23.9 5.7 %collective-permute-start.10 = (bf16[64,256]{1,0:T(8,128)(2,1)S(1)}, bf16[64,256]{1,0:T(8,128)(2,1)S(1)}, u32[]{:S(2)}, u32[]{:S(2)}) collective-permute-start(bf16[64,256]{1,0:T(8,128)(2,1)S(1)} %get-tuple-element.42), channel_id=1, source_target_pairs={{0,24},{8,16},{16,8},{24,0},{1,25},{9,17},{17,9},{25,1},{2,26},{10... | collective-permute-start | bytes 98312 | tf_op jit(solution)/shard_map/ppermute | solution.py:386
  27.5 4.8 %collective-permute-start.11 = (bf16[64,256]{1,0:T(8,128)(2,1)S(1)}, bf16[64,256]{1,0:T(8,128)(2,1)S(1)}, u32[]{:S(2)}, u32[]{:S(2)}) collective-permute-start(bf16[64,256]{1,0:T(8,128)(2,1)S(1)} %get-tuple-element.43), channel_id=1, source_target_pairs={{0,16},{8,24},{16,0},{24,8},{1,17},{9,25},{17,1},{25,9},{2,18},{10... | collective-permute-start | bytes 98312 | tf_op jit(solution)/shard_map/ppermute | solution.py:386
  27.5 4.8 %collective-permute-start.12 = (bf16[64,256]{1,0:T(8,128)(2,1)S(1)}, bf16[64,256]{1,0:T(8,128)(2,1)S(1)}, u32[]{:S(2)}, u32[]{:S(2)}) collective-permute-start(bf16[64,256]{1,0:T(8,128)(2,1)S(1)} %get-tuple-element.44), channel_id=1, source_target_pairs={{0,8},{8,0},{16,24},{24,16},{1,9},{9,1},{17,25},{25,17},{2,10},{10... | collective-permute-start | bytes 98312 | tf_op jit(solution)/shard_map/ppermute | solution.py:386

commit v5 on v4

--- a/solution.py
+++ b/solution.py
@@ -12,6 +12,8 @@
 LOG2E = 1.4426950408889634
 MASKED = -1.0e30
 LOWEST = -1.0e20
+DOC_MOST = {2048: 1280, 8192: 4352}
+CORNER = [(1, 7), (7, 6), (6, 2), (2, 4), (4, 0), (0, 1), (3, 5), (5, 3)]
 F32 = jnp.float32
 BF16 = jnp.bfloat16
 
@@ -86,17 +88,13 @@
 
 
 def add_grads(kv, khot, qds, rhot_ref, sides, causal, norm_ref, dqt_ref, fresh):
-    qts, dots, lows, grads = [], [], [], []
+    qts, dots, lows, grads, all_lanes = [], [], [], [], []
     for lanes, qt, dot, penalty in chunks_of(sides, qds, rhot_ref):
         scores = scores_of(kv, khot, qt, penalty, causal)
         weights = jnp.exp2(scores * (SCALE * LOG2E) - norm_ref[0:1, lanes])
         grad_probs = nn(kv[:, HD:], dot)
         grad_scores = (weights * (grad_probs - norm_ref[1:2, lanes])).astype(BF16)
-        change = tn(kv[:, :HD], grad_scores)
-        if fresh:
-            dqt_ref[:, lanes] = change
-        else:
-            dqt_ref[:, lanes] += change
+        all_lanes.append(lanes)
         qts.append(qt)
         dots.append(dot)
         lows.append(weights.astype(BF16))
@@ -105,6 +103,12 @@
     def joined(parts):
         return jnp.concatenate(parts, axis=1)
 
+    span = slice(all_lanes[0].start, all_lanes[-1].stop)
+    change = tn(kv[:, :HD], joined(grads))
+    if fresh:
+        dqt_ref[:, span] = change
+    else:
+        dqt_ref[:, span] += change
     dkt = nt(joined(qts), joined(grads)) * SCALE
     dvt = nt(joined(dots), joined(lows))
     return jnp.concatenate([dkt, dvt], axis=0)
@@ -197,8 +201,10 @@
 
 
 def far_grads_kernel(
-    first, docs_ref, khot_ref, rhot_ref, qd_own, qd_par, norm_ref, kv_ref, out_ref, dqt_ref
+    later, first, docs_ref, khot_ref, rhot_ref, qd_own, qd_par, norm_ref, kv_ref, *rest
 ):
+    held = (len(rest) - later - 2) // 2
+    out_ref, dqt_ref = rest[later + held : later + held + 2]
     alone = kv_ref.shape[0] == 1
     qds = qd_own, qd_par
 
@@ -242,6 +248,15 @@
 def query_kernel(dq_own, dq_far, dq_ref, token_ref):
     token_ref[...] = jnp.zeros(token_ref.shape, F32)
     dq_ref[...] = jnp.transpose(dq_own[...] + dq_far[...]).astype(BF16)
+
+
+def hops_of(share):
+    return [1, 2, 3] if share == 4 else list(range(1, share))
+
+
+def next_of(share, member, away):
+    line = list(range(share))
+    return line[(line.index(member) + away) % share]
 
 
 def combine_kernel(share, count, dq_in, own_ref, *rest):
@@ -253,8 +268,9 @@
         total = total + part[...].astype(F32)
     sum_ref[...] = total
     member = lax.axis_index("grp") % share
-    for away, out_ref in zip((0, *range(share - 1, 0, -1)), (keep_ref, *send_refs)):
-        first = pl.multiple_of((member ^ away) * width, width)
+    for away, out_ref in zip((0, *hops_of(share)), (keep_ref, *send_refs)):
+        target = sum((member == i) * next_of(share, i, away) for i in range(share))
+        first = pl.multiple_of(target * width, width)
         for half in range(2):
             piece = sum_ref[pl.ds(half * HD + first, width), :]
             out_ref[half * width : (half + 1) * width, :] = piece.astype(out_ref.dtype)
@@ -324,8 +340,13 @@
     )
     docs = doc_ids.reshape(srv, rows)
 
-    def trade(block, away):
-        return lax.ppermute(block, "srv", [(i, i ^ 2 * away) for i in range(srv)])
+    apart = DOC_MOST.get(srv * rows, srv * rows) <= 5 * rows + 1
+
+    def trade(block, away, back=False):
+        pairs = [(i, i ^ 2 * away) for i in range(srv)]
+        if srv == 8 and away == 3 and apart:
+            pairs = [(b, a) for a, b in CORNER] if back else CORNER
+        return lax.ppermute(block, "srv", pairs)
 
     def swap(block):
         return lax.ppermute(block, "srv", [(i, i ^ 1) for i in range(srv)])
@@ -348,7 +369,7 @@
     (stats,) = call(
         own_stats_kernel, [sds((8, lanes), F32)], [*shared[1:], own_kv, blank]
     )
-    for firsts in (list(far_kv)[:1], list(far_kv)[1:]):
+    for firsts in [[first] for first in ([3, 1, 2] if chips == 4 else far_kv)]:
         if firsts:
             (stats,) = call(
                 functools.partial(far_stats_kernel, firsts),
@@ -356,19 +377,36 @@
                 [*shared, stats, *[far_kv[first] for first in firsts]],
             )
     (norm,) = call(norm_kernel, [sds((8, lanes), F32)], [stats, swap(stats)])
-    came, dqt = [], []
-    for first, kv in reversed(far_kv.items()):
-        part, dqt_part = call(
-            functools.partial(far_grads_kernel, first),
-            [sds(kv.shape[:1] + (2 * HD, rows), BF16), sds((HD, lanes), F32)],
-            [*shared, norm, kv],
-            )
+    turns = [3, 2, 1] if chips == 4 else list(far_kv)
+    waits = {} if chips == 4 else {}
+    starts = [3, 2, 1] if chips == 4 else list(far_kv)
+    parts, dqt = {}, []
+    for turn, first in enumerate(turns):
+        kv = far_kv[first]
+        later = dqt[-1:]
+        held = [parts[one] for one in waits.get(turn, [])]
+        base = len(shared) + 2
+        part, dqt_part, *held = call(
+            functools.partial(far_grads_kernel, len(later), first),
+            [sds(kv.shape[:1] + (2 * HD, rows), BF16), sds((HD, lanes), F32)]
+            + [sds(one.shape, BF16) for one in held],
+            [*shared, norm, kv, *later, *held],
+            unread=range(base, base + len(later)),
+            aliases={base + len(later) + i: 2 + i for i in range(len(held))},
+        )
+        for one, passed in zip(waits.get(turn, []), held):
+            parts[one] = passed
+        parts[first] = part
         dqt.append(dqt_part)
-        came += [trade(part[slot], first + slot) for slot in range(kv.shape[0])]
+    came = [
+        trade(parts[first][slot], first + slot, True)
+        for first in starts
+        for slot in range(parts[first].shape[0])
+    ]
     own_dkv, dq_own, dq_par = call(
         own_grads_kernel,
         [sds((2 * HD, rows), F32)] + [sds((columns, rows), F32)] * 2,
-        [came[-1], *shared[1:], norm, own_kv, *dqt],
+        [came[0], *shared[1:], norm, own_kv, *dqt],
         scratch=[pltpu.VMEM((HD, lanes), F32)],
         unread=[0],
         us=4,
@@ -383,8 +421,8 @@
         aliases={0: 0},
     )
     back = [
-        lax.ppermute(part, "grp", [(i, i ^ away) for i in range(grp)])
-        for away, part in zip(range(share - 1, 0, -1), send)
+        lax.ppermute(part, "grp", [(i, i // share * share + next_of(share, i % share, away)) for i in range(grp)])
+        for away, part in zip(hops_of(share), send)
     ]
     grad_query, token = call(
         query_kernel,

time: 33.5 us -> 32.2 us (0.961)
  waiting for transfers between devices: 12.1 us -> 10.6 us
  starting transfers between devices: 15.4 us -> 16 us
    ppermute x9, waiting for transfers between devices: 10.9 us -> 9.43 us  [the longest x6 7.63 us: trade(): return lax.ppermute(block, 'srv', pairs)]
    ppermute x9, starting transfers between devices: 14.6 us -> 15.2 us  [the longest x6 9.65 us: trade(): return lax.ppermute(block, 'srv', pairs)]
    pallas_call x15 -> x16, Pallas kernels: 4.44 us -> 4.13 us  [call(): pl.pallas_call(kernel, out_shape=out_shape, in_specs=kinds, out_specs=res...]
  transfers between devices with their start and end apart: 13 -> 13, of which waited for: 7 -> 6; matrix products, arithmetic and copies ran while one was open for 0% -> 0% of each run, Pallas kernels for 11% -> 10%
where the time goes in v5:
time: 32.2 us; the launch traced here: 31.8 us
  starting transfers between devices  16 us (50%)
  waiting for transfers between devices  10.6 us (33%)
  Pallas kernels  4.13 us (13%)
  between operations  0.78 us (2%)
    ppermute x6, starting transfers between devices, trade(): return lax.ppermute(block, 'srv', pairs)  9.65 us
    ppermute x6, waiting for transfers between devices, trade(): return lax.ppermute(block, 'srv', pairs)  7.63 us
    ppermute x3, starting transfers between devices, on_device(): lax.ppermute(part, 'grp', [(i, i // share * share + next_of(share, i % sh...  5.56 us
    pallas_call x16, Pallas kernels, call(): pl.pallas_call(kernel, out_shape=out_shape, in_specs=kinds, out_specs=res...  4.13 us
    ppermute x3, waiting for transfers between devices, on_device(): lax.ppermute(part, 'grp', [(i, i // share * share + next_of(share, i % sh...  1.8 us
    ppermute x4, waiting for transfers between devices, swap(): return lax.ppermute(block, 'srv', [(i, i ^ 1) for i in range(srv)])  1.2 us
    ppermute x4, starting transfers between devices, swap(): return lax.ppermute(block, 'srv', [(i, i ^ 1) for i in range(srv)])  0.74 us
  transfers between devices with their start and end apart: 13, of which 6 were waited for; matrix products, arithmetic and copies ran while one was open for 0% of the time, Pallas kernels for 10%

profile of v5, /device:TPU:0, one launch (start us, length us, event | category | flops | bytes accessed | tf_op | source)
XLA Modules:
  0.0 31.8 jit_solution(12711416171279679914)
XLA Ops:
  0.7 0.5 %collective-permute-start = (bf16[256,256]{1,0:T(8,128)(2,1)}, bf16[256,256]{1,0:T(8,128)(2,1)S(1)}, u32[]{:S(2)}, u32[]{:S(2)}) collective-permute-start(bf16[256,256]{1,0:T(8,128)(2,1)} %q_own.1), channel_id=1, source_target_pairs={{0,1},{1,0},{2,3},{3,2},{4,5},{5,4},{6,7},{7,6},{8,9},{9,8},{10,11... | collective-permute-start | bytes 393224 | tf_op jit(solution)/shard_map/ppermute | solution.py:352
  1.2 0.1 collective-permute-start.1
  1.3 0.2 copy-done.3
  1.5 0.0 copy-done.2
  1.5 0.5 %collective-permute-start.2 = (bf16[256,256]{1,0:T(8,128)(2,1)S(1)}, bf16[256,256]{1,0:T(8,128)(2,1)S(1)}, u32[]{:S(2)}, u32[]{:S(2)}) collective-permute-start(bf16[256,256]{1,0:T(8,128)(2,1)S(1)} %shard_map.79.kv_ref), channel_id=1, source_target_pairs={{1,7},{7,6},{6,2},{2,4},{4,0},{0,1},{3,5},{5,3},{9,15},{15,14},{14... | collective-permute-start | bytes 393224 | tf_op jit(solution)/shard_map/ppermute | solution.py:349
  2.0 4.0 %collective-permute-start.3 = (bf16[256,256]{1,0:T(8,128)(2,1)S(1)}, bf16[256,256]{1,0:T(8,128)(2,1)S(1)}, u32[]{:S(2)}, u32[]{:S(2)}) collective-permute-start(bf16[256,256]{1,0:T(8,128)(2,1)S(1)} %shard_map.79.kv_ref), channel_id=1, source_target_pairs={{0,2},{1,3},{2,0},{3,1},{4,6},{5,7},{6,4},{7,5},{8,10},{9,11},{10,... | collective-permute-start | bytes 393224 | tf_op jit(solution)/shard_map/ppermute | solution.py:349
  6.0 0.5 %collective-permute-start.4 = (bf16[256,256]{1,0:T(8,128)(2,1)S(1)}, bf16[256,256]{1,0:T(8,128)(2,1)S(1)}, u32[]{:S(2)}, u32[]{:S(2)}) collective-permute-start(bf16[256,256]{1,0:T(8,128)(2,1)S(1)} %shard_map.79.kv_ref), channel_id=1, source_target_pairs={{0,4},{1,5},{2,6},{3,7},{4,0},{5,1},{6,2},{7,3},{8,12},{9,13},{10,... | collective-permute-start | bytes 393224 | tf_op jit(solution)/shard_map/ppermute | solution.py:349
  6.6 0.2 shard_map.76
  6.7 0.0 collective-permute-done.q_par
  6.7 0.0 collective-permute-done.1.do_par
  6.8 0.2 shard_map.77
  7.0 0.8 %shard_map.80.stats_in = f32[8,1024]{1,0:T(8,128)S(1)} custom-call(bf16[4,256,128]{2,1,0:T(8,128)(2,1)S(1)} %get-tuple-element.25.khot_ref, bf16[128,512]{1,0:T(8,128)(2,1)S(1)} %get-tuple-element.26.rhot_ref, bf16[256,512]{1,0:T(8,128)(2,1)S(1)} %get-tuple-element.27.qd_own, bf16[256,512]{1,0:T(8,128)(2,1)S(1)} %get-tuple-element.28.qd_par, ...), custom_call_target="tpu_custom_call" | custom-call | bytes 524288 | tf_op jit(solution)/shard_map/pallas_call | solution.py:305
  7.8 4.3 %collective-permute-done.3 = bf16[256,256]{1,0:T(8,128)(2,1)S(1)} collective-permute-done((bf16[256,256]{1,0:T(8,128)(2,1)S(1)}, bf16[256,256]{1,0:T(8,128)(2,1)S(1)}, u32[]{:S(2)}, u32[]{:S(2)}) %collective-permute-start.3) | collective-permute-done | bytes 131104 | tf_op jit(solution)/shard_map/ppermute | solution.py:349
  12.1 0.1 collective-permute-start.5
  12.2 1.2 %collective-permute-done.5.other_ref = f32[8,1024]{1,0:T(8,128)S(1)} collective-permute-done((f32[8,1024]{1,0:T(8,128)S(1)}, f32[8,1024]{1,0:T(8,128)S(1)}, u32[]{:S(2)}, u32[]{:S(2)}) %collective-permute-start.5) | collective-permute-done | bytes 32800 | tf_op jit(solution)/shard_map/ppermute | solution.py:352
  13.4 0.1 shard_map.85
  13.5 2.6 %collective-permute-start.6 = (bf16[256,256]{1,0:T(8,128)(2,1)S(1)}, bf16[256,256]{1,0:T(8,128)(2,1)S(1)}, u32[]{:S(2)}, u32[]{:S(2)}) collective-permute-start(bf16[256,256]{1,0:T(8,128)(2,1)S(1)} %bitcast.16), channel_id=1, source_target_pairs={{7,1},{6,7},{2,6},{4,2},{0,4},{1,0},{5,3},{3,5},{15,9},{14,15},{10... | collective-permute-start | bytes 393224 | tf_op jit(solution)/shard_map/ppermute | solution.py:349
  16.2 0.4 %collective-permute-start.7 = (bf16[256,256]{1,0:T(8,128)(2,1)S(1)}, bf16[256,256]{1,0:T(8,128)(2,1)S(1)}, u32[]{:S(2)}, u32[]{:S(2)}) collective-permute-start(bf16[256,256]{1,0:T(8,128)(2,1)S(1)} %bitcast.14), channel_id=1, source_target_pairs={{0,4},{1,5},{2,6},{3,7},{4,0},{5,1},{6,2},{7,3},{8,12},{9,13},{10,... | collective-permute-start | bytes 393224 | tf_op jit(solution)/shard_map/ppermute | solution.py:349
  16.6 1.6 %collective-permute-start.8 = (bf16[256,256]{1,0:T(8,128)(2,1)S(1)}, bf16[256,256]{1,0:T(8,128)(2,1)S(1)}, u32[]{:S(2)}, u32[]{:S(2)}) collective-permute-start(bf16[256,256]{1,0:T(8,128)(2,1)S(1)} %bitcast.15), channel_id=1, source_target_pairs={{0,2},{1,3},{2,0},{3,1},{4,6},{5,7},{6,4},{7,5},{8,10},{9,11},{10,... | collective-permute-start | bytes 393224 | tf_op jit(solution)/shard_map/ppermute | solution.py:349
  18.2 2.9 %collective-permute-done.6.after_ref.rest_0_ = bf16[256,256]{1,0:T(8,128)(2,1)S(1)} collective-permute-done((bf16[256,256]{1,0:T(8,128)(2,1)S(1)}, bf16[256,256]{1,0:T(8,128)(2,1)S(1)}, u32[]{:S(2)}, u32[]{:S(2)}) %collective-permute-start.6) | collective-permute-done | bytes 131104 | tf_op jit(solution)/shard_map/ppermute | solution.py:349
  21.1 1.3 %shard_map.88 = (f32[256,256]{1,0:T(8,128)S(1)}, f32[256,256]{1,0:T(8,128)S(1)}, f32[256,256]{1,0:T(8,128)S(1)}) custom-call(bf16[256,256]{1,0:T(8,128)(2,1)S(1)} %collective-permute-done.6.after_ref.rest_0_, bf16[4,256,128]{2,1,0:T(8,128)(2,1)S(1)} %get-tuple-element.25.khot_ref, bf16[128,512]{1,0:T(8,128)(2,1)S(1)} %get-tuple-element.26.rhot_ref, ...), custom_call_target="tpu_custom_call" | custom-call | flops 4000000000 | bytes 524288 | tf_op jit(solution)/shard_map/pallas_call | solution.py:305
  22.4 0.4 %collective-permute-done.7.rest_1_ = bf16[256,256]{1,0:T(8,128)(2,1)S(1)} collective-permute-done((bf16[256,256]{1,0:T(8,128)(2,1)S(1)}, bf16[256,256]{1,0:T(8,128)(2,1)S(1)}, u32[]{:S(2)}, u32[]{:S(2)}) %collective-permute-start.7) | collective-permute-done | bytes 131104 | tf_op jit(solution)/shard_map/ppermute | solution.py:349
  22.8 0.0 collective-permute-done.8.rest_2_
  22.8 0.1 shard_map.89
  22.9 0.1 collective-permute-start.9
  23.0 1.6 %collective-permute-start.10 = (bf16[64,256]{1,0:T(8,128)(2,1)S(1)}, bf16[64,256]{1,0:T(8,128)(2,1)S(1)}, u32[]{:S(2)}, u32[]{:S(2)}) collective-permute-start(bf16[64,256]{1,0:T(8,128)(2,1)S(1)} %get-tuple-element.42), channel_id=1, source_target_pairs={{0,8},{8,16},{16,24},{24,0},{1,9},{9,17},{17,25},{25,1},{2,10},{10... | collective-permute-start | bytes 98312 | tf_op jit(solution)/shard_map/ppermute | solution.py:424
  24.6 2.6 %collective-permute-start.11 = (bf16[64,256]{1,0:T(8,128)(2,1)S(1)}, bf16[64,256]{1,0:T(8,128)(2,1)S(1)}, u32[]{:S(2)}, u32[]{:S(2)}) collective-permute-start(bf16[64,256]{1,0:T(8,128)(2,1)S(1)} %get-tuple-element.43), channel_id=1, source_target_pairs={{0,16},{8,24},{16,0},{24,8},{1,17},{9,25},{17,1},{25,9},{2,18},{10... | collective-permute-start | bytes 98312 | tf_op jit(solution)/shard_map/ppermute | solution.py:424
  27.2 1.3 %collective-permute-start.12 = (bf16[64,256]{1,0:T(8,128)(2,1)S(1)}, bf16[64,256]{1,0:T(8,128)(2,1)S(1)}, u32[]{:S(2)}, u32[]{:S(2)}) collective-permute-start(bf16[64,256]{1,0:T(8,128)(2,1)S(1)} %get-tuple-element.44), channel_id=1, source_target_pairs={{0,24},{8,0},{16,8},{24,16},{1,25},{9,1},{17,9},{25,17},{2,26},{10... | collective-permute-start | bytes 98312 | tf_op jit(solution)/shard_map/ppermute | solution.py:424
  28.6 0.8 %shard_map.90 = (bf16[256,256]{1,0:T(8,128)(2,1)}, f32[8,128]{1,0:T(8,128)S(1)}) custom-call(f32[256,256]{1,0:T(8,128)S(1)} %get-tuple-element.33.dq_own, f32[256,256]{1,0:T(8,128)S(1)} %collective-permute-done.9.dq_far), custom_call_target="tpu_custom_call" | custom-call | flops 2000000000 | bytes 524288 | tf_op jit(solution)/shard_map/pallas_call | solution.py:305
  29.3 0.5 %collective-permute-done.11.rest_1_ = bf16[64,256]{1,0:T(8,128)(2,1)S(1)} collective-permute-done((bf16[64,256]{1,0:T(8,128)(2,1)S(1)}, bf16[64,256]{1,0:T(8,128)(2,1)S(1)}, u32[]{:S(2)}, u32[]{:S(2)}) %collective-permute-start.11) | collective-permute-done | bytes 32800 | tf_op jit(solution)/shard_map/ppermute | solution.py:424
  29.8 1.3 %collective-permute-done.12.rest_2_ = bf16[64,256]{1,0:T(8,128)(2,1)S(1)} collective-permute-done((bf16[64,256]{1,0:T(8,128)(2,1)S(1)}, bf16[64,256]{1,0:T(8,128)(2,1)S(1)}, u32[]{:S(2)}, u32[]{:S(2)}) %collective-permute-start.12) | collective-permute-done | bytes 32800 | tf_op jit(solution)/shard_map/ppermute | solution.py:424
  31.1 0.6 %shard_map.91 = (bf16[32,256]{1,0:T(8,128)(2,1)}, bf16[32,256]{1,0:T(8,128)(2,1)}) custom-call(f32[8,128]{1,0:T(8,128)S(1)} %get-tuple-element.40.after_ref, f32[64,256]{1,0:T(8,128)S(1)} %get-tuple-element.41.keep_ref, bf16[64,256]{1,0:T(8,128)(2,1)S(1)} %collective-permute-done.10.rest_0_, bf16[64,256]{1,0:T(8,128)(2,1)S(1)} %collective-permute-done.11.rest_1_, ...), custom_call_target="tpu_custom_call" | custom-call | bytes 524288 | tf_op jit(solution)/shard_map/pallas_call | solution.py:305
  (21 shorter events, 0.2 us)
Async XLA Ops:
  0.6 0.8 %copy-start.3 = (bf16[256,128]{1,0:T(8,128)(2,1)S(1)}, bf16[256,128]{1,0:T(8,128)(2,1)}, u32[]{:S(2)}) copy-start(bf16[256,128]{1,0:T(8,128)(2,1)} %value_ref.1) | copy-start | bytes 196612
  0.6 0.9 %copy-start.2 = (bf16[256,128]{1,0:T(8,128)(2,1)S(1)}, bf16[256,128]{1,0:T(8,128)(2,1)}, u32[]{:S(2)}) copy-start(bf16[256,128]{1,0:T(8,128)(2,1)} %key_ref.1) | copy-start | bytes 196612
  0.7 6.1 %collective-permute-start = (bf16[256,256]{1,0:T(8,128)(2,1)}, bf16[256,256]{1,0:T(8,128)(2,1)S(1)}, u32[]{:S(2)}, u32[]{:S(2)}) collective-permute-start(bf16[256,256]{1,0:T(8,128)(2,1)} %q_own.1), channel_id=1, source_target_pairs={{0,1},{1,0},{2,3},{3,2},{4,5},{5,4},{6,7},{7,6},{8,9},{9,8},{10,11... | collective-permute-start | bytes 393224 | tf_op jit(solution)/shard_map/ppermute | solution.py:352
  1.2 5.6 %collective-permute-start.1 = (bf16[256,256]{1,0:T(8,128)(2,1)}, bf16[256,256]{1,0:T(8,128)(2,1)S(1)}, u32[]{:S(2)}, u32[]{:S(2)}) collective-permute-start(bf16[256,256]{1,0:T(8,128)(2,1)} %do_own.1), channel_id=1, source_target_pairs={{0,1},{1,0},{2,3},{3,2},{4,5},{5,4},{6,7},{7,6},{8,9},{9,8},{10,11... | collective-permute-start | bytes 393224 | tf_op jit(solution)/shard_map/ppermute | solution.py:352
  1.5 5.1 %copy-start.4 = (s32[2048]{0:T(1024)S(1)}, s32[2048]{0:T(1024)}, u32[]{:S(2)}) copy-start(s32[2048]{0:T(1024)} %param.9) | copy-start | bytes 24580
  1.5 5.2 %copy-start = (bf16[256,256]{1,0:T(8,128)(2,1)S(1)}, bf16[256,256]{1,0:T(8,128)(2,1)}, u32[]{:S(2)}) copy-start(bf16[256,256]{1,0:T(8,128)(2,1)} %q_own.1) | copy-start | bytes 393220
  1.5 5.3 %copy-start.1 = (bf16[256,256]{1,0:T(8,128)(2,1)S(1)}, bf16[256,256]{1,0:T(8,128)(2,1)}, u32[]{:S(2)}) copy-start(bf16[256,256]{1,0:T(8,128)(2,1)} %do_own.1) | copy-start | bytes 393220
  1.5 6.2 %collective-permute-start.2 = (bf16[256,256]{1,0:T(8,128)(2,1)S(1)}, bf16[256,256]{1,0:T(8,128)(2,1)S(1)}, u32[]{:S(2)}, u32[]{:S(2)}) collective-permute-start(bf16[256,256]{1,0:T(8,128)(2,1)S(1)} %shard_map.79.kv_ref), channel_id=1, source_target_pairs={{1,7},{7,6},{6,2},{2,4},{4,0},{0,1},{3,5},{5,3},{9,15},{15,14},{14... | collective-permute-start | bytes 393224 | tf_op jit(solution)/shard_map/ppermute | solution.py:349
  2.0 10.0 %collective-permute-start.3 = (bf16[256,256]{1,0:T(8,128)(2,1)S(1)}, bf16[256,256]{1,0:T(8,128)(2,1)S(1)}, u32[]{:S(2)}, u32[]{:S(2)}) collective-permute-start(bf16[256,256]{1,0:T(8,128)(2,1)S(1)} %shard_map.79.kv_ref), channel_id=1, source_target_pairs={{0,2},{1,3},{2,0},{3,1},{4,6},{5,7},{6,4},{7,5},{8,10},{9,11},{10,... | collective-permute-start | bytes 393224 | tf_op jit(solution)/shard_map/ppermute | solution.py:349
  6.0 6.0 %collective-permute-start.4 = (bf16[256,256]{1,0:T(8,128)(2,1)S(1)}, bf16[256,256]{1,0:T(8,128)(2,1)S(1)}, u32[]{:S(2)}, u32[]{:S(2)}) collective-permute-start(bf16[256,256]{1,0:T(8,128)(2,1)S(1)} %shard_map.79.kv_ref), channel_id=1, source_target_pairs={{0,4},{1,5},{2,6},{3,7},{4,0},{5,1},{6,2},{7,3},{8,12},{9,13},{10,... | collective-permute-start | bytes 393224 | tf_op jit(solution)/shard_map/ppermute | solution.py:349
  12.1 1.3 %collective-permute-start.5 = (f32[8,1024]{1,0:T(8,128)S(1)}, f32[8,1024]{1,0:T(8,128)S(1)}, u32[]{:S(2)}, u32[]{:S(2)}) collective-permute-start(f32[8,1024]{1,0:T(8,128)S(1)} %shard_map.83.stats_ref), channel_id=1, source_target_pairs={{0,1},{1,0},{2,3},{3,2},{4,5},{5,4},{6,7},{7,6},{8,9},{9,8},{10,11... | collective-permute-start | bytes 98312 | tf_op jit(solution)/shard_map/ppermute | solution.py:352
  13.5 7.6 %collective-permute-start.6 = (bf16[256,256]{1,0:T(8,128)(2,1)S(1)}, bf16[256,256]{1,0:T(8,128)(2,1)S(1)}, u32[]{:S(2)}, u32[]{:S(2)}) collective-permute-start(bf16[256,256]{1,0:T(8,128)(2,1)S(1)} %bitcast.16), channel_id=1, source_target_pairs={{7,1},{6,7},{2,6},{4,2},{0,4},{1,0},{5,3},{3,5},{15,9},{14,15},{10... | collective-permute-start | bytes 393224 | tf_op jit(solution)/shard_map/ppermute | solution.py:349
  16.2 6.7 %collective-permute-start.7 = (bf16[256,256]{1,0:T(8,128)(2,1)S(1)}, bf16[256,256]{1,0:T(8,128)(2,1)S(1)}, u32[]{:S(2)}, u32[]{:S(2)}) collective-permute-start(bf16[256,256]{1,0:T(8,128)(2,1)S(1)} %bitcast.14), channel_id=1, source_target_pairs={{0,4},{1,5},{2,6},{3,7},{4,0},{5,1},{6,2},{7,3},{8,12},{9,13},{10,... | collective-permute-start | bytes 393224 | tf_op jit(solution)/shard_map/ppermute | solution.py:349
  16.6 6.2 %collective-permute-start.8 = (bf16[256,256]{1,0:T(8,128)(2,1)S(1)}, bf16[256,256]{1,0:T(8,128)(2,1)S(1)}, u32[]{:S(2)}, u32[]{:S(2)}) collective-permute-start(bf16[256,256]{1,0:T(8,128)(2,1)S(1)} %bitcast.15), channel_id=1, source_target_pairs={{0,2},{1,3},{2,0},{3,1},{4,6},{5,7},{6,4},{7,5},{8,10},{9,11},{10,... | collective-permute-start | bytes 393224 | tf_op jit(solution)/shard_map/ppermute | solution.py:349
  22.9 5.6 %collective-permute-start.9 = (f32[256,256]{1,0:T(8,128)S(1)}, f32[256,256]{1,0:T(8,128)S(1)}, u32[]{:S(2)}, u32[]{:S(2)}) collective-permute-start(f32[256,256]{1,0:T(8,128)S(1)} %get-tuple-element.38), channel_id=1, source_target_pairs={{0,1},{1,0},{2,3},{3,2},{4,5},{5,4},{6,7},{7,6},{8,9},{9,8},{10,11... | collective-permute-start | bytes 786440 | tf_op jit(solution)/shard_map/ppermute | solution.py:352
  23.0 6.3 %collective-permute-start.10 = (bf16[64,256]{1,0:T(8,128)(2,1)S(1)}, bf16[64,256]{1,0:T(8,128)(2,1)S(1)}, u32[]{:S(2)}, u32[]{:S(2)}) collective-permute-start(bf16[64,256]{1,0:T(8,128)(2,1)S(1)} %get-tuple-element.42), channel_id=1, source_target_pairs={{0,8},{8,16},{16,24},{24,0},{1,9},{9,17},{17,25},{25,1},{2,10},{10... | collective-permute-start | bytes 98312 | tf_op jit(solution)/shard_map/ppermute | solution.py:424
  24.6 5.2 %collective-permute-start.11 = (bf16[64,256]{1,0:T(8,128)(2,1)S(1)}, bf16[64,256]{1,0:T(8,128)(2,1)S(1)}, u32[]{:S(2)}, u32[]{:S(2)}) collective-permute-start(bf16[64,256]{1,0:T(8,128)(2,1)S(1)} %get-tuple-element.43), channel_id=1, source_target_pairs={{0,16},{8,24},{16,0},{24,8},{1,17},{9,25},{17,1},{25,9},{2,18},{10... | collective-permute-start | bytes 98312 | tf_op jit(solution)/shard_map/ppermute | solution.py:424
  27.2 3.9 %collective-permute-start.12 = (bf16[64,256]{1,0:T(8,128)(2,1)S(1)}, bf16[64,256]{1,0:T(8,128)(2,1)S(1)}, u32[]{:S(2)}, u32[]{:S(2)}) collective-permute-start(bf16[64,256]{1,0:T(8,128)(2,1)S(1)} %get-tuple-element.44), channel_id=1, source_target_pairs={{0,24},{8,0},{16,8},{24,16},{1,25},{9,1},{17,9},{25,17},{2,26},{10... | collective-permute-start | bytes 98312 | tf_op jit(solution)/shard_map/ppermute | solution.py:424

commit v6 on v5

--- a/solution.py
+++ b/solution.py
@@ -70,7 +70,7 @@
     return scores
 
 
-def add_stats(stats_ref, kv, khot, qds, rhot_ref, sides, causal):
+def add_stats(stats_ref, kv, khot, qds, rhot_ref, sides, causal, keep=()):
     for lanes, qt, dot, penalty in chunks_of(sides, qds, rhot_ref):
         scores = scores_of(kv, khot, qt, penalty, causal)
         grad_probs = nn(kv[:, HD:], dot)
@@ -78,6 +78,8 @@
         new = jnp.maximum(old, jnp.max(scores, axis=0, keepdims=True) * (SCALE * LOG2E))
         factor = jnp.exp2(old - new)
         weights = jnp.exp2(scores * (SCALE * LOG2E) - new)
+        for ref, kept in zip(keep, (weights, grad_probs)):
+            ref[:, lanes] = kept
         stats_ref[0:1, lanes] = new
         stats_ref[1:2, lanes] = stats_ref[1:2, lanes] * factor + jnp.sum(
             weights, axis=0, keepdims=True
@@ -87,12 +89,18 @@
         )
 
 
-def add_grads(kv, khot, qds, rhot_ref, sides, causal, norm_ref, dqt_ref, fresh):
+def add_grads(kv, khot, qds, rhot_ref, sides, causal, norm_ref, dqt_ref, fresh, keep=()):
     qts, dots, lows, grads, all_lanes = [], [], [], [], []
     for lanes, qt, dot, penalty in chunks_of(sides, qds, rhot_ref):
-        scores = scores_of(kv, khot, qt, penalty, causal)
-        weights = jnp.exp2(scores * (SCALE * LOG2E) - norm_ref[0:1, lanes])
-        grad_probs = nn(kv[:, HD:], dot)
+        if keep:
+            top_ref, weights_ref, probs_ref = keep
+            factor = jnp.exp2(top_ref[0:1, lanes] - norm_ref[0:1, lanes])
+            weights = weights_ref[:, lanes] * factor
+            grad_probs = probs_ref[:, lanes]
+        else:
+            scores = scores_of(kv, khot, qt, penalty, causal)
+            weights = jnp.exp2(scores * (SCALE * LOG2E) - norm_ref[0:1, lanes])
+            grad_probs = nn(kv[:, HD:], dot)
         grad_scores = (weights * (grad_probs - norm_ref[1:2, lanes])).astype(BF16)
         all_lanes.append(lanes)
         qts.append(qt)
@@ -174,16 +182,15 @@
         pl.loop(0, count)(step)
 
 
-def far_stats_kernel(firsts, docs_ref, khot_ref, rhot_ref, qd_own, qd_par, stats_in, *rest):
-    kv_refs, stats_ref = rest[:-1], rest[-1]
+def far_stats_kernel(first, docs_ref, khot_ref, rhot_ref, qd_own, qd_par, stats_in, kv_ref, *outs):
+    stats_ref, keep = outs[0], outs[1:]
     stats_ref[...] = stats_in[...]
     qds = qd_own, qd_par
-    for first, kv_ref in zip(firsts, kv_refs):
-
-        def body(slot, source, kv_ref=kv_ref):
-            add_stats(stats_ref, kv_ref[slot], khot_ref[source], qds, rhot_ref, (0, 1), False)
-
-        each_remote(first, kv_ref, docs_ref, body, None)
+
+    def body(slot, source):
+        add_stats(stats_ref, kv_ref[slot], khot_ref[source], qds, rhot_ref, (0, 1), False, keep)
+
+    each_remote(first, kv_ref, docs_ref, body, None)
 
 
 def norm_kernel(stats_ref, other_ref, norm_ref):
@@ -201,10 +208,9 @@
 
 
 def far_grads_kernel(
-    later, first, docs_ref, khot_ref, rhot_ref, qd_own, qd_par, norm_ref, kv_ref, *rest
+    first, docs_ref, khot_ref, rhot_ref, qd_own, qd_par, norm_ref, kv_ref, before_ref, *rest
 ):
-    held = (len(rest) - later - 2) // 2
-    out_ref, dqt_ref = rest[later + held : later + held + 2]
+    keep, (out_ref, dqt_ref) = rest[:-2], rest[-2:]
     alone = kv_ref.shape[0] == 1
     qds = qd_own, qd_par
 
@@ -216,15 +222,16 @@
         clear()
 
     def body(slot, source):
+        kv, khot = kv_ref[slot], khot_ref[source]
         part = add_grads(
-            kv_ref[slot], khot_ref[source], qds, rhot_ref, (0, 1), False, norm_ref, dqt_ref, alone
+            kv, khot, qds, rhot_ref, (0, 1), False, norm_ref, dqt_ref, alone, keep
         )
         out_ref[slot] = part.astype(BF16)
 
     each_remote(first, kv_ref, docs_ref, body, clear if alone else None)
 
 
-def own_grads_kernel(after_ref, khot_ref, rhot_ref, qd_own, qd_par, norm_ref, kv_ref, *rest):
+def own_grads_kernel(khot_ref, rhot_ref, qd_own, qd_par, norm_ref, kv_ref, *rest):
     dqt_in, (dkv_ref, dq_own, dq_par, dqt_ref) = rest[:-4], rest[-4:]
     rows = kv_ref.shape[0]
     heads = qd_own.shape[1] // rows
@@ -345,7 +352,7 @@
     def trade(block, away, back=False):
         pairs = [(i, i ^ 2 * away) for i in range(srv)]
         if srv == 8 and away == 3 and apart:
-            pairs = [(b, a) for a, b in CORNER] if back else CORNER
+            pairs = [(4, 2), (5, 3), (7, 1), (6, 5), (0, 4), (1, 0), (2, 6), (3, 7)] if back else CORNER
         return lax.ppermute(block, "srv", pairs)
 
     def swap(block):
@@ -369,46 +376,38 @@
     (stats,) = call(
         own_stats_kernel, [sds((8, lanes), F32)], [*shared[1:], own_kv, blank]
     )
-    for firsts in [[first] for first in ([3, 1, 2] if chips == 4 else far_kv)]:
-        if firsts:
-            (stats,) = call(
-                functools.partial(far_stats_kernel, firsts),
-                [sds((8, lanes), F32)],
-                [*shared, stats, *[far_kv[first] for first in firsts]],
-            )
+    turns = [3, 1, 2] if chips == 4 else list(far_kv)
+    kept = {}
+    for first in turns:
+        saved = [sds((rows, lanes), F32)] * 2 if chips == 4 else []
+        stats, *saved = call(
+            functools.partial(far_stats_kernel, first),
+            [sds((8, lanes), F32)] + saved,
+            [*shared, stats, far_kv[first]],
+        )
+        kept[first] = [stats, *saved] if saved else []
     (norm,) = call(norm_kernel, [sds((8, lanes), F32)], [stats, swap(stats)])
-    turns = [3, 2, 1] if chips == 4 else list(far_kv)
-    waits = {} if chips == 4 else {}
-    starts = [3, 2, 1] if chips == 4 else list(far_kv)
-    parts, dqt = {}, []
-    for turn, first in enumerate(turns):
+    parts, dqt = {}, [norm]
+    turns = [3, 2, 1] if chips == 4 else turns
+    for first in turns:
         kv = far_kv[first]
-        later = dqt[-1:]
-        held = [parts[one] for one in waits.get(turn, [])]
-        base = len(shared) + 2
-        part, dqt_part, *held = call(
-            functools.partial(far_grads_kernel, len(later), first),
-            [sds(kv.shape[:1] + (2 * HD, rows), BF16), sds((HD, lanes), F32)]
-            + [sds(one.shape, BF16) for one in held],
-            [*shared, norm, kv, *later, *held],
-            unread=range(base, base + len(later)),
-            aliases={base + len(later) + i: 2 + i for i in range(len(held))},
+        parts[first], dqt_part = call(
+            functools.partial(far_grads_kernel, first),
+            [sds(kv.shape[:1] + (2 * HD, rows), BF16), sds((HD, lanes), F32)],
+            [*shared, norm, kv, dqt[-1], *kept[first]],
+            unread=[len(shared) + 2],
         )
-        for one, passed in zip(waits.get(turn, []), held):
-            parts[one] = passed
-        parts[first] = part
         dqt.append(dqt_part)
     came = [
         trade(parts[first][slot], first + slot, True)
-        for first in starts
+        for first in turns
         for slot in range(parts[first].shape[0])
     ]
     own_dkv, dq_own, dq_par = call(
         own_grads_kernel,
         [sds((2 * HD, rows), F32)] + [sds((columns, rows), F32)] * 2,
-        [came[0], *shared[1:], norm, own_kv, *dqt],
+        [*shared[1:], norm, own_kv, *dqt[1:]],
         scratch=[pltpu.VMEM((HD, lanes), F32)],
-        unread=[0],
         us=4,
     )
     width = HD // share

time: 32.2 us -> 30.9 us (0.960)
  waiting for transfers between devices: 10.6 us -> 9.08 us
    ppermute x6, waiting for transfers between devices: 7.63 us -> 6.08 us  [trade(): return lax.ppermute(block, 'srv', pairs)]
    ppermute x6, starting transfers between devices: 9.65 us -> 10 us  [trade(): return lax.ppermute(block, 'srv', pairs)]
  transfers between devices with their start and end apart: 13 -> 13, of which waited for: 6 -> 7; matrix products, arithmetic and copies ran while one was open for 0% -> 0% of each run, Pallas kernels for 10% -> 11%
where the time goes in v6:
time: 30.9 us; the launch traced here: 30.6 us
  starting transfers between devices  16.3 us (53%)
  waiting for transfers between devices  9.08 us (29%)
  Pallas kernels  4.15 us (13%)
  between operations  0.79 us (3%)
    ppermute x6, starting transfers between devices, trade(): return lax.ppermute(block, 'srv', pairs)  10 us
    ppermute x6, waiting for transfers between devices, trade(): return lax.ppermute(block, 'srv', pairs)  6.08 us
    ppermute x3, starting transfers between devices, on_device(): lax.ppermute(part, 'grp', [(i, i // share * share + next_of(share, i % sh...  5.57 us
    pallas_call x16, Pallas kernels, call(): pl.pallas_call(kernel, out_shape=out_shape, in_specs=kinds, out_specs=res...  4.15 us
    ppermute x3, waiting for transfers between devices, on_device(): lax.ppermute(part, 'grp', [(i, i // share * share + next_of(share, i % sh...  1.8 us
    ppermute x4, waiting for transfers between devices, swap(): return lax.ppermute(block, 'srv', [(i, i ^ 1) for i in range(srv)])  1.2 us
    ppermute x4, starting transfers between devices, swap(): return lax.ppermute(block, 'srv', [(i, i ^ 1) for i in range(srv)])  0.74 us
  transfers between devices with their start and end apart: 13, of which 7 were waited for; matrix products, arithmetic and copies ran while one was open for 0% of the time, Pallas kernels for 11%

profile of v6, /device:TPU:0, one launch (start us, length us, event | category | flops | bytes accessed | tf_op | source)
XLA Modules:
  0.0 30.6 jit_solution(2847140692919547734)
XLA Ops:
  0.7 0.5 %collective-permute-start = (bf16[256,256]{1,0:T(8,128)(2,1)}, bf16[256,256]{1,0:T(8,128)(2,1)S(1)}, u32[]{:S(2)}, u32[]{:S(2)}) collective-permute-start(bf16[256,256]{1,0:T(8,128)(2,1)} %q_own.1), channel_id=1, source_target_pairs={{0,1},{1,0},{2,3},{3,2},{4,5},{5,4},{6,7},{7,6},{8,9},{9,8},{10,11... | collective-permute-start | bytes 393224 | tf_op jit(solution)/shard_map/ppermute | solution.py:359
  1.2 0.1 collective-permute-start.1
  1.3 0.2 copy-done.3
  1.5 0.0 copy-done.2
  1.5 0.5 %collective-permute-start.2 = (bf16[256,256]{1,0:T(8,128)(2,1)S(1)}, bf16[256,256]{1,0:T(8,128)(2,1)S(1)}, u32[]{:S(2)}, u32[]{:S(2)}) collective-permute-start(bf16[256,256]{1,0:T(8,128)(2,1)S(1)} %shard_map.79.kv_ref), channel_id=1, source_target_pairs={{1,7},{7,6},{6,2},{2,4},{4,0},{0,1},{3,5},{5,3},{9,15},{15,14},{14... | collective-permute-start | bytes 393224 | tf_op jit(solution)/shard_map/ppermute | solution.py:356
  2.0 4.0 %collective-permute-start.3 = (bf16[256,256]{1,0:T(8,128)(2,1)S(1)}, bf16[256,256]{1,0:T(8,128)(2,1)S(1)}, u32[]{:S(2)}, u32[]{:S(2)}) collective-permute-start(bf16[256,256]{1,0:T(8,128)(2,1)S(1)} %shard_map.79.kv_ref), channel_id=1, source_target_pairs={{0,2},{1,3},{2,0},{3,1},{4,6},{5,7},{6,4},{7,5},{8,10},{9,11},{10,... | collective-permute-start | bytes 393224 | tf_op jit(solution)/shard_map/ppermute | solution.py:356
  6.0 0.5 %collective-permute-start.4 = (bf16[256,256]{1,0:T(8,128)(2,1)S(1)}, bf16[256,256]{1,0:T(8,128)(2,1)S(1)}, u32[]{:S(2)}, u32[]{:S(2)}) collective-permute-start(bf16[256,256]{1,0:T(8,128)(2,1)S(1)} %shard_map.79.kv_ref), channel_id=1, source_target_pairs={{0,4},{1,5},{2,6},{3,7},{4,0},{5,1},{6,2},{7,3},{8,12},{9,13},{10,... | collective-permute-start | bytes 393224 | tf_op jit(solution)/shard_map/ppermute | solution.py:356
  6.6 0.2 shard_map.76
  6.7 0.0 collective-permute-done.q_par
  6.8 0.2 shard_map.77
  7.0 0.8 %shard_map.80.stats_in = f32[8,1024]{1,0:T(8,128)S(1)} custom-call(bf16[4,256,128]{2,1,0:T(8,128)(2,1)S(1)} %get-tuple-element.34.khot_ref, bf16[128,512]{1,0:T(8,128)(2,1)S(1)} %get-tuple-element.35.rhot_ref, bf16[256,512]{1,0:T(8,128)(2,1)S(1)} %get-tuple-element.36.qd_own, bf16[256,512]{1,0:T(8,128)(2,1)S(1)} %get-tuple-element.37.qd_par, ...), custom_call_target="tpu_custom_call" | custom-call | bytes 524288 | tf_op jit(solution)/shard_map/pallas_call | solution.py:312
  7.8 4.3 %collective-permute-done.3 = bf16[256,256]{1,0:T(8,128)(2,1)S(1)} collective-permute-done((bf16[256,256]{1,0:T(8,128)(2,1)S(1)}, bf16[256,256]{1,0:T(8,128)(2,1)S(1)}, u32[]{:S(2)}, u32[]{:S(2)}) %collective-permute-start.3) | collective-permute-done | bytes 131104 | tf_op jit(solution)/shard_map/ppermute | solution.py:356
  12.1 0.1 collective-permute-start.5
  12.2 1.2 %collective-permute-done.5.other_ref = f32[8,1024]{1,0:T(8,128)S(1)} collective-permute-done((f32[8,1024]{1,0:T(8,128)S(1)}, f32[8,1024]{1,0:T(8,128)S(1)}, u32[]{:S(2)}, u32[]{:S(2)}) %collective-permute-start.5) | collective-permute-done | bytes 32800 | tf_op jit(solution)/shard_map/ppermute | solution.py:359
  13.4 0.1 shard_map.85
  13.5 2.9 %collective-permute-start.6 = (bf16[256,256]{1,0:T(8,128)(2,1)S(1)}, bf16[256,256]{1,0:T(8,128)(2,1)S(1)}, u32[]{:S(2)}, u32[]{:S(2)}) collective-permute-start(bf16[256,256]{1,0:T(8,128)(2,1)S(1)} %bitcast.14), channel_id=1, source_target_pairs={{4,2},{5,3},{7,1},{6,5},{0,4},{1,0},{2,6},{3,7},{12,10},{13,11},{1... | collective-permute-start | bytes 393224 | tf_op jit(solution)/shard_map/ppermute | solution.py:356
  16.4 0.1 shard_map.87
  16.5 0.1 collective-permute-start.8
  16.6 2.0 %collective-permute-start.7 = (bf16[256,256]{1,0:T(8,128)(2,1)S(1)}, bf16[256,256]{1,0:T(8,128)(2,1)S(1)}, u32[]{:S(2)}, u32[]{:S(2)}) collective-permute-start(bf16[256,256]{1,0:T(8,128)(2,1)S(1)} %bitcast.15), channel_id=1, source_target_pairs={{0,4},{1,5},{2,6},{3,7},{4,0},{5,1},{6,2},{7,3},{8,12},{9,13},{10,... | collective-permute-start | bytes 393224 | tf_op jit(solution)/shard_map/ppermute | solution.py:356
  18.6 1.3 %shard_map.88 = (f32[256,256]{1,0:T(8,128)S(1)}, f32[256,256]{1,0:T(8,128)S(1)}, f32[256,256]{1,0:T(8,128)S(1)}) custom-call(bf16[4,256,128]{2,1,0:T(8,128)(2,1)S(1)} %get-tuple-element.34.khot_ref, bf16[128,512]{1,0:T(8,128)(2,1)S(1)} %get-tuple-element.35.rhot_ref, bf16[256,512]{1,0:T(8,128)(2,1)S(1)} %get-tuple-element.36.qd_own, ...), custom_call_target="tpu_custom_call" | custom-call | flops 4000000000 | bytes 524288 | tf_op jit(solution)/shard_map/pallas_call | solution.py:312
  19.9 0.1 collective-permute-done.6.rest_0_
  20.0 1.6 %collective-permute-done.8.rest_2_ = bf16[256,256]{1,0:T(8,128)(2,1)S(1)} collective-permute-done((bf16[256,256]{1,0:T(8,128)(2,1)S(1)}, bf16[256,256]{1,0:T(8,128)(2,1)S(1)}, u32[]{:S(2)}, u32[]{:S(2)}) %collective-permute-start.8) | collective-permute-done | bytes 131104 | tf_op jit(solution)/shard_map/ppermute | solution.py:356
  21.5 0.1 collective-permute-done.7.rest_1_
  21.7 0.1 shard_map.89
  21.8 0.1 collective-permute-start.9
  21.9 1.6 %collective-permute-start.10 = (bf16[64,256]{1,0:T(8,128)(2,1)S(1)}, bf16[64,256]{1,0:T(8,128)(2,1)S(1)}, u32[]{:S(2)}, u32[]{:S(2)}) collective-permute-start(bf16[64,256]{1,0:T(8,128)(2,1)S(1)} %get-tuple-element.60), channel_id=1, source_target_pairs={{0,8},{8,16},{16,24},{24,0},{1,9},{9,17},{17,25},{25,1},{2,10},{10... | collective-permute-start | bytes 98312 | tf_op jit(solution)/shard_map/ppermute | solution.py:423
  23.5 2.6 %collective-permute-start.11 = (bf16[64,256]{1,0:T(8,128)(2,1)S(1)}, bf16[64,256]{1,0:T(8,128)(2,1)S(1)}, u32[]{:S(2)}, u32[]{:S(2)}) collective-permute-start(bf16[64,256]{1,0:T(8,128)(2,1)S(1)} %get-tuple-element.61), channel_id=1, source_target_pairs={{0,16},{8,24},{16,0},{24,8},{1,17},{9,25},{17,1},{25,9},{2,18},{10... | collective-permute-start | bytes 98312 | tf_op jit(solution)/shard_map/ppermute | solution.py:423
  26.1 1.3 %collective-permute-start.12 = (bf16[64,256]{1,0:T(8,128)(2,1)S(1)}, bf16[64,256]{1,0:T(8,128)(2,1)S(1)}, u32[]{:S(2)}, u32[]{:S(2)}) collective-permute-start(bf16[64,256]{1,0:T(8,128)(2,1)S(1)} %get-tuple-element.62), channel_id=1, source_target_pairs={{0,24},{8,0},{16,8},{24,16},{1,25},{9,1},{17,9},{25,17},{2,26},{10... | collective-permute-start | bytes 98312 | tf_op jit(solution)/shard_map/ppermute | solution.py:423
  27.4 0.8 %shard_map.90 = (bf16[256,256]{1,0:T(8,128)(2,1)}, f32[8,128]{1,0:T(8,128)S(1)}) custom-call(f32[256,256]{1,0:T(8,128)S(1)} %get-tuple-element.50.dq_own, f32[256,256]{1,0:T(8,128)S(1)} %collective-permute-done.9.dq_far), custom_call_target="tpu_custom_call" | custom-call | flops 2000000000 | bytes 524288 | tf_op jit(solution)/shard_map/pallas_call | solution.py:312
  28.2 0.5 %collective-permute-done.11.rest_1_ = bf16[64,256]{1,0:T(8,128)(2,1)S(1)} collective-permute-done((bf16[64,256]{1,0:T(8,128)(2,1)S(1)}, bf16[64,256]{1,0:T(8,128)(2,1)S(1)}, u32[]{:S(2)}, u32[]{:S(2)}) %collective-permute-start.11) | collective-permute-done | bytes 32800 | tf_op jit(solution)/shard_map/ppermute | solution.py:423
  28.7 1.3 %collective-permute-done.12.rest_2_ = bf16[64,256]{1,0:T(8,128)(2,1)S(1)} collective-permute-done((bf16[64,256]{1,0:T(8,128)(2,1)S(1)}, bf16[64,256]{1,0:T(8,128)(2,1)S(1)}, u32[]{:S(2)}, u32[]{:S(2)}) %collective-permute-start.12) | collective-permute-done | bytes 32800 | tf_op jit(solution)/shard_map/ppermute | solution.py:423
  30.0 0.6 %shard_map.91 = (bf16[32,256]{1,0:T(8,128)(2,1)}, bf16[32,256]{1,0:T(8,128)(2,1)}) custom-call(f32[8,128]{1,0:T(8,128)S(1)} %get-tuple-element.58.after_ref, f32[64,256]{1,0:T(8,128)S(1)} %get-tuple-element.59.keep_ref, bf16[64,256]{1,0:T(8,128)(2,1)S(1)} %collective-permute-done.10.rest_0_, bf16[64,256]{1,0:T(8,128)(2,1)S(1)} %collective-permute-done.11.rest_1_, ...), custom_call_target="tpu_custom_call" | custom-call | bytes 524288 | tf_op jit(solution)/shard_map/pallas_call | solution.py:312
  (21 shorter events, 0.2 us)
Async XLA Ops:
  0.6 0.8 %copy-start.3 = (bf16[256,128]{1,0:T(8,128)(2,1)S(1)}, bf16[256,128]{1,0:T(8,128)(2,1)}, u32[]{:S(2)}) copy-start(bf16[256,128]{1,0:T(8,128)(2,1)} %value_ref.1) | copy-start | bytes 196612
  0.6 0.9 %copy-start.2 = (bf16[256,128]{1,0:T(8,128)(2,1)S(1)}, bf16[256,128]{1,0:T(8,128)(2,1)}, u32[]{:S(2)}) copy-start(bf16[256,128]{1,0:T(8,128)(2,1)} %key_ref.1) | copy-start | bytes 196612
  0.7 6.1 %collective-permute-start = (bf16[256,256]{1,0:T(8,128)(2,1)}, bf16[256,256]{1,0:T(8,128)(2,1)S(1)}, u32[]{:S(2)}, u32[]{:S(2)}) collective-permute-start(bf16[256,256]{1,0:T(8,128)(2,1)} %q_own.1), channel_id=1, source_target_pairs={{0,1},{1,0},{2,3},{3,2},{4,5},{5,4},{6,7},{7,6},{8,9},{9,8},{10,11... | collective-permute-start | bytes 393224 | tf_op jit(solution)/shard_map/ppermute | solution.py:359
  1.2 5.6 %collective-permute-start.1 = (bf16[256,256]{1,0:T(8,128)(2,1)}, bf16[256,256]{1,0:T(8,128)(2,1)S(1)}, u32[]{:S(2)}, u32[]{:S(2)}) collective-permute-start(bf16[256,256]{1,0:T(8,128)(2,1)} %do_own.1), channel_id=1, source_target_pairs={{0,1},{1,0},{2,3},{3,2},{4,5},{5,4},{6,7},{7,6},{8,9},{9,8},{10,11... | collective-permute-start | bytes 393224 | tf_op jit(solution)/shard_map/ppermute | solution.py:359
  1.5 5.1 %copy-start.4 = (s32[2048]{0:T(1024)S(1)}, s32[2048]{0:T(1024)}, u32[]{:S(2)}) copy-start(s32[2048]{0:T(1024)} %param.9) | copy-start | bytes 24580
  1.5 5.2 %copy-start = (bf16[256,256]{1,0:T(8,128)(2,1)S(1)}, bf16[256,256]{1,0:T(8,128)(2,1)}, u32[]{:S(2)}) copy-start(bf16[256,256]{1,0:T(8,128)(2,1)} %q_own.1) | copy-start | bytes 393220
  1.5 5.3 %copy-start.1 = (bf16[256,256]{1,0:T(8,128)(2,1)S(1)}, bf16[256,256]{1,0:T(8,128)(2,1)}, u32[]{:S(2)}) copy-start(bf16[256,256]{1,0:T(8,128)(2,1)} %do_own.1) | copy-start | bytes 393220
  1.5 6.2 %collective-permute-start.2 = (bf16[256,256]{1,0:T(8,128)(2,1)S(1)}, bf16[256,256]{1,0:T(8,128)(2,1)S(1)}, u32[]{:S(2)}, u32[]{:S(2)}) collective-permute-start(bf16[256,256]{1,0:T(8,128)(2,1)S(1)} %shard_map.79.kv_ref), channel_id=1, source_target_pairs={{1,7},{7,6},{6,2},{2,4},{4,0},{0,1},{3,5},{5,3},{9,15},{15,14},{14... | collective-permute-start | bytes 393224 | tf_op jit(solution)/shard_map/ppermute | solution.py:356
  2.0 10.0 %collective-permute-start.3 = (bf16[256,256]{1,0:T(8,128)(2,1)S(1)}, bf16[256,256]{1,0:T(8,128)(2,1)S(1)}, u32[]{:S(2)}, u32[]{:S(2)}) collective-permute-start(bf16[256,256]{1,0:T(8,128)(2,1)S(1)} %shard_map.79.kv_ref), channel_id=1, source_target_pairs={{0,2},{1,3},{2,0},{3,1},{4,6},{5,7},{6,4},{7,5},{8,10},{9,11},{10,... | collective-permute-start | bytes 393224 | tf_op jit(solution)/shard_map/ppermute | solution.py:356
  6.0 6.0 %collective-permute-start.4 = (bf16[256,256]{1,0:T(8,128)(2,1)S(1)}, bf16[256,256]{1,0:T(8,128)(2,1)S(1)}, u32[]{:S(2)}, u32[]{:S(2)}) collective-permute-start(bf16[256,256]{1,0:T(8,128)(2,1)S(1)} %shard_map.79.kv_ref), channel_id=1, source_target_pairs={{0,4},{1,5},{2,6},{3,7},{4,0},{5,1},{6,2},{7,3},{8,12},{9,13},{10,... | collective-permute-start | bytes 393224 | tf_op jit(solution)/shard_map/ppermute | solution.py:356
  12.1 1.3 %collective-permute-start.5 = (f32[8,1024]{1,0:T(8,128)S(1)}, f32[8,1024]{1,0:T(8,128)S(1)}, u32[]{:S(2)}, u32[]{:S(2)}) collective-permute-start(f32[8,1024]{1,0:T(8,128)S(1)} %get-tuple-element.40.stats_ref.rest_0_), channel_id=1, source_target_pairs={{0,1},{1,0},{2,3},{3,2},{4,5},{5,4},{6,7},{7,6},{8,9},{9,8},{10,11... | collective-permute-start | bytes 98312 | tf_op jit(solution)/shard_map/ppermute | solution.py:359
  13.5 6.5 %collective-permute-start.6 = (bf16[256,256]{1,0:T(8,128)(2,1)S(1)}, bf16[256,256]{1,0:T(8,128)(2,1)S(1)}, u32[]{:S(2)}, u32[]{:S(2)}) collective-permute-start(bf16[256,256]{1,0:T(8,128)(2,1)S(1)} %bitcast.14), channel_id=1, source_target_pairs={{4,2},{5,3},{7,1},{6,5},{0,4},{1,0},{2,6},{3,7},{12,10},{13,11},{1... | collective-permute-start | bytes 393224 | tf_op jit(solution)/shard_map/ppermute | solution.py:356
  16.5 5.0 %collective-permute-start.8 = (bf16[256,256]{1,0:T(8,128)(2,1)S(1)}, bf16[256,256]{1,0:T(8,128)(2,1)S(1)}, u32[]{:S(2)}, u32[]{:S(2)}) collective-permute-start(bf16[256,256]{1,0:T(8,128)(2,1)S(1)} %bitcast.16), channel_id=1, source_target_pairs={{0,2},{1,3},{2,0},{3,1},{4,6},{5,7},{6,4},{7,5},{8,10},{9,11},{10,... | collective-permute-start | bytes 393224 | tf_op jit(solution)/shard_map/ppermute | solution.py:356
  16.6 5.1 %collective-permute-start.7 = (bf16[256,256]{1,0:T(8,128)(2,1)S(1)}, bf16[256,256]{1,0:T(8,128)(2,1)S(1)}, u32[]{:S(2)}, u32[]{:S(2)}) collective-permute-start(bf16[256,256]{1,0:T(8,128)(2,1)S(1)} %bitcast.15), channel_id=1, source_target_pairs={{0,4},{1,5},{2,6},{3,7},{4,0},{5,1},{6,2},{7,3},{8,12},{9,13},{10,... | collective-permute-start | bytes 393224 | tf_op jit(solution)/shard_map/ppermute | solution.py:356
  21.8 5.7 %collective-permute-start.9 = (f32[256,256]{1,0:T(8,128)S(1)}, f32[256,256]{1,0:T(8,128)S(1)}, u32[]{:S(2)}, u32[]{:S(2)}) collective-permute-start(f32[256,256]{1,0:T(8,128)S(1)} %get-tuple-element.56), channel_id=1, source_target_pairs={{0,1},{1,0},{2,3},{3,2},{4,5},{5,4},{6,7},{7,6},{8,9},{9,8},{10,11... | collective-permute-start | bytes 786440 | tf_op jit(solution)/shard_map/ppermute | solution.py:359
  21.9 6.3 %collective-permute-start.10 = (bf16[64,256]{1,0:T(8,128)(2,1)S(1)}, bf16[64,256]{1,0:T(8,128)(2,1)S(1)}, u32[]{:S(2)}, u32[]{:S(2)}) collective-permute-start(bf16[64,256]{1,0:T(8,128)(2,1)S(1)} %get-tuple-element.60), channel_id=1, source_target_pairs={{0,8},{8,16},{16,24},{24,0},{1,9},{9,17},{17,25},{25,1},{2,10},{10... | collective-permute-start | bytes 98312 | tf_op jit(solution)/shard_map/ppermute | solution.py:423
  23.5 5.2 %collective-permute-start.11 = (bf16[64,256]{1,0:T(8,128)(2,1)S(1)}, bf16[64,256]{1,0:T(8,128)(2,1)S(1)}, u32[]{:S(2)}, u32[]{:S(2)}) collective-permute-start(bf16[64,256]{1,0:T(8,128)(2,1)S(1)} %get-tuple-element.61), channel_id=1, source_target_pairs={{0,16},{8,24},{16,0},{24,8},{1,17},{9,25},{17,1},{25,9},{2,18},{10... | collective-permute-start | bytes 98312 | tf_op jit(solution)/shard_map/ppermute | solution.py:423
  26.1 3.9 %collective-permute-start.12 = (bf16[64,256]{1,0:T(8,128)(2,1)S(1)}, bf16[64,256]{1,0:T(8,128)(2,1)S(1)}, u32[]{:S(2)}, u32[]{:S(2)}) collective-permute-start(bf16[64,256]{1,0:T(8,128)(2,1)S(1)} %get-tuple-element.62), channel_id=1, source_target_pairs={{0,24},{8,0},{16,8},{24,16},{1,25},{9,1},{17,9},{25,17},{2,26},{10... | collective-permute-start | bytes 98312 | tf_op jit(solution)/shard_map/ppermute | solution.py:423

commit v7 on v6

--- a/solution.py
+++ b/solution.py
@@ -262,7 +262,7 @@
 
 
 def next_of(share, member, away):
-    line = list(range(share))
+    line = [i ^ i >> 1 for i in range(share)]
     return line[(line.index(member) + away) % share]
 
 

time: 30.9 us -> 30.7 us (level)
  no operation moved by 1% of the time
where the time goes in v7:
time: 30.7 us; the launch traced here: 30.5 us
  starting transfers between devices  16.4 us (53%)
  waiting for transfers between devices  8.85 us (29%)
  Pallas kernels  4.15 us (14%)
  between operations  0.79 us (3%)
    ppermute x6, starting transfers between devices, trade(): return lax.ppermute(block, 'srv', pairs)  10 us
    ppermute x6, waiting for transfers between devices, trade(): return lax.ppermute(block, 'srv', pairs)  6.08 us
    ppermute x3, starting transfers between devices, on_device(): lax.ppermute(part, 'grp', [(i, i // share * share + next_of(share, i % sh...  5.69 us
    pallas_call x16, Pallas kernels, call(): pl.pallas_call(kernel, out_shape=out_shape, in_specs=kinds, out_specs=res...  4.15 us
    ppermute x3, waiting for transfers between devices, on_device(): lax.ppermute(part, 'grp', [(i, i // share * share + next_of(share, i % sh...  1.56 us
    ppermute x4, waiting for transfers between devices, swap(): return lax.ppermute(block, 'srv', [(i, i ^ 1) for i in range(srv)])  1.2 us
    ppermute x4, starting transfers between devices, swap(): return lax.ppermute(block, 'srv', [(i, i ^ 1) for i in range(srv)])  0.74 us
  transfers between devices with their start and end apart: 13, of which 7 were waited for; matrix products, arithmetic and copies ran while one was open for 0% of the time, Pallas kernels for 11%

profile of v7, /device:TPU:0, one launch (start us, length us, event | category | flops | bytes accessed | tf_op | source)
XLA Modules:
  0.0 30.5 jit_solution(8509749925033951775)
XLA Ops:
  0.7 0.5 %collective-permute-start = (bf16[256,256]{1,0:T(8,128)(2,1)}, bf16[256,256]{1,0:T(8,128)(2,1)S(1)}, u32[]{:S(2)}, u32[]{:S(2)}) collective-permute-start(bf16[256,256]{1,0:T(8,128)(2,1)} %q_own.1), channel_id=1, source_target_pairs={{0,1},{1,0},{2,3},{3,2},{4,5},{5,4},{6,7},{7,6},{8,9},{9,8},{10,11... | collective-permute-start | bytes 393224 | tf_op jit(solution)/shard_map/ppermute | solution.py:359
  1.2 0.1 collective-permute-start.1
  1.3 0.2 copy-done.3
  1.5 0.0 copy-done.2
  1.5 0.5 %collective-permute-start.2 = (bf16[256,256]{1,0:T(8,128)(2,1)S(1)}, bf16[256,256]{1,0:T(8,128)(2,1)S(1)}, u32[]{:S(2)}, u32[]{:S(2)}) collective-permute-start(bf16[256,256]{1,0:T(8,128)(2,1)S(1)} %shard_map.79.kv_ref), channel_id=1, source_target_pairs={{1,7},{7,6},{6,2},{2,4},{4,0},{0,1},{3,5},{5,3},{9,15},{15,14},{14... | collective-permute-start | bytes 393224 | tf_op jit(solution)/shard_map/ppermute | solution.py:356
  2.0 4.0 %collective-permute-start.3 = (bf16[256,256]{1,0:T(8,128)(2,1)S(1)}, bf16[256,256]{1,0:T(8,128)(2,1)S(1)}, u32[]{:S(2)}, u32[]{:S(2)}) collective-permute-start(bf16[256,256]{1,0:T(8,128)(2,1)S(1)} %shard_map.79.kv_ref), channel_id=1, source_target_pairs={{0,2},{1,3},{2,0},{3,1},{4,6},{5,7},{6,4},{7,5},{8,10},{9,11},{10,... | collective-permute-start | bytes 393224 | tf_op jit(solution)/shard_map/ppermute | solution.py:356
  6.0 0.5 %collective-permute-start.4 = (bf16[256,256]{1,0:T(8,128)(2,1)S(1)}, bf16[256,256]{1,0:T(8,128)(2,1)S(1)}, u32[]{:S(2)}, u32[]{:S(2)}) collective-permute-start(bf16[256,256]{1,0:T(8,128)(2,1)S(1)} %shard_map.79.kv_ref), channel_id=1, source_target_pairs={{0,4},{1,5},{2,6},{3,7},{4,0},{5,1},{6,2},{7,3},{8,12},{9,13},{10,... | collective-permute-start | bytes 393224 | tf_op jit(solution)/shard_map/ppermute | solution.py:356
  6.6 0.2 shard_map.76
  6.7 0.0 collective-permute-done.q_par
  6.8 0.2 shard_map.77
  7.0 0.8 %shard_map.80.stats_in = f32[8,1024]{1,0:T(8,128)S(1)} custom-call(bf16[4,256,128]{2,1,0:T(8,128)(2,1)S(1)} %get-tuple-element.34.khot_ref, bf16[128,512]{1,0:T(8,128)(2,1)S(1)} %get-tuple-element.35.rhot_ref, bf16[256,512]{1,0:T(8,128)(2,1)S(1)} %get-tuple-element.36.qd_own, bf16[256,512]{1,0:T(8,128)(2,1)S(1)} %get-tuple-element.37.qd_par, ...), custom_call_target="tpu_custom_call" | custom-call | bytes 524288 | tf_op jit(solution)/shard_map/pallas_call | solution.py:312
  7.8 4.3 %collective-permute-done.3 = bf16[256,256]{1,0:T(8,128)(2,1)S(1)} collective-permute-done((bf16[256,256]{1,0:T(8,128)(2,1)S(1)}, bf16[256,256]{1,0:T(8,128)(2,1)S(1)}, u32[]{:S(2)}, u32[]{:S(2)}) %collective-permute-start.3) | collective-permute-done | bytes 131104 | tf_op jit(solution)/shard_map/ppermute | solution.py:356
  12.1 0.1 collective-permute-start.5
  12.2 1.2 %collective-permute-done.5.other_ref = f32[8,1024]{1,0:T(8,128)S(1)} collective-permute-done((f32[8,1024]{1,0:T(8,128)S(1)}, f32[8,1024]{1,0:T(8,128)S(1)}, u32[]{:S(2)}, u32[]{:S(2)}) %collective-permute-start.5) | collective-permute-done | bytes 32800 | tf_op jit(solution)/shard_map/ppermute | solution.py:359
  13.4 0.1 shard_map.85
  13.5 2.9 %collective-permute-start.6 = (bf16[256,256]{1,0:T(8,128)(2,1)S(1)}, bf16[256,256]{1,0:T(8,128)(2,1)S(1)}, u32[]{:S(2)}, u32[]{:S(2)}) collective-permute-start(bf16[256,256]{1,0:T(8,128)(2,1)S(1)} %bitcast.14), channel_id=1, source_target_pairs={{4,2},{5,3},{7,1},{6,5},{0,4},{1,0},{2,6},{3,7},{12,10},{13,11},{1... | collective-permute-start | bytes 393224 | tf_op jit(solution)/shard_map/ppermute | solution.py:356
  16.4 0.1 shard_map.87
  16.5 0.1 collective-permute-start.8
  16.6 2.0 %collective-permute-start.7 = (bf16[256,256]{1,0:T(8,128)(2,1)S(1)}, bf16[256,256]{1,0:T(8,128)(2,1)S(1)}, u32[]{:S(2)}, u32[]{:S(2)}) collective-permute-start(bf16[256,256]{1,0:T(8,128)(2,1)S(1)} %bitcast.15), channel_id=1, source_target_pairs={{0,4},{1,5},{2,6},{3,7},{4,0},{5,1},{6,2},{7,3},{8,12},{9,13},{10,... | collective-permute-start | bytes 393224 | tf_op jit(solution)/shard_map/ppermute | solution.py:356
  18.6 1.3 %shard_map.88 = (f32[256,256]{1,0:T(8,128)S(1)}, f32[256,256]{1,0:T(8,128)S(1)}, f32[256,256]{1,0:T(8,128)S(1)}) custom-call(bf16[4,256,128]{2,1,0:T(8,128)(2,1)S(1)} %get-tuple-element.34.khot_ref, bf16[128,512]{1,0:T(8,128)(2,1)S(1)} %get-tuple-element.35.rhot_ref, bf16[256,512]{1,0:T(8,128)(2,1)S(1)} %get-tuple-element.36.qd_own, ...), custom_call_target="tpu_custom_call" | custom-call | flops 4000000000 | bytes 524288 | tf_op jit(solution)/shard_map/pallas_call | solution.py:312
  19.9 0.1 collective-permute-done.6.rest_0_
  20.0 1.6 %collective-permute-done.8.rest_2_ = bf16[256,256]{1,0:T(8,128)(2,1)S(1)} collective-permute-done((bf16[256,256]{1,0:T(8,128)(2,1)S(1)}, bf16[256,256]{1,0:T(8,128)(2,1)S(1)}, u32[]{:S(2)}, u32[]{:S(2)}) %collective-permute-start.8) | collective-permute-done | bytes 131104 | tf_op jit(solution)/shard_map/ppermute | solution.py:356
  21.5 0.1 collective-permute-done.7.rest_1_
  21.7 0.1 shard_map.89
  21.8 0.1 collective-permute-start.9
  21.9 1.6 %collective-permute-start.10 = (bf16[64,256]{1,0:T(8,128)(2,1)S(1)}, bf16[64,256]{1,0:T(8,128)(2,1)S(1)}, u32[]{:S(2)}, u32[]{:S(2)}) collective-permute-start(bf16[64,256]{1,0:T(8,128)(2,1)S(1)} %get-tuple-element.60), channel_id=1, source_target_pairs={{0,8},{8,24},{16,0},{24,16},{1,9},{9,25},{17,1},{25,17},{2,10},{10... | collective-permute-start | bytes 98312 | tf_op jit(solution)/shard_map/ppermute | solution.py:423
  23.5 2.5 %collective-permute-start.11 = (bf16[64,256]{1,0:T(8,128)(2,1)S(1)}, bf16[64,256]{1,0:T(8,128)(2,1)S(1)}, u32[]{:S(2)}, u32[]{:S(2)}) collective-permute-start(bf16[64,256]{1,0:T(8,128)(2,1)S(1)} %get-tuple-element.61), channel_id=1, source_target_pairs={{0,24},{8,16},{16,8},{24,0},{1,25},{9,17},{17,9},{25,1},{2,26},{10... | collective-permute-start | bytes 98312 | tf_op jit(solution)/shard_map/ppermute | solution.py:423
  26.0 1.6 %collective-permute-start.12 = (bf16[64,256]{1,0:T(8,128)(2,1)S(1)}, bf16[64,256]{1,0:T(8,128)(2,1)S(1)}, u32[]{:S(2)}, u32[]{:S(2)}) collective-permute-start(bf16[64,256]{1,0:T(8,128)(2,1)S(1)} %get-tuple-element.62), channel_id=1, source_target_pairs={{0,16},{8,0},{16,24},{24,8},{1,17},{9,1},{17,25},{25,9},{2,18},{10... | collective-permute-start | bytes 98312 | tf_op jit(solution)/shard_map/ppermute | solution.py:423
  27.5 0.8 %shard_map.90 = (bf16[256,256]{1,0:T(8,128)(2,1)}, f32[8,128]{1,0:T(8,128)S(1)}) custom-call(f32[256,256]{1,0:T(8,128)S(1)} %get-tuple-element.50.dq_own, f32[256,256]{1,0:T(8,128)S(1)} %collective-permute-done.9.dq_far), custom_call_target="tpu_custom_call" | custom-call | flops 2000000000 | bytes 524288 | tf_op jit(solution)/shard_map/pallas_call | solution.py:312
  28.3 0.9 %collective-permute-done.11.rest_1_ = bf16[64,256]{1,0:T(8,128)(2,1)S(1)} collective-permute-done((bf16[64,256]{1,0:T(8,128)(2,1)S(1)}, bf16[64,256]{1,0:T(8,128)(2,1)S(1)}, u32[]{:S(2)}, u32[]{:S(2)}) %collective-permute-start.11) | collective-permute-done | bytes 32800 | tf_op jit(solution)/shard_map/ppermute | solution.py:423
  29.2 0.6 %collective-permute-done.12.rest_2_ = bf16[64,256]{1,0:T(8,128)(2,1)S(1)} collective-permute-done((bf16[64,256]{1,0:T(8,128)(2,1)S(1)}, bf16[64,256]{1,0:T(8,128)(2,1)S(1)}, u32[]{:S(2)}, u32[]{:S(2)}) %collective-permute-start.12) | collective-permute-done | bytes 32800 | tf_op jit(solution)/shard_map/ppermute | solution.py:423
  29.9 0.6 %shard_map.91 = (bf16[32,256]{1,0:T(8,128)(2,1)}, bf16[32,256]{1,0:T(8,128)(2,1)}) custom-call(f32[8,128]{1,0:T(8,128)S(1)} %get-tuple-element.58.after_ref, f32[64,256]{1,0:T(8,128)S(1)} %get-tuple-element.59.keep_ref, bf16[64,256]{1,0:T(8,128)(2,1)S(1)} %collective-permute-done.10.rest_0_, bf16[64,256]{1,0:T(8,128)(2,1)S(1)} %collective-permute-done.11.rest_1_, ...), custom_call_target="tpu_custom_call" | custom-call | bytes 524288 | tf_op jit(solution)/shard_map/pallas_call | solution.py:312
  (21 shorter events, 0.2 us)
Async XLA Ops:
  0.6 0.8 %copy-start.3 = (bf16[256,128]{1,0:T(8,128)(2,1)S(1)}, bf16[256,128]{1,0:T(8,128)(2,1)}, u32[]{:S(2)}) copy-start(bf16[256,128]{1,0:T(8,128)(2,1)} %value_ref.1) | copy-start | bytes 196612
  0.6 0.9 %copy-start.2 = (bf16[256,128]{1,0:T(8,128)(2,1)S(1)}, bf16[256,128]{1,0:T(8,128)(2,1)}, u32[]{:S(2)}) copy-start(bf16[256,128]{1,0:T(8,128)(2,1)} %key_ref.1) | copy-start | bytes 196612
  0.7 6.1 %collective-permute-start = (bf16[256,256]{1,0:T(8,128)(2,1)}, bf16[256,256]{1,0:T(8,128)(2,1)S(1)}, u32[]{:S(2)}, u32[]{:S(2)}) collective-permute-start(bf16[256,256]{1,0:T(8,128)(2,1)} %q_own.1), channel_id=1, source_target_pairs={{0,1},{1,0},{2,3},{3,2},{4,5},{5,4},{6,7},{7,6},{8,9},{9,8},{10,11... | collective-permute-start | bytes 393224 | tf_op jit(solution)/shard_map/ppermute | solution.py:359
  1.2 5.6 %collective-permute-start.1 = (bf16[256,256]{1,0:T(8,128)(2,1)}, bf16[256,256]{1,0:T(8,128)(2,1)S(1)}, u32[]{:S(2)}, u32[]{:S(2)}) collective-permute-start(bf16[256,256]{1,0:T(8,128)(2,1)} %do_own.1), channel_id=1, source_target_pairs={{0,1},{1,0},{2,3},{3,2},{4,5},{5,4},{6,7},{7,6},{8,9},{9,8},{10,11... | collective-permute-start | bytes 393224 | tf_op jit(solution)/shard_map/ppermute | solution.py:359
  1.5 5.1 %copy-start.4 = (s32[2048]{0:T(1024)S(1)}, s32[2048]{0:T(1024)}, u32[]{:S(2)}) copy-start(s32[2048]{0:T(1024)} %param.9) | copy-start | bytes 24580
  1.5 5.2 %copy-start = (bf16[256,256]{1,0:T(8,128)(2,1)S(1)}, bf16[256,256]{1,0:T(8,128)(2,1)}, u32[]{:S(2)}) copy-start(bf16[256,256]{1,0:T(8,128)(2,1)} %q_own.1) | copy-start | bytes 393220
  1.5 5.3 %copy-start.1 = (bf16[256,256]{1,0:T(8,128)(2,1)S(1)}, bf16[256,256]{1,0:T(8,128)(2,1)}, u32[]{:S(2)}) copy-start(bf16[256,256]{1,0:T(8,128)(2,1)} %do_own.1) | copy-start | bytes 393220
  1.5 6.2 %collective-permute-start.2 = (bf16[256,256]{1,0:T(8,128)(2,1)S(1)}, bf16[256,256]{1,0:T(8,128)(2,1)S(1)}, u32[]{:S(2)}, u32[]{:S(2)}) collective-permute-start(bf16[256,256]{1,0:T(8,128)(2,1)S(1)} %shard_map.79.kv_ref), channel_id=1, source_target_pairs={{1,7},{7,6},{6,2},{2,4},{4,0},{0,1},{3,5},{5,3},{9,15},{15,14},{14... | collective-permute-start | bytes 393224 | tf_op jit(solution)/shard_map/ppermute | solution.py:356
  2.0 10.0 %collective-permute-start.3 = (bf16[256,256]{1,0:T(8,128)(2,1)S(1)}, bf16[256,256]{1,0:T(8,128)(2,1)S(1)}, u32[]{:S(2)}, u32[]{:S(2)}) collective-permute-start(bf16[256,256]{1,0:T(8,128)(2,1)S(1)} %shard_map.79.kv_ref), channel_id=1, source_target_pairs={{0,2},{1,3},{2,0},{3,1},{4,6},{5,7},{6,4},{7,5},{8,10},{9,11},{10,... | collective-permute-start | bytes 393224 | tf_op jit(solution)/shard_map/ppermute | solution.py:356
  6.0 6.0 %collective-permute-start.4 = (bf16[256,256]{1,0:T(8,128)(2,1)S(1)}, bf16[256,256]{1,0:T(8,128)(2,1)S(1)}, u32[]{:S(2)}, u32[]{:S(2)}) collective-permute-start(bf16[256,256]{1,0:T(8,128)(2,1)S(1)} %shard_map.79.kv_ref), channel_id=1, source_target_pairs={{0,4},{1,5},{2,6},{3,7},{4,0},{5,1},{6,2},{7,3},{8,12},{9,13},{10,... | collective-permute-start | bytes 393224 | tf_op jit(solution)/shard_map/ppermute | solution.py:356
  12.1 1.3 %collective-permute-start.5 = (f32[8,1024]{1,0:T(8,128)S(1)}, f32[8,1024]{1,0:T(8,128)S(1)}, u32[]{:S(2)}, u32[]{:S(2)}) collective-permute-start(f32[8,1024]{1,0:T(8,128)S(1)} %get-tuple-element.40.stats_ref.rest_0_), channel_id=1, source_target_pairs={{0,1},{1,0},{2,3},{3,2},{4,5},{5,4},{6,7},{7,6},{8,9},{9,8},{10,11... | collective-permute-start | bytes 98312 | tf_op jit(solution)/shard_map/ppermute | solution.py:359
  13.5 6.5 %collective-permute-start.6 = (bf16[256,256]{1,0:T(8,128)(2,1)S(1)}, bf16[256,256]{1,0:T(8,128)(2,1)S(1)}, u32[]{:S(2)}, u32[]{:S(2)}) collective-permute-start(bf16[256,256]{1,0:T(8,128)(2,1)S(1)} %bitcast.14), channel_id=1, source_target_pairs={{4,2},{5,3},{7,1},{6,5},{0,4},{1,0},{2,6},{3,7},{12,10},{13,11},{1... | collective-permute-start | bytes 393224 | tf_op jit(solution)/shard_map/ppermute | solution.py:356
  16.5 5.0 %collective-permute-start.8 = (bf16[256,256]{1,0:T(8,128)(2,1)S(1)}, bf16[256,256]{1,0:T(8,128)(2,1)S(1)}, u32[]{:S(2)}, u32[]{:S(2)}) collective-permute-start(bf16[256,256]{1,0:T(8,128)(2,1)S(1)} %bitcast.16), channel_id=1, source_target_pairs={{0,2},{1,3},{2,0},{3,1},{4,6},{5,7},{6,4},{7,5},{8,10},{9,11},{10,... | collective-permute-start | bytes 393224 | tf_op jit(solution)/shard_map/ppermute | solution.py:356
  16.6 5.1 %collective-permute-start.7 = (bf16[256,256]{1,0:T(8,128)(2,1)S(1)}, bf16[256,256]{1,0:T(8,128)(2,1)S(1)}, u32[]{:S(2)}, u32[]{:S(2)}) collective-permute-start(bf16[256,256]{1,0:T(8,128)(2,1)S(1)} %bitcast.15), channel_id=1, source_target_pairs={{0,4},{1,5},{2,6},{3,7},{4,0},{5,1},{6,2},{7,3},{8,12},{9,13},{10,... | collective-permute-start | bytes 393224 | tf_op jit(solution)/shard_map/ppermute | solution.py:356
  21.8 5.8 %collective-permute-start.9 = (f32[256,256]{1,0:T(8,128)S(1)}, f32[256,256]{1,0:T(8,128)S(1)}, u32[]{:S(2)}, u32[]{:S(2)}) collective-permute-start(f32[256,256]{1,0:T(8,128)S(1)} %get-tuple-element.56), channel_id=1, source_target_pairs={{0,1},{1,0},{2,3},{3,2},{4,5},{5,4},{6,7},{7,6},{8,9},{9,8},{10,11... | collective-permute-start | bytes 786440 | tf_op jit(solution)/shard_map/ppermute | solution.py:359
  21.9 6.5 %collective-permute-start.10 = (bf16[64,256]{1,0:T(8,128)(2,1)S(1)}, bf16[64,256]{1,0:T(8,128)(2,1)S(1)}, u32[]{:S(2)}, u32[]{:S(2)}) collective-permute-start(bf16[64,256]{1,0:T(8,128)(2,1)S(1)} %get-tuple-element.60), channel_id=1, source_target_pairs={{0,8},{8,24},{16,0},{24,16},{1,9},{9,25},{17,1},{25,17},{2,10},{10... | collective-permute-start | bytes 98312 | tf_op jit(solution)/shard_map/ppermute | solution.py:423
  23.5 5.7 %collective-permute-start.11 = (bf16[64,256]{1,0:T(8,128)(2,1)S(1)}, bf16[64,256]{1,0:T(8,128)(2,1)S(1)}, u32[]{:S(2)}, u32[]{:S(2)}) collective-permute-start(bf16[64,256]{1,0:T(8,128)(2,1)S(1)} %get-tuple-element.61), channel_id=1, source_target_pairs={{0,24},{8,16},{16,8},{24,0},{1,25},{9,17},{17,9},{25,1},{2,26},{10... | collective-permute-start | bytes 98312 | tf_op jit(solution)/shard_map/ppermute | solution.py:423
  26.0 3.9 %collective-permute-start.12 = (bf16[64,256]{1,0:T(8,128)(2,1)S(1)}, bf16[64,256]{1,0:T(8,128)(2,1)S(1)}, u32[]{:S(2)}, u32[]{:S(2)}) collective-permute-start(bf16[64,256]{1,0:T(8,128)(2,1)S(1)} %get-tuple-element.62), channel_id=1, source_target_pairs={{0,16},{8,0},{16,24},{24,8},{1,17},{9,1},{17,25},{25,9},{2,18},{10... | collective-permute-start | bytes 98312 | tf_op jit(solution)/shard_map/ppermute | solution.py:423

commit v8 on v7

--- a/solution.py
+++ b/solution.py
@@ -352,7 +352,7 @@
     def trade(block, away, back=False):
         pairs = [(i, i ^ 2 * away) for i in range(srv)]
         if srv == 8 and away == 3 and apart:
-            pairs = [(4, 2), (5, 3), (7, 1), (6, 5), (0, 4), (1, 0), (2, 6), (3, 7)] if back else CORNER
+            pairs = [(4, 2), (5, 3), (7, 1), (6, 7), (0, 4), (1, 5), (2, 6), (3, 0)] if back else CORNER
         return lax.ppermute(block, "srv", pairs)
 
     def swap(block):

time: 30.7 us -> 31 us (level)
  waiting for transfers between devices: 8.85 us -> 10.1 us
  starting transfers between devices: 16.4 us -> 15.5 us
    ppermute x6, waiting for transfers between devices: 6.08 us -> 7.29 us  [trade(): return lax.ppermute(block, 'srv', pairs)]
    ppermute x6, starting transfers between devices: 10 us -> 9.1 us  [trade(): return lax.ppermute(block, 'srv', pairs)]
where the time goes in v8:
time: 31 us; the launch traced here: 30.8 us
  starting transfers between devices  15.5 us (50%)
  waiting for transfers between devices  10.1 us (33%)
  Pallas kernels  4.15 us (13%)
  between operations  0.79 us (3%)
    ppermute x6, starting transfers between devices, trade(): return lax.ppermute(block, 'srv', pairs)  9.1 us
    ppermute x6, waiting for transfers between devices, trade(): return lax.ppermute(block, 'srv', pairs)  7.29 us
    ppermute x3, starting transfers between devices, on_device(): lax.ppermute(part, 'grp', [(i, i // share * share + next_of(share, i % sh...  5.68 us
    pallas_call x16, Pallas kernels, call(): pl.pallas_call(kernel, out_shape=out_shape, in_specs=kinds, out_specs=res...  4.15 us
    ppermute x3, waiting for transfers between devices, on_device(): lax.ppermute(part, 'grp', [(i, i // share * share + next_of(share, i % sh...  1.57 us
    ppermute x4, waiting for transfers between devices, swap(): return lax.ppermute(block, 'srv', [(i, i ^ 1) for i in range(srv)])  1.2 us
    ppermute x4, starting transfers between devices, swap(): return lax.ppermute(block, 'srv', [(i, i ^ 1) for i in range(srv)])  0.74 us
  transfers between devices with their start and end apart: 13, of which 7 were waited for; matrix products, arithmetic and copies ran while one was open for 0% of the time, Pallas kernels for 11%

profile of v8, /device:TPU:0, one launch (start us, length us, event | category | flops | bytes accessed | tf_op | source)
XLA Modules:
  0.0 30.8 jit_solution(2115340499312723868)
XLA Ops:
  0.7 0.5 %collective-permute-start = (bf16[256,256]{1,0:T(8,128)(2,1)}, bf16[256,256]{1,0:T(8,128)(2,1)S(1)}, u32[]{:S(2)}, u32[]{:S(2)}) collective-permute-start(bf16[256,256]{1,0:T(8,128)(2,1)} %q_own.1), channel_id=1, source_target_pairs={{0,1},{1,0},{2,3},{3,2},{4,5},{5,4},{6,7},{7,6},{8,9},{9,8},{10,11... | collective-permute-start | bytes 393224 | tf_op jit(solution)/shard_map/ppermute | solution.py:359
  1.2 0.1 collective-permute-start.1
  1.3 0.2 copy-done.3
  1.5 0.0 copy-done.2
  1.5 0.5 %collective-permute-start.2 = (bf16[256,256]{1,0:T(8,128)(2,1)S(1)}, bf16[256,256]{1,0:T(8,128)(2,1)S(1)}, u32[]{:S(2)}, u32[]{:S(2)}) collective-permute-start(bf16[256,256]{1,0:T(8,128)(2,1)S(1)} %shard_map.79.kv_ref), channel_id=1, source_target_pairs={{1,7},{7,6},{6,2},{2,4},{4,0},{0,1},{3,5},{5,3},{9,15},{15,14},{14... | collective-permute-start | bytes 393224 | tf_op jit(solution)/shard_map/ppermute | solution.py:356
  2.0 4.0 %collective-permute-start.3 = (bf16[256,256]{1,0:T(8,128)(2,1)S(1)}, bf16[256,256]{1,0:T(8,128)(2,1)S(1)}, u32[]{:S(2)}, u32[]{:S(2)}) collective-permute-start(bf16[256,256]{1,0:T(8,128)(2,1)S(1)} %shard_map.79.kv_ref), channel_id=1, source_target_pairs={{0,2},{1,3},{2,0},{3,1},{4,6},{5,7},{6,4},{7,5},{8,10},{9,11},{10,... | collective-permute-start | bytes 393224 | tf_op jit(solution)/shard_map/ppermute | solution.py:356
  6.0 0.5 %collective-permute-start.4 = (bf16[256,256]{1,0:T(8,128)(2,1)S(1)}, bf16[256,256]{1,0:T(8,128)(2,1)S(1)}, u32[]{:S(2)}, u32[]{:S(2)}) collective-permute-start(bf16[256,256]{1,0:T(8,128)(2,1)S(1)} %shard_map.79.kv_ref), channel_id=1, source_target_pairs={{0,4},{1,5},{2,6},{3,7},{4,0},{5,1},{6,2},{7,3},{8,12},{9,13},{10,... | collective-permute-start | bytes 393224 | tf_op jit(solution)/shard_map/ppermute | solution.py:356
  6.6 0.2 shard_map.76
  6.7 0.0 collective-permute-done.q_par
  6.8 0.2 shard_map.77
  7.0 0.8 %shard_map.80.stats_in = f32[8,1024]{1,0:T(8,128)S(1)} custom-call(bf16[4,256,128]{2,1,0:T(8,128)(2,1)S(1)} %get-tuple-element.34.khot_ref, bf16[128,512]{1,0:T(8,128)(2,1)S(1)} %get-tuple-element.35.rhot_ref, bf16[256,512]{1,0:T(8,128)(2,1)S(1)} %get-tuple-element.36.qd_own, bf16[256,512]{1,0:T(8,128)(2,1)S(1)} %get-tuple-element.37.qd_par, ...), custom_call_target="tpu_custom_call" | custom-call | bytes 524288 | tf_op jit(solution)/shard_map/pallas_call | solution.py:312
  7.8 4.3 %collective-permute-done.3 = bf16[256,256]{1,0:T(8,128)(2,1)S(1)} collective-permute-done((bf16[256,256]{1,0:T(8,128)(2,1)S(1)}, bf16[256,256]{1,0:T(8,128)(2,1)S(1)}, u32[]{:S(2)}, u32[]{:S(2)}) %collective-permute-start.3) | collective-permute-done | bytes 131104 | tf_op jit(solution)/shard_map/ppermute | solution.py:356
  12.1 0.1 collective-permute-start.5
  12.2 1.2 %collective-permute-done.5.other_ref = f32[8,1024]{1,0:T(8,128)S(1)} collective-permute-done((f32[8,1024]{1,0:T(8,128)S(1)}, f32[8,1024]{1,0:T(8,128)S(1)}, u32[]{:S(2)}, u32[]{:S(2)}) %collective-permute-start.5) | collective-permute-done | bytes 32800 | tf_op jit(solution)/shard_map/ppermute | solution.py:359
  13.4 0.1 shard_map.85
  13.5 2.4 %collective-permute-start.6 = (bf16[256,256]{1,0:T(8,128)(2,1)S(1)}, bf16[256,256]{1,0:T(8,128)(2,1)S(1)}, u32[]{:S(2)}, u32[]{:S(2)}) collective-permute-start(bf16[256,256]{1,0:T(8,128)(2,1)S(1)} %bitcast.14), channel_id=1, source_target_pairs={{4,2},{5,3},{7,1},{6,7},{0,4},{1,5},{2,6},{3,0},{12,10},{13,11},{1... | collective-permute-start | bytes 393224 | tf_op jit(solution)/shard_map/ppermute | solution.py:356
  15.9 0.1 shard_map.87
  16.0 0.2 collective-permute-start.8
  16.1 1.5 %collective-permute-start.7 = (bf16[256,256]{1,0:T(8,128)(2,1)S(1)}, bf16[256,256]{1,0:T(8,128)(2,1)S(1)}, u32[]{:S(2)}, u32[]{:S(2)}) collective-permute-start(bf16[256,256]{1,0:T(8,128)(2,1)S(1)} %bitcast.15), channel_id=1, source_target_pairs={{0,4},{1,5},{2,6},{3,7},{4,0},{5,1},{6,2},{7,3},{8,12},{9,13},{10,... | collective-permute-start | bytes 393224 | tf_op jit(solution)/shard_map/ppermute | solution.py:356
  17.7 1.3 %shard_map.88 = (f32[256,256]{1,0:T(8,128)S(1)}, f32[256,256]{1,0:T(8,128)S(1)}, f32[256,256]{1,0:T(8,128)S(1)}) custom-call(bf16[4,256,128]{2,1,0:T(8,128)(2,1)S(1)} %get-tuple-element.34.khot_ref, bf16[128,512]{1,0:T(8,128)(2,1)S(1)} %get-tuple-element.35.rhot_ref, bf16[256,512]{1,0:T(8,128)(2,1)S(1)} %get-tuple-element.36.qd_own, ...), custom_call_target="tpu_custom_call" | custom-call | flops 4000000000 | bytes 524288 | tf_op jit(solution)/shard_map/pallas_call | solution.py:312
  19.0 0.4 %collective-permute-done.6.rest_0_ = bf16[256,256]{1,0:T(8,128)(2,1)S(1)} collective-permute-done((bf16[256,256]{1,0:T(8,128)(2,1)S(1)}, bf16[256,256]{1,0:T(8,128)(2,1)S(1)}, u32[]{:S(2)}, u32[]{:S(2)}) %collective-permute-start.6) | collective-permute-done | bytes 131104 | tf_op jit(solution)/shard_map/ppermute | solution.py:356
  19.3 2.0 %collective-permute-done.8.rest_2_ = bf16[256,256]{1,0:T(8,128)(2,1)S(1)} collective-permute-done((bf16[256,256]{1,0:T(8,128)(2,1)S(1)}, bf16[256,256]{1,0:T(8,128)(2,1)S(1)}, u32[]{:S(2)}, u32[]{:S(2)}) %collective-permute-start.8) | collective-permute-done | bytes 131104 | tf_op jit(solution)/shard_map/ppermute | solution.py:356
  21.3 0.7 %collective-permute-done.7.rest_1_ = bf16[256,256]{1,0:T(8,128)(2,1)S(1)} collective-permute-done((bf16[256,256]{1,0:T(8,128)(2,1)S(1)}, bf16[256,256]{1,0:T(8,128)(2,1)S(1)}, u32[]{:S(2)}, u32[]{:S(2)}) %collective-permute-start.7) | collective-permute-done | bytes 131104 | tf_op jit(solution)/shard_map/ppermute | solution.py:356
  22.0 0.1 shard_map.89
  22.1 0.1 collective-permute-start.9
  22.1 1.6 %collective-permute-start.10 = (bf16[64,256]{1,0:T(8,128)(2,1)S(1)}, bf16[64,256]{1,0:T(8,128)(2,1)S(1)}, u32[]{:S(2)}, u32[]{:S(2)}) collective-permute-start(bf16[64,256]{1,0:T(8,128)(2,1)S(1)} %get-tuple-element.60), channel_id=1, source_target_pairs={{0,8},{8,24},{16,0},{24,16},{1,9},{9,25},{17,1},{25,17},{2,10},{10... | collective-permute-start | bytes 98312 | tf_op jit(solution)/shard_map/ppermute | solution.py:423
  23.8 2.5 %collective-permute-start.11 = (bf16[64,256]{1,0:T(8,128)(2,1)S(1)}, bf16[64,256]{1,0:T(8,128)(2,1)S(1)}, u32[]{:S(2)}, u32[]{:S(2)}) collective-permute-start(bf16[64,256]{1,0:T(8,128)(2,1)S(1)} %get-tuple-element.61), channel_id=1, source_target_pairs={{0,24},{8,16},{16,8},{24,0},{1,25},{9,17},{17,9},{25,1},{2,26},{10... | collective-permute-start | bytes 98312 | tf_op jit(solution)/shard_map/ppermute | solution.py:423
  26.2 1.6 %collective-permute-start.12 = (bf16[64,256]{1,0:T(8,128)(2,1)S(1)}, bf16[64,256]{1,0:T(8,128)(2,1)S(1)}, u32[]{:S(2)}, u32[]{:S(2)}) collective-permute-start(bf16[64,256]{1,0:T(8,128)(2,1)S(1)} %get-tuple-element.62), channel_id=1, source_target_pairs={{0,16},{8,0},{16,24},{24,8},{1,17},{9,1},{17,25},{25,9},{2,18},{10... | collective-permute-start | bytes 98312 | tf_op jit(solution)/shard_map/ppermute | solution.py:423
  27.8 0.8 %shard_map.90 = (bf16[256,256]{1,0:T(8,128)(2,1)}, f32[8,128]{1,0:T(8,128)S(1)}) custom-call(f32[256,256]{1,0:T(8,128)S(1)} %get-tuple-element.50.dq_own, f32[256,256]{1,0:T(8,128)S(1)} %collective-permute-done.9.dq_far), custom_call_target="tpu_custom_call" | custom-call | flops 2000000000 | bytes 524288 | tf_op jit(solution)/shard_map/pallas_call | solution.py:312
  28.6 0.9 %collective-permute-done.11.rest_1_ = bf16[64,256]{1,0:T(8,128)(2,1)S(1)} collective-permute-done((bf16[64,256]{1,0:T(8,128)(2,1)S(1)}, bf16[64,256]{1,0:T(8,128)(2,1)S(1)}, u32[]{:S(2)}, u32[]{:S(2)}) %collective-permute-start.11) | collective-permute-done | bytes 32800 | tf_op jit(solution)/shard_map/ppermute | solution.py:423
  29.5 0.7 %collective-permute-done.12.rest_2_ = bf16[64,256]{1,0:T(8,128)(2,1)S(1)} collective-permute-done((bf16[64,256]{1,0:T(8,128)(2,1)S(1)}, bf16[64,256]{1,0:T(8,128)(2,1)S(1)}, u32[]{:S(2)}, u32[]{:S(2)}) %collective-permute-start.12) | collective-permute-done | bytes 32800 | tf_op jit(solution)/shard_map/ppermute | solution.py:423
  30.2 0.6 %shard_map.91 = (bf16[32,256]{1,0:T(8,128)(2,1)}, bf16[32,256]{1,0:T(8,128)(2,1)}) custom-call(f32[8,128]{1,0:T(8,128)S(1)} %get-tuple-element.58.after_ref, f32[64,256]{1,0:T(8,128)S(1)} %get-tuple-element.59.keep_ref, bf16[64,256]{1,0:T(8,128)(2,1)S(1)} %collective-permute-done.10.rest_0_, bf16[64,256]{1,0:T(8,128)(2,1)S(1)} %collective-permute-done.11.rest_1_, ...), custom_call_target="tpu_custom_call" | custom-call | bytes 524288 | tf_op jit(solution)/shard_map/pallas_call | solution.py:312
  (21 shorter events, 0.2 us)
Async XLA Ops:
  0.6 0.8 %copy-start.3 = (bf16[256,128]{1,0:T(8,128)(2,1)S(1)}, bf16[256,128]{1,0:T(8,128)(2,1)}, u32[]{:S(2)}) copy-start(bf16[256,128]{1,0:T(8,128)(2,1)} %value_ref.1) | copy-start | bytes 196612
  0.6 0.9 %copy-start.2 = (bf16[256,128]{1,0:T(8,128)(2,1)S(1)}, bf16[256,128]{1,0:T(8,128)(2,1)}, u32[]{:S(2)}) copy-start(bf16[256,128]{1,0:T(8,128)(2,1)} %key_ref.1) | copy-start | bytes 196612
  0.7 6.1 %collective-permute-start = (bf16[256,256]{1,0:T(8,128)(2,1)}, bf16[256,256]{1,0:T(8,128)(2,1)S(1)}, u32[]{:S(2)}, u32[]{:S(2)}) collective-permute-start(bf16[256,256]{1,0:T(8,128)(2,1)} %q_own.1), channel_id=1, source_target_pairs={{0,1},{1,0},{2,3},{3,2},{4,5},{5,4},{6,7},{7,6},{8,9},{9,8},{10,11... | collective-permute-start | bytes 393224 | tf_op jit(solution)/shard_map/ppermute | solution.py:359
  1.2 5.6 %collective-permute-start.1 = (bf16[256,256]{1,0:T(8,128)(2,1)}, bf16[256,256]{1,0:T(8,128)(2,1)S(1)}, u32[]{:S(2)}, u32[]{:S(2)}) collective-permute-start(bf16[256,256]{1,0:T(8,128)(2,1)} %do_own.1), channel_id=1, source_target_pairs={{0,1},{1,0},{2,3},{3,2},{4,5},{5,4},{6,7},{7,6},{8,9},{9,8},{10,11... | collective-permute-start | bytes 393224 | tf_op jit(solution)/shard_map/ppermute | solution.py:359
  1.5 5.1 %copy-start.4 = (s32[2048]{0:T(1024)S(1)}, s32[2048]{0:T(1024)}, u32[]{:S(2)}) copy-start(s32[2048]{0:T(1024)} %param.9) | copy-start | bytes 24580
  1.5 5.2 %copy-start = (bf16[256,256]{1,0:T(8,128)(2,1)S(1)}, bf16[256,256]{1,0:T(8,128)(2,1)}, u32[]{:S(2)}) copy-start(bf16[256,256]{1,0:T(8,128)(2,1)} %q_own.1) | copy-start | bytes 393220
  1.5 5.3 %copy-start.1 = (bf16[256,256]{1,0:T(8,128)(2,1)S(1)}, bf16[256,256]{1,0:T(8,128)(2,1)}, u32[]{:S(2)}) copy-start(bf16[256,256]{1,0:T(8,128)(2,1)} %do_own.1) | copy-start | bytes 393220
  1.5 6.2 %collective-permute-start.2 = (bf16[256,256]{1,0:T(8,128)(2,1)S(1)}, bf16[256,256]{1,0:T(8,128)(2,1)S(1)}, u32[]{:S(2)}, u32[]{:S(2)}) collective-permute-start(bf16[256,256]{1,0:T(8,128)(2,1)S(1)} %shard_map.79.kv_ref), channel_id=1, source_target_pairs={{1,7},{7,6},{6,2},{2,4},{4,0},{0,1},{3,5},{5,3},{9,15},{15,14},{14... | collective-permute-start | bytes 393224 | tf_op jit(solution)/shard_map/ppermute | solution.py:356
  2.0 10.0 %collective-permute-start.3 = (bf16[256,256]{1,0:T(8,128)(2,1)S(1)}, bf16[256,256]{1,0:T(8,128)(2,1)S(1)}, u32[]{:S(2)}, u32[]{:S(2)}) collective-permute-start(bf16[256,256]{1,0:T(8,128)(2,1)S(1)} %shard_map.79.kv_ref), channel_id=1, source_target_pairs={{0,2},{1,3},{2,0},{3,1},{4,6},{5,7},{6,4},{7,5},{8,10},{9,11},{10,... | collective-permute-start | bytes 393224 | tf_op jit(solution)/shard_map/ppermute | solution.py:356
  6.0 6.0 %collective-permute-start.4 = (bf16[256,256]{1,0:T(8,128)(2,1)S(1)}, bf16[256,256]{1,0:T(8,128)(2,1)S(1)}, u32[]{:S(2)}, u32[]{:S(2)}) collective-permute-start(bf16[256,256]{1,0:T(8,128)(2,1)S(1)} %shard_map.79.kv_ref), channel_id=1, source_target_pairs={{0,4},{1,5},{2,6},{3,7},{4,0},{5,1},{6,2},{7,3},{8,12},{9,13},{10,... | collective-permute-start | bytes 393224 | tf_op jit(solution)/shard_map/ppermute | solution.py:356
  12.1 1.3 %collective-permute-start.5 = (f32[8,1024]{1,0:T(8,128)S(1)}, f32[8,1024]{1,0:T(8,128)S(1)}, u32[]{:S(2)}, u32[]{:S(2)}) collective-permute-start(f32[8,1024]{1,0:T(8,128)S(1)} %get-tuple-element.40.stats_ref.rest_0_), channel_id=1, source_target_pairs={{0,1},{1,0},{2,3},{3,2},{4,5},{5,4},{6,7},{7,6},{8,9},{9,8},{10,11... | collective-permute-start | bytes 98312 | tf_op jit(solution)/shard_map/ppermute | solution.py:359
  13.5 5.9 %collective-permute-start.6 = (bf16[256,256]{1,0:T(8,128)(2,1)S(1)}, bf16[256,256]{1,0:T(8,128)(2,1)S(1)}, u32[]{:S(2)}, u32[]{:S(2)}) collective-permute-start(bf16[256,256]{1,0:T(8,128)(2,1)S(1)} %bitcast.14), channel_id=1, source_target_pairs={{4,2},{5,3},{7,1},{6,7},{0,4},{1,5},{2,6},{3,0},{12,10},{13,11},{1... | collective-permute-start | bytes 393224 | tf_op jit(solution)/shard_map/ppermute | solution.py:356
  16.0 5.3 %collective-permute-start.8 = (bf16[256,256]{1,0:T(8,128)(2,1)S(1)}, bf16[256,256]{1,0:T(8,128)(2,1)S(1)}, u32[]{:S(2)}, u32[]{:S(2)}) collective-permute-start(bf16[256,256]{1,0:T(8,128)(2,1)S(1)} %bitcast.16), channel_id=1, source_target_pairs={{0,2},{1,3},{2,0},{3,1},{4,6},{5,7},{6,4},{7,5},{8,10},{9,11},{10,... | collective-permute-start | bytes 393224 | tf_op jit(solution)/shard_map/ppermute | solution.py:356
  16.1 5.8 %collective-permute-start.7 = (bf16[256,256]{1,0:T(8,128)(2,1)S(1)}, bf16[256,256]{1,0:T(8,128)(2,1)S(1)}, u32[]{:S(2)}, u32[]{:S(2)}) collective-permute-start(bf16[256,256]{1,0:T(8,128)(2,1)S(1)} %bitcast.15), channel_id=1, source_target_pairs={{0,4},{1,5},{2,6},{3,7},{4,0},{5,1},{6,2},{7,3},{8,12},{9,13},{10,... | collective-permute-start | bytes 393224 | tf_op jit(solution)/shard_map/ppermute | solution.py:356
  22.1 5.8 %collective-permute-start.9 = (f32[256,256]{1,0:T(8,128)S(1)}, f32[256,256]{1,0:T(8,128)S(1)}, u32[]{:S(2)}, u32[]{:S(2)}) collective-permute-start(f32[256,256]{1,0:T(8,128)S(1)} %get-tuple-element.56), channel_id=1, source_target_pairs={{0,1},{1,0},{2,3},{3,2},{4,5},{5,4},{6,7},{7,6},{8,9},{9,8},{10,11... | collective-permute-start | bytes 786440 | tf_op jit(solution)/shard_map/ppermute | solution.py:359
  22.1 6.5 %collective-permute-start.10 = (bf16[64,256]{1,0:T(8,128)(2,1)S(1)}, bf16[64,256]{1,0:T(8,128)(2,1)S(1)}, u32[]{:S(2)}, u32[]{:S(2)}) collective-permute-start(bf16[64,256]{1,0:T(8,128)(2,1)S(1)} %get-tuple-element.60), channel_id=1, source_target_pairs={{0,8},{8,24},{16,0},{24,16},{1,9},{9,25},{17,1},{25,17},{2,10},{10... | collective-permute-start | bytes 98312 | tf_op jit(solution)/shard_map/ppermute | solution.py:423
  23.8 5.7 %collective-permute-start.11 = (bf16[64,256]{1,0:T(8,128)(2,1)S(1)}, bf16[64,256]{1,0:T(8,128)(2,1)S(1)}, u32[]{:S(2)}, u32[]{:S(2)}) collective-permute-start(bf16[64,256]{1,0:T(8,128)(2,1)S(1)} %get-tuple-element.61), channel_id=1, source_target_pairs={{0,24},{8,16},{16,8},{24,0},{1,25},{9,17},{17,9},{25,1},{2,26},{10... | collective-permute-start | bytes 98312 | tf_op jit(solution)/shard_map/ppermute | solution.py:423
  26.2 3.9 %collective-permute-start.12 = (bf16[64,256]{1,0:T(8,128)(2,1)S(1)}, bf16[64,256]{1,0:T(8,128)(2,1)S(1)}, u32[]{:S(2)}, u32[]{:S(2)}) collective-permute-start(bf16[64,256]{1,0:T(8,128)(2,1)S(1)} %get-tuple-element.62), channel_id=1, source_target_pairs={{0,16},{8,0},{16,24},{24,8},{1,17},{9,1},{17,25},{25,9},{2,18},{10... | collective-permute-start | bytes 98312 | tf_op jit(solution)/shard_map/ppermute | solution.py:423

commit v9 on v8

--- a/solution.py
+++ b/solution.py
@@ -352,7 +352,7 @@
     def trade(block, away, back=False):
         pairs = [(i, i ^ 2 * away) for i in range(srv)]
         if srv == 8 and away == 3 and apart:
-            pairs = [(4, 2), (5, 3), (7, 1), (6, 7), (0, 4), (1, 5), (2, 6), (3, 0)] if back else CORNER
+            pairs = [(4, 2), (5, 3), (7, 1), (6, 5), (0, 4), (1, 0), (2, 7), (3, 6)] if back else CORNER
         return lax.ppermute(block, "srv", pairs)
 
     def swap(block):

time: 31 us -> 30.7 us (level)
  waiting for transfers between devices: 10.1 us -> 8.85 us
  starting transfers between devices: 15.5 us -> 16.4 us
    ppermute x6, waiting for transfers between devices: 7.29 us -> 6.08 us  [trade(): return lax.ppermute(block, 'srv', pairs)]
    ppermute x6, starting transfers between devices: 9.1 us -> 10 us  [trade(): return lax.ppermute(block, 'srv', pairs)]
where the time goes in v9:
time: 30.7 us; the launch traced here: 30.5 us
  starting transfers between devices  16.4 us (53%)
  waiting for transfers between devices  8.85 us (29%)
  Pallas kernels  4.15 us (14%)
  between operations  0.79 us (3%)
    ppermute x6, starting transfers between devices, trade(): return lax.ppermute(block, 'srv', pairs)  10 us
    ppermute x6, waiting for transfers between devices, trade(): return lax.ppermute(block, 'srv', pairs)  6.08 us
    ppermute x3, starting transfers between devices, on_device(): lax.ppermute(part, 'grp', [(i, i // share * share + next_of(share, i % sh...  5.69 us
    pallas_call x16, Pallas kernels, call(): pl.pallas_call(kernel, out_shape=out_shape, in_specs=kinds, out_specs=res...  4.15 us
    ppermute x3, waiting for transfers between devices, on_device(): lax.ppermute(part, 'grp', [(i, i // share * share + next_of(share, i % sh...  1.56 us
    ppermute x4, waiting for transfers between devices, swap(): return lax.ppermute(block, 'srv', [(i, i ^ 1) for i in range(srv)])  1.2 us
    ppermute x4, starting transfers between devices, swap(): return lax.ppermute(block, 'srv', [(i, i ^ 1) for i in range(srv)])  0.74 us
  transfers between devices with their start and end apart: 13, of which 7 were waited for; matrix products, arithmetic and copies ran while one was open for 0% of the time, Pallas kernels for 11%

profile of v9, /device:TPU:0, one launch (start us, length us, event | category | flops | bytes accessed | tf_op | source)
XLA Modules:
  0.0 30.5 jit_solution(15925605454043177827)
XLA Ops:
  0.7 0.5 %collective-permute-start = (bf16[256,256]{1,0:T(8,128)(2,1)}, bf16[256,256]{1,0:T(8,128)(2,1)S(1)}, u32[]{:S(2)}, u32[]{:S(2)}) collective-permute-start(bf16[256,256]{1,0:T(8,128)(2,1)} %q_own.1), channel_id=1, source_target_pairs={{0,1},{1,0},{2,3},{3,2},{4,5},{5,4},{6,7},{7,6},{8,9},{9,8},{10,11... | collective-permute-start | bytes 393224 | tf_op jit(solution)/shard_map/ppermute | solution.py:359
  1.2 0.1 collective-permute-start.1
  1.3 0.2 copy-done.3
  1.5 0.0 copy-done.2
  1.5 0.5 %collective-permute-start.2 = (bf16[256,256]{1,0:T(8,128)(2,1)S(1)}, bf16[256,256]{1,0:T(8,128)(2,1)S(1)}, u32[]{:S(2)}, u32[]{:S(2)}) collective-permute-start(bf16[256,256]{1,0:T(8,128)(2,1)S(1)} %shard_map.79.kv_ref), channel_id=1, source_target_pairs={{1,7},{7,6},{6,2},{2,4},{4,0},{0,1},{3,5},{5,3},{9,15},{15,14},{14... | collective-permute-start | bytes 393224 | tf_op jit(solution)/shard_map/ppermute | solution.py:356
  2.0 4.0 %collective-permute-start.3 = (bf16[256,256]{1,0:T(8,128)(2,1)S(1)}, bf16[256,256]{1,0:T(8,128)(2,1)S(1)}, u32[]{:S(2)}, u32[]{:S(2)}) collective-permute-start(bf16[256,256]{1,0:T(8,128)(2,1)S(1)} %shard_map.79.kv_ref), channel_id=1, source_target_pairs={{0,2},{1,3},{2,0},{3,1},{4,6},{5,7},{6,4},{7,5},{8,10},{9,11},{10,... | collective-permute-start | bytes 393224 | tf_op jit(solution)/shard_map/ppermute | solution.py:356
  6.0 0.5 %collective-permute-start.4 = (bf16[256,256]{1,0:T(8,128)(2,1)S(1)}, bf16[256,256]{1,0:T(8,128)(2,1)S(1)}, u32[]{:S(2)}, u32[]{:S(2)}) collective-permute-start(bf16[256,256]{1,0:T(8,128)(2,1)S(1)} %shard_map.79.kv_ref), channel_id=1, source_target_pairs={{0,4},{1,5},{2,6},{3,7},{4,0},{5,1},{6,2},{7,3},{8,12},{9,13},{10,... | collective-permute-start | bytes 393224 | tf_op jit(solution)/shard_map/ppermute | solution.py:356
  6.6 0.2 shard_map.76
  6.7 0.0 collective-permute-done.q_par
  6.8 0.2 shard_map.77
  7.0 0.8 %shard_map.80.stats_in = f32[8,1024]{1,0:T(8,128)S(1)} custom-call(bf16[4,256,128]{2,1,0:T(8,128)(2,1)S(1)} %get-tuple-element.34.khot_ref, bf16[128,512]{1,0:T(8,128)(2,1)S(1)} %get-tuple-element.35.rhot_ref, bf16[256,512]{1,0:T(8,128)(2,1)S(1)} %get-tuple-element.36.qd_own, bf16[256,512]{1,0:T(8,128)(2,1)S(1)} %get-tuple-element.37.qd_par, ...), custom_call_target="tpu_custom_call" | custom-call | bytes 524288 | tf_op jit(solution)/shard_map/pallas_call | solution.py:312
  7.8 4.3 %collective-permute-done.3 = bf16[256,256]{1,0:T(8,128)(2,1)S(1)} collective-permute-done((bf16[256,256]{1,0:T(8,128)(2,1)S(1)}, bf16[256,256]{1,0:T(8,128)(2,1)S(1)}, u32[]{:S(2)}, u32[]{:S(2)}) %collective-permute-start.3) | collective-permute-done | bytes 131104 | tf_op jit(solution)/shard_map/ppermute | solution.py:356
  12.1 0.1 collective-permute-start.5
  12.2 1.2 %collective-permute-done.5.other_ref = f32[8,1024]{1,0:T(8,128)S(1)} collective-permute-done((f32[8,1024]{1,0:T(8,128)S(1)}, f32[8,1024]{1,0:T(8,128)S(1)}, u32[]{:S(2)}, u32[]{:S(2)}) %collective-permute-start.5) | collective-permute-done | bytes 32800 | tf_op jit(solution)/shard_map/ppermute | solution.py:359
  13.4 0.1 shard_map.85
  13.5 2.9 %collective-permute-start.6 = (bf16[256,256]{1,0:T(8,128)(2,1)S(1)}, bf16[256,256]{1,0:T(8,128)(2,1)S(1)}, u32[]{:S(2)}, u32[]{:S(2)}) collective-permute-start(bf16[256,256]{1,0:T(8,128)(2,1)S(1)} %bitcast.14), channel_id=1, source_target_pairs={{4,2},{5,3},{7,1},{6,5},{0,4},{1,0},{2,7},{3,6},{12,10},{13,11},{1... | collective-permute-start | bytes 393224 | tf_op jit(solution)/shard_map/ppermute | solution.py:356
  16.4 0.1 shard_map.87
  16.5 0.1 collective-permute-start.8
  16.6 2.0 %collective-permute-start.7 = (bf16[256,256]{1,0:T(8,128)(2,1)S(1)}, bf16[256,256]{1,0:T(8,128)(2,1)S(1)}, u32[]{:S(2)}, u32[]{:S(2)}) collective-permute-start(bf16[256,256]{1,0:T(8,128)(2,1)S(1)} %bitcast.15), channel_id=1, source_target_pairs={{0,4},{1,5},{2,6},{3,7},{4,0},{5,1},{6,2},{7,3},{8,12},{9,13},{10,... | collective-permute-start | bytes 393224 | tf_op jit(solution)/shard_map/ppermute | solution.py:356
  18.6 1.3 %shard_map.88 = (f32[256,256]{1,0:T(8,128)S(1)}, f32[256,256]{1,0:T(8,128)S(1)}, f32[256,256]{1,0:T(8,128)S(1)}) custom-call(bf16[4,256,128]{2,1,0:T(8,128)(2,1)S(1)} %get-tuple-element.34.khot_ref, bf16[128,512]{1,0:T(8,128)(2,1)S(1)} %get-tuple-element.35.rhot_ref, bf16[256,512]{1,0:T(8,128)(2,1)S(1)} %get-tuple-element.36.qd_own, ...), custom_call_target="tpu_custom_call" | custom-call | flops 4000000000 | bytes 524288 | tf_op jit(solution)/shard_map/pallas_call | solution.py:312
  19.9 0.1 collective-permute-done.6.rest_0_
  20.0 1.6 %collective-permute-done.8.rest_2_ = bf16[256,256]{1,0:T(8,128)(2,1)S(1)} collective-permute-done((bf16[256,256]{1,0:T(8,128)(2,1)S(1)}, bf16[256,256]{1,0:T(8,128)(2,1)S(1)}, u32[]{:S(2)}, u32[]{:S(2)}) %collective-permute-start.8) | collective-permute-done | bytes 131104 | tf_op jit(solution)/shard_map/ppermute | solution.py:356
  21.5 0.1 collective-permute-done.7.rest_1_
  21.7 0.1 shard_map.89
  21.8 0.1 collective-permute-start.9
  21.9 1.6 %collective-permute-start.10 = (bf16[64,256]{1,0:T(8,128)(2,1)S(1)}, bf16[64,256]{1,0:T(8,128)(2,1)S(1)}, u32[]{:S(2)}, u32[]{:S(2)}) collective-permute-start(bf16[64,256]{1,0:T(8,128)(2,1)S(1)} %get-tuple-element.60), channel_id=1, source_target_pairs={{0,8},{8,24},{16,0},{24,16},{1,9},{9,25},{17,1},{25,17},{2,10},{10... | collective-permute-start | bytes 98312 | tf_op jit(solution)/shard_map/ppermute | solution.py:423
  23.5 2.5 %collective-permute-start.11 = (bf16[64,256]{1,0:T(8,128)(2,1)S(1)}, bf16[64,256]{1,0:T(8,128)(2,1)S(1)}, u32[]{:S(2)}, u32[]{:S(2)}) collective-permute-start(bf16[64,256]{1,0:T(8,128)(2,1)S(1)} %get-tuple-element.61), channel_id=1, source_target_pairs={{0,24},{8,16},{16,8},{24,0},{1,25},{9,17},{17,9},{25,1},{2,26},{10... | collective-permute-start | bytes 98312 | tf_op jit(solution)/shard_map/ppermute | solution.py:423
  26.0 1.6 %collective-permute-start.12 = (bf16[64,256]{1,0:T(8,128)(2,1)S(1)}, bf16[64,256]{1,0:T(8,128)(2,1)S(1)}, u32[]{:S(2)}, u32[]{:S(2)}) collective-permute-start(bf16[64,256]{1,0:T(8,128)(2,1)S(1)} %get-tuple-element.62), channel_id=1, source_target_pairs={{0,16},{8,0},{16,24},{24,8},{1,17},{9,1},{17,25},{25,9},{2,18},{10... | collective-permute-start | bytes 98312 | tf_op jit(solution)/shard_map/ppermute | solution.py:423
  27.5 0.8 %shard_map.90 = (bf16[256,256]{1,0:T(8,128)(2,1)}, f32[8,128]{1,0:T(8,128)S(1)}) custom-call(f32[256,256]{1,0:T(8,128)S(1)} %get-tuple-element.50.dq_own, f32[256,256]{1,0:T(8,128)S(1)} %collective-permute-done.9.dq_far), custom_call_target="tpu_custom_call" | custom-call | flops 2000000000 | bytes 524288 | tf_op jit(solution)/shard_map/pallas_call | solution.py:312
  28.3 0.9 %collective-permute-done.11.rest_1_ = bf16[64,256]{1,0:T(8,128)(2,1)S(1)} collective-permute-done((bf16[64,256]{1,0:T(8,128)(2,1)S(1)}, bf16[64,256]{1,0:T(8,128)(2,1)S(1)}, u32[]{:S(2)}, u32[]{:S(2)}) %collective-permute-start.11) | collective-permute-done | bytes 32800 | tf_op jit(solution)/shard_map/ppermute | solution.py:423
  29.2 0.7 %collective-permute-done.12.rest_2_ = bf16[64,256]{1,0:T(8,128)(2,1)S(1)} collective-permute-done((bf16[64,256]{1,0:T(8,128)(2,1)S(1)}, bf16[64,256]{1,0:T(8,128)(2,1)S(1)}, u32[]{:S(2)}, u32[]{:S(2)}) %collective-permute-start.12) | collective-permute-done | bytes 32800 | tf_op jit(solution)/shard_map/ppermute | solution.py:423
  29.9 0.6 %shard_map.91 = (bf16[32,256]{1,0:T(8,128)(2,1)}, bf16[32,256]{1,0:T(8,128)(2,1)}) custom-call(f32[8,128]{1,0:T(8,128)S(1)} %get-tuple-element.58.after_ref, f32[64,256]{1,0:T(8,128)S(1)} %get-tuple-element.59.keep_ref, bf16[64,256]{1,0:T(8,128)(2,1)S(1)} %collective-permute-done.10.rest_0_, bf16[64,256]{1,0:T(8,128)(2,1)S(1)} %collective-permute-done.11.rest_1_, ...), custom_call_target="tpu_custom_call" | custom-call | bytes 524288 | tf_op jit(solution)/shard_map/pallas_call | solution.py:312
  (21 shorter events, 0.2 us)
Async XLA Ops:
  0.6 0.8 %copy-start.3 = (bf16[256,128]{1,0:T(8,128)(2,1)S(1)}, bf16[256,128]{1,0:T(8,128)(2,1)}, u32[]{:S(2)}) copy-start(bf16[256,128]{1,0:T(8,128)(2,1)} %value_ref.1) | copy-start | bytes 196612
  0.6 0.9 %copy-start.2 = (bf16[256,128]{1,0:T(8,128)(2,1)S(1)}, bf16[256,128]{1,0:T(8,128)(2,1)}, u32[]{:S(2)}) copy-start(bf16[256,128]{1,0:T(8,128)(2,1)} %key_ref.1) | copy-start | bytes 196612
  0.7 6.1 %collective-permute-start = (bf16[256,256]{1,0:T(8,128)(2,1)}, bf16[256,256]{1,0:T(8,128)(2,1)S(1)}, u32[]{:S(2)}, u32[]{:S(2)}) collective-permute-start(bf16[256,256]{1,0:T(8,128)(2,1)} %q_own.1), channel_id=1, source_target_pairs={{0,1},{1,0},{2,3},{3,2},{4,5},{5,4},{6,7},{7,6},{8,9},{9,8},{10,11... | collective-permute-start | bytes 393224 | tf_op jit(solution)/shard_map/ppermute | solution.py:359
  1.2 5.6 %collective-permute-start.1 = (bf16[256,256]{1,0:T(8,128)(2,1)}, bf16[256,256]{1,0:T(8,128)(2,1)S(1)}, u32[]{:S(2)}, u32[]{:S(2)}) collective-permute-start(bf16[256,256]{1,0:T(8,128)(2,1)} %do_own.1), channel_id=1, source_target_pairs={{0,1},{1,0},{2,3},{3,2},{4,5},{5,4},{6,7},{7,6},{8,9},{9,8},{10,11... | collective-permute-start | bytes 393224 | tf_op jit(solution)/shard_map/ppermute | solution.py:359
  1.5 5.1 %copy-start.4 = (s32[2048]{0:T(1024)S(1)}, s32[2048]{0:T(1024)}, u32[]{:S(2)}) copy-start(s32[2048]{0:T(1024)} %param.9) | copy-start | bytes 24580
  1.5 5.2 %copy-start = (bf16[256,256]{1,0:T(8,128)(2,1)S(1)}, bf16[256,256]{1,0:T(8,128)(2,1)}, u32[]{:S(2)}) copy-start(bf16[256,256]{1,0:T(8,128)(2,1)} %q_own.1) | copy-start | bytes 393220
  1.5 5.3 %copy-start.1 = (bf16[256,256]{1,0:T(8,128)(2,1)S(1)}, bf16[256,256]{1,0:T(8,128)(2,1)}, u32[]{:S(2)}) copy-start(bf16[256,256]{1,0:T(8,128)(2,1)} %do_own.1) | copy-start | bytes 393220
  1.5 6.2 %collective-permute-start.2 = (bf16[256,256]{1,0:T(8,128)(2,1)S(1)}, bf16[256,256]{1,0:T(8,128)(2,1)S(1)}, u32[]{:S(2)}, u32[]{:S(2)}) collective-permute-start(bf16[256,256]{1,0:T(8,128)(2,1)S(1)} %shard_map.79.kv_ref), channel_id=1, source_target_pairs={{1,7},{7,6},{6,2},{2,4},{4,0},{0,1},{3,5},{5,3},{9,15},{15,14},{14... | collective-permute-start | bytes 393224 | tf_op jit(solution)/shard_map/ppermute | solution.py:356
  2.0 10.0 %collective-permute-start.3 = (bf16[256,256]{1,0:T(8,128)(2,1)S(1)}, bf16[256,256]{1,0:T(8,128)(2,1)S(1)}, u32[]{:S(2)}, u32[]{:S(2)}) collective-permute-start(bf16[256,256]{1,0:T(8,128)(2,1)S(1)} %shard_map.79.kv_ref), channel_id=1, source_target_pairs={{0,2},{1,3},{2,0},{3,1},{4,6},{5,7},{6,4},{7,5},{8,10},{9,11},{10,... | collective-permute-start | bytes 393224 | tf_op jit(solution)/shard_map/ppermute | solution.py:356
  6.0 6.0 %collective-permute-start.4 = (bf16[256,256]{1,0:T(8,128)(2,1)S(1)}, bf16[256,256]{1,0:T(8,128)(2,1)S(1)}, u32[]{:S(2)}, u32[]{:S(2)}) collective-permute-start(bf16[256,256]{1,0:T(8,128)(2,1)S(1)} %shard_map.79.kv_ref), channel_id=1, source_target_pairs={{0,4},{1,5},{2,6},{3,7},{4,0},{5,1},{6,2},{7,3},{8,12},{9,13},{10,... | collective-permute-start | bytes 393224 | tf_op jit(solution)/shard_map/ppermute | solution.py:356
  12.1 1.3 %collective-permute-start.5 = (f32[8,1024]{1,0:T(8,128)S(1)}, f32[8,1024]{1,0:T(8,128)S(1)}, u32[]{:S(2)}, u32[]{:S(2)}) collective-permute-start(f32[8,1024]{1,0:T(8,128)S(1)} %get-tuple-element.40.stats_ref.rest_0_), channel_id=1, source_target_pairs={{0,1},{1,0},{2,3},{3,2},{4,5},{5,4},{6,7},{7,6},{8,9},{9,8},{10,11... | collective-permute-start | bytes 98312 | tf_op jit(solution)/shard_map/ppermute | solution.py:359
  13.5 6.5 %collective-permute-start.6 = (bf16[256,256]{1,0:T(8,128)(2,1)S(1)}, bf16[256,256]{1,0:T(8,128)(2,1)S(1)}, u32[]{:S(2)}, u32[]{:S(2)}) collective-permute-start(bf16[256,256]{1,0:T(8,128)(2,1)S(1)} %bitcast.14), channel_id=1, source_target_pairs={{4,2},{5,3},{7,1},{6,5},{0,4},{1,0},{2,7},{3,6},{12,10},{13,11},{1... | collective-permute-start | bytes 393224 | tf_op jit(solution)/shard_map/ppermute | solution.py:356
  16.5 5.0 %collective-permute-start.8 = (bf16[256,256]{1,0:T(8,128)(2,1)S(1)}, bf16[256,256]{1,0:T(8,128)(2,1)S(1)}, u32[]{:S(2)}, u32[]{:S(2)}) collective-permute-start(bf16[256,256]{1,0:T(8,128)(2,1)S(1)} %bitcast.16), channel_id=1, source_target_pairs={{0,2},{1,3},{2,0},{3,1},{4,6},{5,7},{6,4},{7,5},{8,10},{9,11},{10,... | collective-permute-start | bytes 393224 | tf_op jit(solution)/shard_map/ppermute | solution.py:356
  16.6 5.1 %collective-permute-start.7 = (bf16[256,256]{1,0:T(8,128)(2,1)S(1)}, bf16[256,256]{1,0:T(8,128)(2,1)S(1)}, u32[]{:S(2)}, u32[]{:S(2)}) collective-permute-start(bf16[256,256]{1,0:T(8,128)(2,1)S(1)} %bitcast.15), channel_id=1, source_target_pairs={{0,4},{1,5},{2,6},{3,7},{4,0},{5,1},{6,2},{7,3},{8,12},{9,13},{10,... | collective-permute-start | bytes 393224 | tf_op jit(solution)/shard_map/ppermute | solution.py:356
  21.8 5.8 %collective-permute-start.9 = (f32[256,256]{1,0:T(8,128)S(1)}, f32[256,256]{1,0:T(8,128)S(1)}, u32[]{:S(2)}, u32[]{:S(2)}) collective-permute-start(f32[256,256]{1,0:T(8,128)S(1)} %get-tuple-element.56), channel_id=1, source_target_pairs={{0,1},{1,0},{2,3},{3,2},{4,5},{5,4},{6,7},{7,6},{8,9},{9,8},{10,11... | collective-permute-start | bytes 786440 | tf_op jit(solution)/shard_map/ppermute | solution.py:359
  21.9 6.5 %collective-permute-start.10 = (bf16[64,256]{1,0:T(8,128)(2,1)S(1)}, bf16[64,256]{1,0:T(8,128)(2,1)S(1)}, u32[]{:S(2)}, u32[]{:S(2)}) collective-permute-start(bf16[64,256]{1,0:T(8,128)(2,1)S(1)} %get-tuple-element.60), channel_id=1, source_target_pairs={{0,8},{8,24},{16,0},{24,16},{1,9},{9,25},{17,1},{25,17},{2,10},{10... | collective-permute-start | bytes 98312 | tf_op jit(solution)/shard_map/ppermute | solution.py:423
  23.5 5.7 %collective-permute-start.11 = (bf16[64,256]{1,0:T(8,128)(2,1)S(1)}, bf16[64,256]{1,0:T(8,128)(2,1)S(1)}, u32[]{:S(2)}, u32[]{:S(2)}) collective-permute-start(bf16[64,256]{1,0:T(8,128)(2,1)S(1)} %get-tuple-element.61), channel_id=1, source_target_pairs={{0,24},{8,16},{16,8},{24,0},{1,25},{9,17},{17,9},{25,1},{2,26},{10... | collective-permute-start | bytes 98312 | tf_op jit(solution)/shard_map/ppermute | solution.py:423
  26.0 3.9 %collective-permute-start.12 = (bf16[64,256]{1,0:T(8,128)(2,1)S(1)}, bf16[64,256]{1,0:T(8,128)(2,1)S(1)}, u32[]{:S(2)}, u32[]{:S(2)}) collective-permute-start(bf16[64,256]{1,0:T(8,128)(2,1)S(1)} %get-tuple-element.62), channel_id=1, source_target_pairs={{0,16},{8,0},{16,24},{24,8},{1,17},{9,1},{17,25},{25,9},{2,18},{10... | collective-permute-start | bytes 98312 | tf_op jit(solution)/shard_map/ppermute | solution.py:423
